TPU v7x, 512 devices: a whole 4x8x8 slice. The times are simulated.
512 devices in a mesh: row: 16 (over z_lo, x, core), col: 8 (over y), depth: 4 (over z_hi).
Axes of the slice: x: 4, y: 8, z: 8 (z_hi: 4, z_lo: 2; z = z_hi * 2 + z_lo), core: 2. Of those that a mesh axis runs over, the one named last changes fastest.
Arguments:
- density: bfloat16 [2048, 64, 4096], P(('row', 'col'), None, 'depth'), as said below
- pattern: int32 [2048, 64], P(('row', 'col'), 'depth'), may hold values from 0 to 1, as said below
- keep_filter: int32 [2048, 16], P(('row', 'col'), 'depth'), may hold values from 0 to 1, as said below
Outputs:
- square: bfloat16 [2048, 64, 1024], P(('row', 'col'), None, 'depth')
Inputs may be any that keep to these rules, and one draw needn't show every extreme that they name: density is exactly symmetric: for t of 1 or more, block (i, t) is the transpose of block ((i + t - 32) mod 2048, 64 - t). pattern is symmetric in the same sense; slot 0 is 0, and slots within 7 of slot 32 are 1. `keep_filter`: offsets below 4 are 1.
All inputs are finite; a program needn't handle non-finite values.
Results may differ from a plain program's by a relative error of at most 0.013.
Values may be sent and summed in bfloat16 or wider, within the bound.
No kernel may reach another device: no remote copies, remote signals or barrier semaphores. Data moves between devices by JAX's collectives and lax.ppermute only.
A program may use at most 64 MiB of HBM per device.

v0:
```python
import jax
import jax.numpy as jnp
from jax import lax
from jax.sharding import PartitionSpec as P


def from_behind(block, axis, distance):
    devices = range(lax.axis_size(axis))
    route = [(i - distance, i) for i in devices if i - distance in devices]
    return lax.ppermute(block, axis, route)


def passed_along(block, axis, distance):
    devices = range(lax.axis_size(axis))
    route = [((i - distance) % len(devices), i) for i in devices]
    return lax.ppermute(block, axis, route)


def spread_blocks(block_mask, block_side):
    row_count, slot_count = block_mask.shape
    spread = jnp.broadcast_to(
        block_mask[:, None, :, None], (row_count, block_side, slot_count, block_side)
    )
    return spread.reshape(row_count, block_side, slot_count * block_side)


def per_device(density, pattern, keep_filter):
    rows_dev, block_side, stored_cols = density.shape
    slot_share = stored_cols // block_side
    keep_share = keep_filter.shape[1]
    keep_count = keep_share * lax.axis_size("depth")
    masked = density * spread_blocks(pattern.astype(jnp.bfloat16), block_side)
    lower_rim = from_behind(masked, "depth", 1)
    band_rows = jnp.concatenate([lower_rim, masked], axis=2)
    next_panel = passed_along(band_rows, ("row", "col"), -1)
    band_slab = jnp.concatenate([band_rows, next_panel], axis=0)
    partial_value = jnp.zeros((rows_dev, block_side, keep_count * block_side), jnp.float32)

    def one_offset(offset, partial_value):
        rows_part = lax.dynamic_slice_in_dim(band_slab, offset, rows_dev, 0)
        partner = lax.dynamic_slice_in_dim(
            rows_part, (slot_share - offset) * block_side, stored_cols, 2
        )
        product_block = jnp.einsum(
            "iab,icb->iac", masked, partner, preferred_element_type=jnp.float32
        )
        return lax.dynamic_update_slice_in_dim(partial_value, product_block, offset * block_side, 2)

    partial_value = lax.fori_loop(0, keep_count, one_offset, partial_value)
    summed = lax.psum_scatter(
        partial_value.astype(jnp.bfloat16), "depth", scatter_dimension=2, tiled=True
    ).astype(jnp.float32)
    keep_mask = spread_blocks(keep_filter.astype(jnp.float32), block_side)
    return (summed * keep_mask).astype(jnp.bfloat16)


def solution(mesh):
    placed = (
        P(("row", "col"), None, "depth"),
        P(("row", "col"), "depth"),
        P(("row", "col"), "depth"),
    )
    return jax.shard_map(
        per_device,
        mesh=mesh,
        in_specs=placed,
        out_specs=P(("row", "col"), None, "depth"),
        check_vma=False,
    )
```

profile of v0, /device:TPU:63, one launch (start us, length us, event | category | flops | bytes accessed | tf_op | source)
XLA Modules:
  0.0 385.4 jit_solution(12794212234706996046)
XLA Ops:
  9.2 5.9 %collective-permute-start = (bf16[16,64,1024]{2,1,0:T(8,128)(2,1)S(1)}, bf16[16,64,1024]{2,1,0:T(8,128)(2,1)S(1)}, u32[]{:S(2)}, u32[]{:S(2)}) collective-permute-start(bf16[16,64,1024]{2,1,0:T(8,128)(2,1)S(1)} %broadcast_multiply_fusion), channel_id=1, source_target_pairs={{0,1},{1,2},{2,3},{4,5},{5,6},{6,7},{8,9},{9,10},{10,11},{12,13},{... | collective-permute-start | bytes 6291464 | tf_op jit(solution)/shard_map/ppermute | solution.py:10
  15.1 44.2 %collective-permute-done = bf16[16,64,1024]{2,1,0:T(8,128)(2,1)S(1)} collective-permute-done((bf16[16,64,1024]{2,1,0:T(8,128)(2,1)S(1)}, bf16[16,64,1024]{2,1,0:T(8,128)(2,1)S(1)}, u32[]{:S(2)}, u32[]{:S(2)}) %collective-permute-start) | collective-permute-done | bytes 2097184 | tf_op jit(solution)/shard_map/ppermute | solution.py:10
  59.3 2.6 pad_maximum_fusion.1
  61.9 3.0 collective-permute-start.1
  64.9 134.1 %collective-permute-done.1 = bf16[16,64,2048]{2,1,0:T(8,128)(2,1)} collective-permute-done((bf16[16,64,2048]{2,1,0:T(8,128)(2,1)}, bf16[16,64,2048]{2,1,0:T(8,128)(2,1)}, u32[]{:S(2)}, u32[]{:S(2)}) %collective-permute-start.1) | collective-permute-done | bytes 4194336 | tf_op jit(solution)/shard_map/ppermute | solution.py:16
  199.0 6.5 %pad_maximum_fusion = bf16[32,64,2048]{2,1,0:T(8,128)(2,1)} fusion(bf16[16,64,2048]{2,1,0:T(8,128)(2,1)} %collective-permute-done.1, bf16[16,64,1024]{2,1,0:T(8,128)(2,1)S(1)} %broadcast_multiply_fusion, bf16[16,64,1024]{2,1,0:T(8,128)(2,1)} %copy-done), kind=kLoop, calls=%fused_computation.4 | loop fusion | flops 25165824 | bytes 16777216 | tf_op jit(solution)/shard_map/concatenate | solution.py:36
  207.1 109.4 %while.16 = (s32[]{:T(128)}, bf16[16,64,1024]{2,1,0:T(8,128)(2,1)}, bf16[32,64,2048]{2,1,0:T(8,128)(2,1)}, bf16[16,64,1024]{2,1,0:T(8,128)(2,1)S(1)}, s32[]{:T(1...) while((s32[]{:T(128)}, bf16[16,64,1024]{2,1,0:T(8,128)(2,1)}, ...), condition=%wide.region_1.0_spmd, body=%wide.region_0.0_spmd.sunk | while | flops 134217728 | bytes 4587769 | solution.py:49
  209.6 3.6 dynamic_update_slice.12
  213.2 2.5 fusion.12
  215.7 5.2 %dynamic_update_slice.12 = bf16[16,64,1024]{2,1,0:T(8,128)(2,1)} dynamic-update-slice(bf16[16,64,1024]{2,1,0:T(8,128)(2,1)} %get-tuple-element.174, bf16[16,64,64]{2,1,0:T(8,128)(2,1)S(1)} %fusion.12, s32[]{:T(128)} %constant.127.clone.1..sunk, s32[]{:T(128)} %constant.127.clone.1..sunk, s32[]{:T(128)S(6)} %select_n.42) | dynamic-update-slice | bytes 262148 | tf_op jit(solution)/shard_map/while/body/eval_jaxpr/dynamic_update_slice | solution.py:47
  223.5 3.6 dynamic_update_slice.12
  229.6 5.2 %dynamic_update_slice.12 = bf16[16,64,1024]{2,1,0:T(8,128)(2,1)} dynamic-update-slice(bf16[16,64,1024]{2,1,0:T(8,128)(2,1)} %get-tuple-element.174, bf16[16,64,64]{2,1,0:T(8,128)(2,1)S(1)} %fusion.12, s32[]{:T(128)} %constant.127.clone.1..sunk, s32[]{:T(128)} %constant.127.clone.1..sunk, s32[]{:T(128)S(6)} %select_n.42) | dynamic-update-slice | bytes 262148 | tf_op jit(solution)/shard_map/while/body/eval_jaxpr/dynamic_update_slice | solution.py:47
  234.8 2.5 fusion.12
  237.3 3.6 dynamic_update_slice.12
  240.9 2.5 fusion.12
  243.5 5.2 %dynamic_update_slice.12 = bf16[16,64,1024]{2,1,0:T(8,128)(2,1)} dynamic-update-slice(bf16[16,64,1024]{2,1,0:T(8,128)(2,1)} %get-tuple-element.174, bf16[16,64,64]{2,1,0:T(8,128)(2,1)S(1)} %fusion.12, s32[]{:T(128)} %constant.127.clone.1..sunk, s32[]{:T(128)} %constant.127.clone.1..sunk, s32[]{:T(128)S(6)} %select_n.42) | dynamic-update-slice | bytes 262148 | tf_op jit(solution)/shard_map/while/body/eval_jaxpr/dynamic_update_slice | solution.py:47
  248.6 2.5 fusion.12
  251.2 3.6 dynamic_update_slice.12
  254.8 2.5 fusion.12
  257.3 5.2 %dynamic_update_slice.12 = bf16[16,64,1024]{2,1,0:T(8,128)(2,1)} dynamic-update-slice(bf16[16,64,1024]{2,1,0:T(8,128)(2,1)} %get-tuple-element.174, bf16[16,64,64]{2,1,0:T(8,128)(2,1)S(1)} %fusion.12, s32[]{:T(128)} %constant.127.clone.1..sunk, s32[]{:T(128)} %constant.127.clone.1..sunk, s32[]{:T(128)S(6)} %select_n.42) | dynamic-update-slice | bytes 262148 | tf_op jit(solution)/shard_map/while/body/eval_jaxpr/dynamic_update_slice | solution.py:47
  265.1 3.6 dynamic_update_slice.12
  268.6 2.5 fusion.12
  271.2 5.1 %dynamic_update_slice.12 = bf16[16,64,1024]{2,1,0:T(8,128)(2,1)} dynamic-update-slice(bf16[16,64,1024]{2,1,0:T(8,128)(2,1)} %get-tuple-element.174, bf16[16,64,64]{2,1,0:T(8,128)(2,1)S(1)} %fusion.12, s32[]{:T(128)} %constant.127.clone.1..sunk, s32[]{:T(128)} %constant.127.clone.1..sunk, s32[]{:T(128)S(6)} %select_n.42) | dynamic-update-slice | bytes 262148 | tf_op jit(solution)/shard_map/while/body/eval_jaxpr/dynamic_update_slice | solution.py:47
  278.9 3.6 dynamic_update_slice.12
  285.0 5.1 %dynamic_update_slice.12 = bf16[16,64,1024]{2,1,0:T(8,128)(2,1)} dynamic-update-slice(bf16[16,64,1024]{2,1,0:T(8,128)(2,1)} %get-tuple-element.174, bf16[16,64,64]{2,1,0:T(8,128)(2,1)S(1)} %fusion.12, s32[]{:T(128)} %constant.127.clone.1..sunk, s32[]{:T(128)} %constant.127.clone.1..sunk, s32[]{:T(128)S(6)} %select_n.42) | dynamic-update-slice | bytes 262148 | tf_op jit(solution)/shard_map/while/body/eval_jaxpr/dynamic_update_slice | solution.py:47
  290.2 2.5 fusion.12
  292.7 3.6 dynamic_update_slice.12
  298.8 5.1 %dynamic_update_slice.12 = bf16[16,64,1024]{2,1,0:T(8,128)(2,1)} dynamic-update-slice(bf16[16,64,1024]{2,1,0:T(8,128)(2,1)} %get-tuple-element.174, bf16[16,64,64]{2,1,0:T(8,128)(2,1)S(1)} %fusion.12, s32[]{:T(128)} %constant.127.clone.1..sunk, s32[]{:T(128)} %constant.127.clone.1..sunk, s32[]{:T(128)S(6)} %select_n.42) | dynamic-update-slice | bytes 262148 | tf_op jit(solution)/shard_map/while/body/eval_jaxpr/dynamic_update_slice | solution.py:47
  306.6 2.9 dynamic_update_slice.12
  309.5 2.5 fusion.12
  312.1 4.4 %dynamic_update_slice.12 = bf16[16,64,1024]{2,1,0:T(8,128)(2,1)} dynamic-update-slice(bf16[16,64,1024]{2,1,0:T(8,128)(2,1)} %get-tuple-element.174, bf16[16,64,64]{2,1,0:T(8,128)(2,1)S(1)} %fusion.12, s32[]{:T(128)} %constant.127.clone.1..sunk, s32[]{:T(128)} %constant.127.clone.1..sunk, s32[]{:T(128)S(6)} %select_n.42) | dynamic-update-slice | bytes 262148 | tf_op jit(solution)/shard_map/while/body/eval_jaxpr/dynamic_update_slice | solution.py:47
  316.8 59.8 %reduce-scatter.2.cloned.1.call-done = bf16[16,64,256]{2,1,0:T(8,128)(2,1)} async-done(((bf16[16,64,1024]{2,1,0:T(8,128)(2,1)}), bf16[16,64,256]{2,1,0:T(8,128)(2,1)}) %reduce-scatter.2.cloned.1.call-update) | async-done | bytes 524304 | tf_op jit(solution)/shard_map/reduce_scatter | solution.py:50
  (24 shorter events, 26.8 us)
Async XLA Ops:
  6.5 370.1 %reduce-scatter.2.cloned.1.call-start = ((), (), s32[]{:S(2)}) async-start(), calls=%async_computation.1 | async-start | bytes 2621440 | tf_op jit(solution)/shard_map/reduce_scatter | solution.py:50
  9.2 50.1 %collective-permute-start = (bf16[16,64,1024]{2,1,0:T(8,128)(2,1)S(1)}, bf16[16,64,1024]{2,1,0:T(8,128)(2,1)S(1)}, u32[]{:S(2)}, u32[]{:S(2)}) collective-permute-start(bf16[16,64,1024]{2,1,0:T(8,128)(2,1)S(1)} %broadcast_multiply_fusion), channel_id=1, source_target_pairs={{0,1},{1,2},{2,3},{4,5},{5,6},{6,7},{8,9},{9,10},{10,11},{12,13},{... | collective-permute-start | bytes 6291464 | tf_op jit(solution)/shard_map/ppermute | solution.py:10
  59.3 2.6 copy-start
  61.9 137.1 %collective-permute-start.1 = (bf16[16,64,2048]{2,1,0:T(8,128)(2,1)}, bf16[16,64,2048]{2,1,0:T(8,128)(2,1)}, u32[]{:S(2)}, u32[]{:S(2)}) collective-permute-start(bf16[16,64,2048]{2,1,0:T(8,128)(2,1)} %pad_maximum_fusion.1), channel_id=1, source_target_pairs={{4,0},{8,4},{12,8},{16,12},{20,16},{24,20},{28,24},{32,28},{36,32}... | collective-permute-start | bytes 12582920 | tf_op jit(solution)/shard_map/ppermute | solution.py:16
  207.1 109.4 %copy-start.1 = (s32[16,4]{0,1:T(4,128)S(1)}, s32[16,4]{0,1:T(4,128)}, u32[]{:S(2)}) copy-start(s32[16,4]{0,1:T(4,128)} %param.7) | copy-start | bytes 772
Sparse Core Ops, SparseCore 0:
  316.7 59.9 reduce-scatter.1
where the time goes:
time: 389 us; the launch traced here: 385 us
  waiting for transfers between devices  238 us (61%)
  local copies, waits for them, and re-layouts  70.5 us (18%)
  matrix products  40.7 us (10%)
  other arithmetic  13.5 us (3%)
  between operations  13.4 us (3%)
  starting transfers between devices  8.91 us (2%)
    ppermute x1, waiting for transfers between devices, passed_along(): return lax.ppermute(block, axis, route)  134 us
    dynamic_update_slice x16, local copies, waits for them, and re-layouts, one_offset(): lax.dynamic_update_slice_in_dim(partial_value, product_block, offset * bl...  68.4 us
    reduce_scatter x1, waiting for transfers between devices, per_device(): lax.psum_scatter(partial_value.astype(jnp.bfloat16), 'depth', scatter_dim...  59.8 us
    ppermute x1, waiting for transfers between devices, from_behind(): return lax.ppermute(block, axis, route)  44.2 us
    dot_general x16, matrix products, one_offset(): jnp.einsum('iab,icb->iac', masked, partner, preferred_element_type=jnp.fl...  40.7 us
  transfers between devices with their start and end apart: 3, of which 3 were waited for; matrix products, arithmetic and copies ran while one was open for 0% of the time, Pallas kernels for 0%

commit v1 on v0

v1 whole, which is shorter than its diff:
```python
import functools
import jax
import jax.numpy as jnp
from jax import lax
from jax.experimental import pallas as pl
from jax.experimental.pallas import tpu as pltpu
from jax.sharding import PartitionSpec as P

BS = 64
ROWS = 16
WIDE = ROWS * BS
TILE = 256
AXES = ("row", "col", "depth")
NT = (((1,), (1,)), ((), ()))
NN = (((1,), (0,)), ((), ()))


def dot(a, b, dims):
    return lax.dot_general(a, b, dims, preferred_element_type=jnp.float32)


def expand(flags, cols):
    count = flags.shape[1]
    slot = lax.broadcasted_iota(jnp.int32, (count, cols), 0)
    col = lax.broadcasted_iota(jnp.int32, (count, cols), 1)
    spread = jnp.where((col >= slot * BS) & (col < slot * BS + BS), 1.0, 0.0)
    return dot(flags.astype(jnp.float32), spread, NN)


def masked_lanes(dens, mask, i, lo, hi):
    m = jnp.broadcast_to(mask[i : i + 1, lo:hi], (16, hi - lo)).astype(jnp.bfloat16)
    x = dens[i, :, lo:hi].reshape(BS // 16, 16, hi - lo)
    return (x * m[None]).reshape(BS, hi - lo)


def upper_width(i):
    return WIDE - 128 * (i // 2)


def upper_place(i):
    a, e = i // 2, i % 2
    if a < 4:
        return i, 0
    if a == 4:
        return 8, 512 * e
    return 2 * (8 - a) + e, 128 * a


def lower_width(i):
    return 128 * ((i - 1) // 2 + 1)


def lower_place(i):
    a, e = (i - 1) // 2, (i - 1) % 2
    if i == ROWS - 1:
        return 7, 0
    if a < 3:
        return 2 * a + e, WIDE - 128 * (a + 1)
    if a == 3:
        return 6, 512 * e
    return 2 * (6 - a) + e, 0


def pack_kernel(dens, pat, send_a, send_b, mask):
    q = lax.axis_index("depth")
    mask[...] = expand(pat[...], WIDE)

    for i in range(ROWS):
        width = upper_width(i)
        row, lane = upper_place(i)
        part = masked_lanes(dens, mask, i, 0, width)
        send_b[row, :, lane : lane + width] = part

        @pl.when(q != 2)
        def _():
            send_a[row, :, lane : lane + width] = part

    @pl.when(q == 2)
    def _():
        for i in range(1, ROWS):
            width = lower_width(i)
            row, lane = lower_place(i)
            send_a[row, :, lane : lane + width] = masked_lanes(dens, mask, i, WIDE - width, WIDE)
        send_a[8] = jnp.zeros((BS, WIDE), jnp.bfloat16)


def main_kernel(dens, pat, buf_a, buf_b, own, out1, out2, out3, mask, z, y):
    q = lax.axis_index("depth")
    mask[...] = expand(pat[...], WIDE)
    outs = (own, out1, out2, out3)

    def own_upper(i):
        return masked_lanes(dens, mask, i, 0, upper_width(i))

    def own_lower(i):
        return masked_lanes(dens, mask, i, WIDE - lower_width(i), WIDE)

    def sent_upper(buf):
        def get(i):
            row, lane = upper_place(i)
            return buf[row, :, lane : lane + upper_width(i)]

        return get

    def sent_lower(buf):
        def get(i):
            row, lane = lower_place(i)
            return buf[row, :, lane : lane + lower_width(i)]

        return get

    def build(dst, base, lower, upper):
        for i in range(ROWS):
            parts = []
            if i > 0:
                width = lower_width(i)
                parts.append(lower(i) if lower else jnp.zeros((BS, width), jnp.bfloat16))
            width = upper_width(i)
            parts.append(upper(i) if upper else jnp.zeros((BS, width), jnp.bfloat16))
            both = jnp.concatenate(parts, axis=1) if i > 0 else parts[0]
            if i % 2:
                both = both[:, BS : BS + WIDE]
            if not lower and i % 2:
                lane = lax.broadcasted_iota(jnp.int32, (BS, WIDE), 1)
                both = jnp.where(lane >= i * BS, both, jnp.zeros_like(both))
            if not upper and i % 2:
                lane = lax.broadcasted_iota(jnp.int32, (BS, WIDE), 1)
                both = jnp.where(lane < i * BS, both, jnp.zeros_like(both))
            dst[base + i * BS : base + (i + 1) * BS, :] = both

    def mirror(dst, base):
        r = lax.broadcasted_iota(jnp.int32, (TILE, TILE), 0)
        c = lax.broadcasted_iota(jnp.int32, (TILE, TILE), 1)
        eye = jnp.where(r == c, 1.0, 0.0).astype(jnp.bfloat16)
        strict = jnp.where(r // BS < c // BS, 1.0, 0.0).astype(jnp.bfloat16)
        for n in range(WIDE // TILE):
            rows = slice(base + n * TILE, base + (n + 1) * TILE)
            cols = slice(n * TILE, (n + 1) * TILE)
            diag = dst[rows, cols]
            dst[rows, cols] = diag + dot(eye, diag * strict, NT).astype(jnp.bfloat16)
            for m in range(n + 1, WIDE // TILE):
                tile = dst[rows, m * TILE : (m + 1) * TILE]
                dst[base + m * TILE : base + (m + 1) * TILE, cols] = dot(eye, tile, NT).astype(jnp.bfloat16)

    def finish(static_q, tile_row, window):
        for n in range(TILE // BS):
            i = tile_row * (TILE // BS) + n
            row = window[n * BS : (n + 1) * BS, n * BS : n * BS + WIDE].astype(jnp.bfloat16)
            for p in range(4):
                outs[(p - static_q) % 4][i] = row[:, p * TILE : (p + 1) * TILE]

    def products(static_q):
        for t in range(WIDE // TILE):
            lo, hi = t * TILE, (t + 1) * TILE
            depth_hi = hi if static_q == 3 else WIDE
            window = dot(z[lo:hi, :depth_hi], z[lo : lo + WIDE + TILE, :depth_hi], NT)
            if static_q == 0:
                first = dot(y[lo:hi, lo:], y[lo:, lo:], NT)
                window = jnp.concatenate(
                    [window[:, : WIDE - lo] + first, window[:, WIDE - lo :]], axis=1
                )
            if static_q == 2:
                first = dot(y[lo:hi, :], y[lo:, :], NT)
                second = dot(y[lo:hi, :], z[:WIDE, :hi], NN)
                window = window + jnp.concatenate([first, second], axis=1)
            finish(static_q, t, window)

    @pl.when(q == 0)
    def _():
        build(z, 0, own_lower, sent_upper(buf_a))
        build(z, WIDE, None, sent_upper(buf_b))
        build(y, 0, None, own_upper)
        products(0)

    @pl.when(q == 1)
    def _():
        own[...] = jnp.zeros_like(own)

    @pl.when(q == 2)
    def _():
        build(z, 0, own_lower, sent_upper(buf_a))
        build(z, WIDE, None, sent_upper(buf_b))
        mirror(z, WIDE)
        build(y, 0, None, own_upper)
        mirror(y, 0)
        products(2)

    @pl.when(q == 3)
    def _():
        build(z, 0, own_lower, None)
        build(z, WIDE, sent_lower(buf_a), sent_upper(buf_b))
        products(3)


def final_kernel(own, in1, in2, in3, keep, out, mask):
    mask[...] = expand(keep[...], TILE)
    for i in range(ROWS):
        total = own[i].astype(jnp.float32) + in1[i].astype(jnp.float32)
        total = total + in2[i].astype(jnp.float32) + in3[i].astype(jnp.float32)
        out[i] = (total * mask[i : i + 1, :]).astype(jnp.bfloat16)


def vmem(count):
    return [pl.BlockSpec(memory_space=pltpu.VMEM)] * count


def per_device(groups, density, pattern, keep_filter):
    packed = jax.ShapeDtypeStruct((9, BS, WIDE), jnp.bfloat16)
    share = jax.ShapeDtypeStruct((ROWS, BS, TILE), jnp.bfloat16)
    mib = 1024 * 1024

    send_a, send_b = pl.pallas_call(
        pack_kernel,
        out_shape=(packed, packed),
        in_specs=vmem(2),
        out_specs=tuple(vmem(2)),
        scratch_shapes=[pltpu.VMEM((ROWS, WIDE), jnp.float32)],
        compiler_params=pltpu.CompilerParams(vmem_limit_bytes=24 * mib),
        cost_estimate=pl.CostEstimate(flops=4_000_000, bytes_accessed=4_500_000, transcendentals=0),
    )(density, pattern)

    def device(g, q):
        return (g % groups) * 4 + q

    route_a, route_b = [], []
    for g in range(groups):
        route_a += [(device(g, 1), device(g, 0)), (device(g, 3), device(g, 2))]
        route_a += [(device(g + 1, 2), device(g, 3))]
        route_b += [(device(g + 1, q), device(g, q)) for q in (0, 2, 3)]
    buf_a = lax.ppermute(send_a, AXES, route_a)
    buf_b = lax.ppermute(send_b, AXES, route_b)

    parts = pl.pallas_call(
        main_kernel,
        out_shape=(share,) * 4,
        in_specs=vmem(4),
        out_specs=tuple(vmem(4)),
        scratch_shapes=[
            pltpu.VMEM((ROWS, WIDE), jnp.float32),
            pltpu.VMEM((2 * WIDE, WIDE), jnp.bfloat16),
            pltpu.VMEM((WIDE, WIDE), jnp.bfloat16),
        ],
        compiler_params=pltpu.CompilerParams(vmem_limit_bytes=40 * mib),
        cost_estimate=pl.CostEstimate(flops=8_000_000_000, bytes_accessed=7_000_000, transcendentals=0),
    )(density, pattern, buf_a, buf_b)

    landed = [parts[0]]
    for shift in (1, 2, 3):
        route = [(q, (q + shift) % 4) for q in (0, 2, 3)]
        landed.append(lax.ppermute(parts[shift], "depth", route))

    return pl.pallas_call(
        final_kernel,
        out_shape=share,
        in_specs=vmem(5),
        out_specs=pl.BlockSpec(memory_space=pltpu.VMEM),
        scratch_shapes=[pltpu.VMEM((ROWS, TILE), jnp.float32)],
        compiler_params=pltpu.CompilerParams(vmem_limit_bytes=16 * mib),
        cost_estimate=pl.CostEstimate(flops=1_500_000, bytes_accessed=2_700_000, transcendentals=0),
    )(*landed, keep_filter)


def solution(mesh):
    placed = (
        P(("row", "col"), None, "depth"),
        P(("row", "col"), "depth"),
        P(("row", "col"), "depth"),
    )
    groups = mesh.shape["row"] * mesh.shape["col"]
    return jax.shard_map(
        functools.partial(per_device, groups),
        mesh=mesh,
        in_specs=placed,
        out_specs=P(("row", "col"), None, "depth"),
        check_vma=False,
    )
```

time: 389 us -> 141 us (0.36)
  the two profiles are of different devices: /device:TPU:63 before, /device:TPU:59 now
where the time goes in v1:
time: 141 us; the launch traced here: 140 us
  waiting for transfers between devices  85.1 us (60%)
  starting transfers between devices  45.7 us (32%)
  Pallas kernels  7.08 us (5%)
  local copies, waits for them, and re-layouts  2.38 us (2%)
    ppermute x1, waiting for transfers between devices, per_device(): buf_a = lax.ppermute(send_a, AXES, route_a)  51.9 us
    ppermute x3, starting transfers between devices, per_device(): landed.append(lax.ppermute(parts[shift], 'depth', route))  41.3 us
    ppermute x3, waiting for transfers between devices, per_device(): landed.append(lax.ppermute(parts[shift], 'depth', route))  33.2 us
    pallas_call x1, Pallas kernels, per_device(): pl.pallas_call(main_kernel, out_shape=(share,) * 4, in_specs=vmem(4), out...  5.57 us
    ppermute x1, starting transfers between devices, per_device(): buf_b = lax.ppermute(send_b, AXES, route_b)  2.98 us
  transfers between devices with their start and end apart: 5, of which 3 were waited for; matrix products, arithmetic and copies ran while one was open for 0% of the time, Pallas kernels for 0%

profile of v1, /device:TPU:59, one launch (start us, length us, event | category | flops | bytes accessed | tf_op | source)
XLA Modules:
  0.0 140.4 jit_solution(3444796742943563723)
XLA Ops:
  0.0 0.0 copy-start
  0.0 1.6 %copy-done = bf16[16,64,1024]{2,1,0:T(8,128)(2,1)S(1)} copy-done((bf16[16,64,1024]{2,1,0:T(8,128)(2,1)S(1)}, bf16[16,64,1024]{2,1,0:T(8,128)(2,1)}, u32[]{:S(2)}) %copy-start) | copy-done | bytes 2097176
  1.6 0.0 copy-start.2
  1.6 0.7 copy-done.2
  2.3 0.0 copy-start.1
  2.3 0.0 copy-start.3
  2.3 0.4 shard_map.37
  2.7 1.4 %collective-permute-start = (bf16[9,64,1024]{2,1,0:T(8,128)(2,1)S(1)}, bf16[9,64,1024]{2,1,0:T(8,128)(2,1)S(1)}, u32[]{:S(2)}, u32[]{:S(2)}) collective-permute-start(bf16[9,64,1024]{2,1,0:T(8,128)(2,1)S(1)} %get-tuple-element.11), channel_id=1, source_target_pairs={{1,0},{3,2},{6,3},{5,4},{7,6},{10,7},{9,8},{11,10},{14,11},{13,12}... | collective-permute-start | bytes 3538952 | tf_op jit(solution)/shard_map/ppermute | solution.py:230
  4.1 0.0 copy-start.4
  4.1 3.0 %collective-permute-start.1 = (bf16[9,64,1024]{2,1,0:T(8,128)(2,1)S(1)}, bf16[9,64,1024]{2,1,0:T(8,128)(2,1)S(1)}, u32[]{:S(2)}, u32[]{:S(2)}) collective-permute-start(bf16[9,64,1024]{2,1,0:T(8,128)(2,1)S(1)} %get-tuple-element.12), channel_id=1, source_target_pairs={{4,0},{6,2},{7,3},{8,4},{10,6},{11,7},{12,8},{14,10},{15,11},{16,1... | collective-permute-start | bytes 3538952 | tf_op jit(solution)/shard_map/ppermute | solution.py:231
  7.1 51.9 %collective-permute-done.buf_a = bf16[9,64,1024]{2,1,0:T(8,128)(2,1)S(1)} collective-permute-done((bf16[9,64,1024]{2,1,0:T(8,128)(2,1)S(1)}, bf16[9,64,1024]{2,1,0:T(8,128)(2,1)S(1)}, u32[]{:S(2)}, u32[]{:S(2)}) %collective-permute-start) | collective-permute-done | bytes 1179680 | tf_op jit(solution)/shard_map/ppermute | solution.py:230
  59.0 0.0 collective-permute-done.1.buf_b
  59.0 0.0 copy-done.1
  59.0 0.0 copy-done.3
  59.0 5.6 %shard_map.38 = (bf16[16,64,256]{2,1,0:T(8,128)(2,1)S(1)}, bf16[16,64,256]{2,1,0:T(8,128)(2,1)}, bf16[16,64,256]{2,1,0:T(8,128)(2,1)S(1)}, bf16[16,64,256]{2,1,0:T(8,128)(2,1)S(1)}) custom-call(bf16[16,64,1024]{2,1,0:T(8,128)(2,1)S(1)} %copy-done.1, s32[16,16]{1,0:T(8,128)S(1)} %copy-done.3, bf16[9,64,1024]{2,1,0:T(8,128)(2,1)S(1)} %collective-permute-done.buf_a, ...), custom_call_target="tpu_custom_call" | custom-call | flops 8000000000 | bytes 7000000 | tf_op jit(solution)/shard_map/pallas_call | solution.py:233
  64.5 1.9 %collective-permute-start.2 = (bf16[16,64,256]{2,1,0:T(8,128)(2,1)}, bf16[16,64,256]{2,1,0:T(8,128)(2,1)S(1)}, u32[]{:S(2)}, u32[]{:S(2)}) collective-permute-start(bf16[16,64,256]{2,1,0:T(8,128)(2,1)} %get-tuple-element.14), channel_id=1, source_target_pairs={{0,1},{2,3},{3,0},{4,5},{6,7},{7,4},{8,9},{10,11},{11,8},{12,13},{... | collective-permute-start | bytes 1572872 | tf_op jit(solution)/shard_map/ppermute | solution.py:250
  66.5 38.1 %collective-permute-start.3 = (bf16[16,64,256]{2,1,0:T(8,128)(2,1)S(1)}, bf16[16,64,256]{2,1,0:T(8,128)(2,1)S(1)}, u32[]{:S(2)}, u32[]{:S(2)}) collective-permute-start(bf16[16,64,256]{2,1,0:T(8,128)(2,1)S(1)} %get-tuple-element.15), channel_id=1, source_target_pairs={{0,2},{2,0},{3,1},{4,6},{6,4},{7,5},{8,10},{10,8},{11,9},{12,14},{... | collective-permute-start | bytes 1572872 | tf_op jit(solution)/shard_map/ppermute | solution.py:250
  104.6 1.3 collective-permute-start.4
  105.9 0.0 copy-done.4
  105.9 0.1 copy.4.keep
  106.0 0.0 collective-permute-done.2.in1
  106.0 20.5 %collective-permute-done.3.in2 = bf16[16,64,256]{2,1,0:T(8,128)(2,1)S(1)} collective-permute-done((bf16[16,64,256]{2,1,0:T(8,128)(2,1)S(1)}, bf16[16,64,256]{2,1,0:T(8,128)(2,1)S(1)}, u32[]{:S(2)}, u32[]{:S(2)}) %collective-permute-start.3) | collective-permute-done | bytes 524320 | tf_op jit(solution)/shard_map/ppermute | solution.py:250
  126.5 12.7 %collective-permute-done.4.in3 = bf16[16,64,256]{2,1,0:T(8,128)(2,1)S(1)} collective-permute-done((bf16[16,64,256]{2,1,0:T(8,128)(2,1)S(1)}, bf16[16,64,256]{2,1,0:T(8,128)(2,1)S(1)}, u32[]{:S(2)}, u32[]{:S(2)}) %collective-permute-start.4) | collective-permute-done | bytes 524320 | tf_op jit(solution)/shard_map/ppermute | solution.py:250
  139.2 1.1 shard_map.39
Async XLA Ops:
  0.0 1.6 %copy-start = (bf16[16,64,1024]{2,1,0:T(8,128)(2,1)S(1)}, bf16[16,64,1024]{2,1,0:T(8,128)(2,1)}, u32[]{:S(2)}) copy-start(bf16[16,64,1024]{2,1,0:T(8,128)(2,1)} %dens.3) | copy-start | bytes 6291460
  1.6 0.7 copy-start.2
  2.3 56.7 %copy-start.1 = (bf16[16,64,1024]{2,1,0:T(8,128)(2,1)S(1)}, bf16[16,64,1024]{2,1,0:T(8,128)(2,1)}, u32[]{:S(2)}) copy-start(bf16[16,64,1024]{2,1,0:T(8,128)(2,1)} %dens.3) | copy-start | bytes 6291460
  2.3 56.7 %copy-start.3 = (s32[16,16]{1,0:T(8,128)S(1)}, s32[16,16]{1,0:T(8,128)}, u32[]{:S(2)}) copy-start(s32[16,16]{1,0:T(8,128)} %pat.3) | copy-start | bytes 3076
  2.7 56.3 %collective-permute-start = (bf16[9,64,1024]{2,1,0:T(8,128)(2,1)S(1)}, bf16[9,64,1024]{2,1,0:T(8,128)(2,1)S(1)}, u32[]{:S(2)}, u32[]{:S(2)}) collective-permute-start(bf16[9,64,1024]{2,1,0:T(8,128)(2,1)S(1)} %get-tuple-element.11), channel_id=1, source_target_pairs={{1,0},{3,2},{6,3},{5,4},{7,6},{10,7},{9,8},{11,10},{14,11},{13,12}... | collective-permute-start | bytes 3538952 | tf_op jit(solution)/shard_map/ppermute | solution.py:230
  4.1 101.8 %copy-start.4 = (s32[16,4]{0,1:T(4,128)S(1)}, s32[16,4]{0,1:T(4,128)}, u32[]{:S(2)}) copy-start(s32[16,4]{0,1:T(4,128)} %param.5) | copy-start | bytes 772
  4.1 54.8 %collective-permute-start.1 = (bf16[9,64,1024]{2,1,0:T(8,128)(2,1)S(1)}, bf16[9,64,1024]{2,1,0:T(8,128)(2,1)S(1)}, u32[]{:S(2)}, u32[]{:S(2)}) collective-permute-start(bf16[9,64,1024]{2,1,0:T(8,128)(2,1)S(1)} %get-tuple-element.12), channel_id=1, source_target_pairs={{4,0},{6,2},{7,3},{8,4},{10,6},{11,7},{12,8},{14,10},{15,11},{16,1... | collective-permute-start | bytes 3538952 | tf_op jit(solution)/shard_map/ppermute | solution.py:231
  64.5 41.5 %collective-permute-start.2 = (bf16[16,64,256]{2,1,0:T(8,128)(2,1)}, bf16[16,64,256]{2,1,0:T(8,128)(2,1)S(1)}, u32[]{:S(2)}, u32[]{:S(2)}) collective-permute-start(bf16[16,64,256]{2,1,0:T(8,128)(2,1)} %get-tuple-element.14), channel_id=1, source_target_pairs={{0,1},{2,3},{3,0},{4,5},{6,7},{7,4},{8,9},{10,11},{11,8},{12,13},{... | collective-permute-start | bytes 1572872 | tf_op jit(solution)/shard_map/ppermute | solution.py:250
  66.5 60.0 %collective-permute-start.3 = (bf16[16,64,256]{2,1,0:T(8,128)(2,1)S(1)}, bf16[16,64,256]{2,1,0:T(8,128)(2,1)S(1)}, u32[]{:S(2)}, u32[]{:S(2)}) collective-permute-start(bf16[16,64,256]{2,1,0:T(8,128)(2,1)S(1)} %get-tuple-element.15), channel_id=1, source_target_pairs={{0,2},{2,0},{3,1},{4,6},{6,4},{7,5},{8,10},{10,8},{11,9},{12,14},{... | collective-permute-start | bytes 1572872 | tf_op jit(solution)/shard_map/ppermute | solution.py:250
  104.6 34.7 %collective-permute-start.4 = (bf16[16,64,256]{2,1,0:T(8,128)(2,1)S(1)}, bf16[16,64,256]{2,1,0:T(8,128)(2,1)S(1)}, u32[]{:S(2)}, u32[]{:S(2)}) collective-permute-start(bf16[16,64,256]{2,1,0:T(8,128)(2,1)S(1)} %get-tuple-element.16), channel_id=1, source_target_pairs={{0,3},{2,1},{3,2},{4,7},{6,5},{7,6},{8,11},{10,9},{11,10},{12,15},... | collective-permute-start | bytes 1572872 | tf_op jit(solution)/shard_map/ppermute | solution.py:250

commit v2 on v1

v2 whole, which is shorter than its diff:
```python
import functools
import jax
import jax.numpy as jnp
from jax import lax
from jax.experimental import pallas as pl
from jax.experimental.pallas import tpu as pltpu
from jax.sharding import PartitionSpec as P

BS = 64
ROWS = 16
WIDE = ROWS * BS
HALF = WIDE // 2
TILE = 256
AXES = ("row", "col", "depth")
NT = (((1,), (1,)), ((), ()))
NN = (((1,), (0,)), ((), ()))


def dot(a, b, dims):
    return lax.dot_general(a, b, dims, preferred_element_type=jnp.float32)


def expand(flags, cols):
    count = flags.shape[1]
    slot = lax.broadcasted_iota(jnp.int32, (count, cols), 0)
    col = lax.broadcasted_iota(jnp.int32, (count, cols), 1)
    spread = jnp.where((col >= slot * BS) & (col < slot * BS + BS), 1.0, 0.0)
    return dot(flags.astype(jnp.float32), spread, NN)


def masked_lanes(dens, mask, i, lo, hi):
    m = jnp.broadcast_to(mask[i : i + 1, lo:hi], (16, hi - lo)).astype(jnp.bfloat16)
    x = dens[i, :, lo:hi].reshape(BS // 16, 16, hi - lo)
    return (x * m[None]).reshape(BS, hi - lo)


def upper_width(i):
    return WIDE - 128 * (i // 2)


def lower_width(i):
    return 128 * ((i - 1) // 2 + 1)


def lower_place(i):
    a, e = (i - 1) // 2, (i - 1) % 2
    width = lower_width(i)
    if a < 3:
        return [(2 * (2 * a + e) + 1, HALF - width, 0, width)]
    if a == 3:
        return [(12 + e, 0, 0, width)]
    row = 7 if i == ROWS - 1 else 2 * (6 - a) + e
    return [(2 * row, 0, 0, HALF), (2 * row + 1, 0, HALF, width - HALF)]


def pack_kernel(dens, pat, send_a, send_b, mask):
    q = lax.axis_index("depth")
    mask[...] = expand(pat[...], WIDE)

    def put(n, lo, hi, part):
        send_b[n, :, lo:hi] = part

        @pl.when(q != 2)
        def _():
            send_a[n, :, lo:hi] = part

    def own(i, lo, hi):
        return masked_lanes(dens, mask, i, lo, hi)

    put(0, 0, HALF, own(0, 0, HALF))
    put(1, 0, HALF, own(0, HALF, WIDE))
    for i in range(1, 8):
        put(1 + i, 0, HALF, own(i, 0, HALF))
        split = HALF - BS * i
        left = own(i, HALF, WIDE - 128 * (i // 2))[:, :split]
        right = own(ROWS - i, 0, 128 * ((i + 1) // 2))[:, : BS * i]
        put(9 + i, 0, HALF, jnp.concatenate([left, right], axis=1))
    put(9, 0, HALF, own(8, 0, HALF))

    @pl.when(q == 2)
    def _():
        for i in range(1, ROWS):
            width = lower_width(i)
            part = own(i, WIDE - width, WIDE)
            for n, lane, first, lanes in lower_place(i):
                send_a[n, :, lane : lane + lanes] = part[:, first : first + lanes]
        send_a[16] = jnp.zeros((BS, HALF), jnp.bfloat16)


def own_parts(dens, mask):
    def upper(i):
        return masked_lanes(dens, mask, i, 0, upper_width(i))

    def lower(i):
        return masked_lanes(dens, mask, i, WIDE - lower_width(i), WIDE)

    return lower, upper


def sent_upper(buf):
    def get(i):
        if i == 0:
            return jnp.concatenate([buf[0], buf[1]], axis=1)
        if i < 8:
            rest = HALF - 128 * (i // 2)
            if rest == 0:
                return buf[1 + i]
            return jnp.concatenate([buf[1 + i], buf[9 + i, :, :rest]], axis=1)
        return buf[9 + ROWS - i if i > 8 else 9]

    return get


def sent_lower(buf):
    def get(i):
        pieces = [buf[n, :, lane : lane + lanes] for n, lane, _, lanes in lower_place(i)]
        return pieces[0] if len(pieces) == 1 else jnp.concatenate(pieces, axis=1)

    return get


def build(dst, base, lower, upper, packed=False):
    lane = lax.broadcasted_iota(jnp.int32, (BS, WIDE), 1)
    for i in range(ROWS):
        rows = slice(base + i * BS, base + (i + 1) * BS)
        parts = []
        if i > 0:
            parts.append(lower(i) if lower else jnp.zeros((BS, lower_width(i)), jnp.bfloat16))
        placed = packed and i >= 8
        if upper and not placed:
            parts.append(upper(i))
        else:
            parts.append(jnp.zeros((BS, upper_width(i)), jnp.bfloat16))
        both = jnp.concatenate(parts, axis=1) if i > 0 else parts[0]
        if i % 2:
            both = both[:, BS : BS + WIDE]
            if not lower:
                both = jnp.where(lane >= i * BS, both, jnp.zeros_like(both))
            if not upper or placed:
                both = jnp.where(lane < i * BS, both, jnp.zeros_like(both))
        if placed:
            dst[rows, :HALF] = both[:, :HALF]
            right = jnp.where(lane[:, HALF:] >= i * BS, upper(i), both[:, HALF:])
            dst[rows, HALF:] = right
        else:
            dst[rows, :] = both


def mirror(dst, base):
    r = lax.broadcasted_iota(jnp.int32, (TILE, TILE), 0)
    c = lax.broadcasted_iota(jnp.int32, (TILE, TILE), 1)
    eye = jnp.where(r == c, 1.0, 0.0).astype(jnp.bfloat16)
    above = lax.shift_right_logical(r, 6) < lax.shift_right_logical(c, 6)
    strict = jnp.where(above, 1.0, 0.0).astype(jnp.bfloat16)
    for n in range(WIDE // TILE):
        rows = slice(base + n * TILE, base + (n + 1) * TILE)
        cols = slice(n * TILE, (n + 1) * TILE)
        diag = dst[rows, cols]
        dst[rows, cols] = diag + dot(eye, diag * strict, NT).astype(jnp.bfloat16)
        for m in range(n + 1, WIDE // TILE):
            tile = dst[rows, m * TILE : (m + 1) * TILE]
            turned = dot(eye, tile, NT).astype(jnp.bfloat16)
            dst[base + m * TILE : base + (m + 1) * TILE, cols] = turned


def prepare_kernel(dens, pat, y, mask):
    q = lax.axis_index("depth")

    @pl.when((q == 0) | (q == 2))
    def _():
        mask[...] = expand(pat[...], WIDE)
        build(y, 0, None, own_parts(dens, mask)[1])

    @pl.when(q == 2)
    def _():
        mirror(y, 0)


def main_kernel(dens, pat, y, buf_a, buf_b, own, up1, down1, up2, down2, mask, z):
    q = lax.axis_index("depth")
    mask[...] = expand(pat[...], WIDE)
    own_lower, own_upper = own_parts(dens, mask)

    def finish(static_q, tile_row, window):
        for n in range(TILE // BS):
            i = tile_row * (TILE // BS) + n
            row = window[n * BS : (n + 1) * BS, n * BS : n * BS + WIDE].astype(jnp.bfloat16)

            def share(p):
                p = p % 4
                return row[:, p * TILE : (p + 1) * TILE]

            own[i] = share(static_q)
            up2[i] = share(static_q + 1)
            down2[i] = share(static_q - 1)
            if i < 8:
                up1[i] = share(static_q + 2)
            else:
                down1[i - 8] = share(static_q + 2)

    def products(static_q):
        for t in range(WIDE // TILE):
            lo, hi = t * TILE, (t + 1) * TILE
            depth_hi = hi if static_q == 3 else WIDE
            window = dot(z[lo:hi, :depth_hi], z[lo : lo + WIDE + TILE, :depth_hi], NT)
            if static_q == 0:
                first = dot(y[lo:hi, lo:], y[lo:, lo:], NT)
                window = jnp.concatenate(
                    [window[:, : WIDE - lo] + first, window[:, WIDE - lo :]], axis=1
                )
            if static_q == 2:
                first = dot(y[lo:hi, :], y[lo:, :], NT)
                second = dot(y[lo:hi, :], z[:WIDE, :hi], NN)
                window = window + jnp.concatenate([first, second], axis=1)
            finish(static_q, t, window)

    @pl.when(q == 0)
    def _():
        build(z, 0, own_lower, sent_upper(buf_a), True)
        build(z, WIDE, None, sent_upper(buf_b), True)
        products(0)

    @pl.when(q == 1)
    def _():
        for ref in (own, up1, down1, up2, down2):
            ref[...] = jnp.zeros_like(ref)

    @pl.when(q == 2)
    def _():
        build(z, 0, own_lower, sent_upper(buf_a), True)
        build(z, WIDE, None, sent_upper(buf_b), True)
        mirror(z, WIDE)
        products(2)

    @pl.when(q == 3)
    def _():
        build(z, 0, own_lower, None)
        build(z, WIDE, sent_lower(buf_a), sent_upper(buf_b), True)
        products(3)


def add_kernel(up2, down2, got_up, got_down, up_out, down_out):
    for i in range(8):
        total = up2[i].astype(jnp.float32) + got_up[i].astype(jnp.float32)
        up_out[i] = total.astype(jnp.bfloat16)
        down_out[i] = down2[i]
        total = down2[8 + i].astype(jnp.float32) + got_down[i].astype(jnp.float32)
        down_out[8 + i] = total.astype(jnp.bfloat16)
        up_out[8 + i] = up2[8 + i]


def final_kernel(own, got_up, got_down, keep, out, mask):
    mask[...] = expand(keep[...], TILE)
    for i in range(ROWS):
        total = own[i].astype(jnp.float32) + got_up[i].astype(jnp.float32)
        total = total + got_down[i].astype(jnp.float32)
        out[i] = (total * mask[i : i + 1, :]).astype(jnp.bfloat16)


def vmem(count):
    return [pl.BlockSpec(memory_space=pltpu.VMEM)] * count


def per_device(groups, density, pattern, keep_filter):
    mib = 1024 * 1024

    def call(kernel, outs, scratch, limit, flops, moved, *operands):
        return pl.pallas_call(
            kernel,
            out_shape=tuple(jax.ShapeDtypeStruct(shape, jnp.bfloat16) for shape in outs),
            in_specs=vmem(len(operands)),
            out_specs=tuple(vmem(len(outs))),
            scratch_shapes=scratch,
            compiler_params=pltpu.CompilerParams(vmem_limit_bytes=limit * mib),
            cost_estimate=pl.CostEstimate(flops=flops, bytes_accessed=moved, transcendentals=0),
        )(*operands)

    packed = (17, BS, HALF)
    share = (ROWS, BS, TILE)
    half_share = (ROWS // 2, BS, TILE)
    slot_mask = pltpu.VMEM((ROWS, WIDE), jnp.float32)

    send_a, send_b = call(
        pack_kernel, (packed,) * 2, [slot_mask], 24, 4_000_000, 4_500_000, density, pattern
    )

    def device(g, q):
        return (g % groups) * 4 + q

    route_a, route_b = [], []
    for g in range(groups):
        route_a += [(device(g, 1), device(g, 0)), (device(g, 3), device(g, 2))]
        route_a += [(device(g + 1, 2), device(g, 3))]
        route_b += [(device(g + 1, q), device(g, q)) for q in (0, 2, 3)]
    buf_a = lax.ppermute(send_a, AXES, route_a)
    buf_b = lax.ppermute(send_b, AXES, route_b)

    (prepared,) = call(
        prepare_kernel, ((WIDE, WIDE),), [slot_mask], 24, 1_000_000_000, 4_500_000, density, pattern
    )
    own, up1, down1, up2, down2 = call(
        main_kernel,
        (share, half_share, half_share, share, share),
        [slot_mask, pltpu.VMEM((2 * WIDE, WIDE), jnp.bfloat16)],
        40,
        8_000_000_000,
        9_000_000,
        density,
        pattern,
        prepared,
        buf_a,
        buf_b,
    )

    upwards = [(q, (q + 1) % 4) for q in range(4)]
    downwards = [(q, (q - 1) % 4) for q in range(4)]
    got_up = lax.ppermute(up1, "depth", upwards)
    got_down = lax.ppermute(down1, "depth", downwards)
    up2, down2 = call(
        add_kernel, (share,) * 2, [], 16, 1_000_000, 3_000_000, up2, down2, got_up, got_down
    )
    got_up = lax.ppermute(up2, "depth", upwards)
    got_down = lax.ppermute(down2, "depth", downwards)
    (out,) = call(
        final_kernel,
        (share,),
        [pltpu.VMEM((ROWS, TILE), jnp.float32)],
        16,
        1_500_000,
        2_700_000,
        own,
        got_up,
        got_down,
        keep_filter,
    )
    return out


def solution(mesh):
    placed = (
        P(("row", "col"), None, "depth"),
        P(("row", "col"), "depth"),
        P(("row", "col"), "depth"),
    )
    groups = mesh.shape["row"] * mesh.shape["col"]
    return jax.shard_map(
        functools.partial(per_device, groups),
        mesh=mesh,
        in_specs=placed,
        out_specs=P(("row", "col"), None, "depth"),
        check_vma=False,
    )
```

time: 141 us -> 145 us (1.028)
  the two profiles are of different devices: /device:TPU:59 before, /device:TPU:122 now
where the time goes in v2:
time: 145 us
  waiting for transfers between devices  85.6 us (59%)
  starting transfers between devices  49.9 us (34%)
  Pallas kernels  6.9 us (5%)
  local copies, waits for them, and re-layouts  2.39 us (2%)
    ppermute x1, starting transfers between devices, per_device(): got_down = lax.ppermute(down1, 'depth', downwards)  31.3 us
    ppermute x1, waiting for transfers between devices, per_device(): buf_a = lax.ppermute(send_a, AXES, route_a)  25 us
    ppermute x1, waiting for transfers between devices, per_device(): got_down = lax.ppermute(down1, 'depth', downwards)  23.3 us
    ppermute x1, waiting for transfers between devices, per_device(): got_up = lax.ppermute(up2, 'depth', upwards)  20.2 us
    ppermute x1, waiting for transfers between devices, per_device(): got_up = lax.ppermute(up1, 'depth', upwards)  10.8 us
    ppermute x1, starting transfers between devices, per_device(): got_up = lax.ppermute(up2, 'depth', upwards)  10.1 us
    pallas_call x5, Pallas kernels, call(): pl.pallas_call(kernel, out_shape=tuple((jax.ShapeDtypeStruct(shape, jnp.b...  6.9 us
    ppermute x1, waiting for transfers between devices, per_device(): got_down = lax.ppermute(down2, 'depth', downwards)  5.05 us
  transfers between devices with their start and end apart: 6, of which 6 were waited for; matrix products, arithmetic and copies ran while one was open for 0% of the time, Pallas kernels for 0%

profile of v2, /device:TPU:122, one launch (start us, length us, event | category | flops | bytes accessed | tf_op | source)
XLA Modules:
  0.0 144.8 jit_solution(7098299779130436689)
XLA Ops:
  0.0 0.0 copy-start
  0.0 1.6 %copy-done = bf16[16,64,1024]{2,1,0:T(8,128)(2,1)S(1)} copy-done((bf16[16,64,1024]{2,1,0:T(8,128)(2,1)S(1)}, bf16[16,64,1024]{2,1,0:T(8,128)(2,1)}, u32[]{:S(2)}) %copy-start) | copy-done | bytes 2097176
  1.6 0.0 copy-start.2
  1.6 0.7 copy-done.2
  2.3 0.6 shard_map.38
  2.9 1.3 collective-permute-start
  4.2 0.0 copy-start.1
  4.2 0.0 copy-start.3
  4.2 3.4 %collective-permute-start.1 = (bf16[17,64,512]{2,1,0:T(8,128)(2,1)S(1)}, bf16[17,64,512]{2,1,0:T(8,128)(2,1)S(1)}, u32[]{:S(2)}, u32[]{:S(2)}) collective-permute-start(bf16[17,64,512]{2,1,0:T(8,128)(2,1)S(1)} %get-tuple-element.15), channel_id=1, source_target_pairs={{4,0},{6,2},{7,3},{8,4},{10,6},{11,7},{12,8},{14,10},{15,11},{16,1... | collective-permute-start | bytes 3342344 | tf_op jit(solution)/shard_map/ppermute | solution.py:296
  7.6 0.4 shard_map.37.y
  8.1 25.0 %collective-permute-done.buf_a = bf16[17,64,512]{2,1,0:T(8,128)(2,1)S(1)} collective-permute-done((bf16[17,64,512]{2,1,0:T(8,128)(2,1)S(1)}, bf16[17,64,512]{2,1,0:T(8,128)(2,1)S(1)}, u32[]{:S(2)}, u32[]{:S(2)}) %collective-permute-start) | collective-permute-done | bytes 1114144 | tf_op jit(solution)/shard_map/ppermute | solution.py:295
  33.0 1.3 collective-permute-done.1.buf_b
  34.3 0.0 copy-done.1
  34.3 0.0 copy-done.3
  34.3 4.7 %shard_map.39 = (bf16[16,64,256]{2,1,0:T(8,128)(2,1)S(1)}, bf16[8,64,256]{2,1,0:T(8,128)(2,1)S(1)}, bf16[8,64,256]{2,1,0:T(8,128)(2,1)S(1)}, bf16[16,64,256]{2,1,0:T(8,128)(2,1)S(1)}, bf16[16,64,256]{2,1,0:T(8,128)(2,1)S(1)}) custom-call(bf16[16,64,1024]{2,1,0:T(8,128)(2,1)S(1)} %copy-done.1, s32[16,16]{1,0:T(8,128)S(1)} %copy-done.3, ...), custom_call_target="tpu_custom_call" | custom-call | flops 8000000000 | bytes 9000000 | tf_op jit(solution)/shard_map/pallas_call | solution.py:268
  39.0 0.0 copy-start.4
  39.0 1.9 %collective-permute-start.2 = (bf16[8,64,256]{2,1,0:T(8,128)(2,1)S(1)}, bf16[8,64,256]{2,1,0:T(8,128)(2,1)S(1)}, u32[]{:S(2)}, u32[]{:S(2)}) collective-permute-start(bf16[8,64,256]{2,1,0:T(8,128)(2,1)S(1)} %get-tuple-element.19), channel_id=1, source_target_pairs={{0,1},{1,2},{2,3},{3,0},{4,5},{5,6},{6,7},{7,4},{8,9},{9,10},{10,1... | collective-permute-start | bytes 786440 | tf_op jit(solution)/shard_map/ppermute | solution.py:317
  40.9 31.3 %collective-permute-start.3 = (bf16[8,64,256]{2,1,0:T(8,128)(2,1)S(1)}, bf16[8,64,256]{2,1,0:T(8,128)(2,1)S(1)}, u32[]{:S(2)}, u32[]{:S(2)}) collective-permute-start(bf16[8,64,256]{2,1,0:T(8,128)(2,1)S(1)} %get-tuple-element.20), channel_id=1, source_target_pairs={{0,3},{1,0},{2,1},{3,2},{4,7},{5,4},{6,5},{7,6},{8,11},{9,8},{10,9... | collective-permute-start | bytes 786440 | tf_op jit(solution)/shard_map/ppermute | solution.py:318
  72.2 10.8 %collective-permute-done.2.got_up = bf16[8,64,256]{2,1,0:T(8,128)(2,1)S(1)} collective-permute-done((bf16[8,64,256]{2,1,0:T(8,128)(2,1)S(1)}, bf16[8,64,256]{2,1,0:T(8,128)(2,1)S(1)}, u32[]{:S(2)}, u32[]{:S(2)}) %collective-permute-start.2) | collective-permute-done | bytes 262176 | tf_op jit(solution)/shard_map/ppermute | solution.py:317
  83.0 23.3 %collective-permute-done.3.got_down = bf16[8,64,256]{2,1,0:T(8,128)(2,1)S(1)} collective-permute-done((bf16[8,64,256]{2,1,0:T(8,128)(2,1)S(1)}, bf16[8,64,256]{2,1,0:T(8,128)(2,1)S(1)}, u32[]{:S(2)}, u32[]{:S(2)}) %collective-permute-start.3) | collective-permute-done | bytes 262176 | tf_op jit(solution)/shard_map/ppermute | solution.py:318
  106.3 0.1 shard_map.40
  106.4 10.1 %collective-permute-start.4 = (bf16[16,64,256]{2,1,0:T(8,128)(2,1)S(1)}, bf16[16,64,256]{2,1,0:T(8,128)(2,1)S(1)}, u32[]{:S(2)}, u32[]{:S(2)}) collective-permute-start(bf16[16,64,256]{2,1,0:T(8,128)(2,1)S(1)} %get-tuple-element.21), channel_id=1, source_target_pairs={{0,1},{1,2},{2,3},{3,0},{4,5},{5,6},{6,7},{7,4},{8,9},{9,10},{10,1... | collective-permute-start | bytes 1572872 | tf_op jit(solution)/shard_map/ppermute | solution.py:322
  116.5 1.9 %collective-permute-start.5 = (bf16[16,64,256]{2,1,0:T(8,128)(2,1)S(1)}, bf16[16,64,256]{2,1,0:T(8,128)(2,1)S(1)}, u32[]{:S(2)}, u32[]{:S(2)}) collective-permute-start(bf16[16,64,256]{2,1,0:T(8,128)(2,1)S(1)} %get-tuple-element.22), channel_id=1, source_target_pairs={{0,3},{1,0},{2,1},{3,2},{4,7},{5,4},{6,5},{7,6},{8,11},{9,8},{10,9... | collective-permute-start | bytes 1572872 | tf_op jit(solution)/shard_map/ppermute | solution.py:323
  118.4 0.0 copy-done.4
  118.4 0.1 copy.4.keep
  118.5 20.2 %collective-permute-done.4.got_up = bf16[16,64,256]{2,1,0:T(8,128)(2,1)S(1)} collective-permute-done((bf16[16,64,256]{2,1,0:T(8,128)(2,1)S(1)}, bf16[16,64,256]{2,1,0:T(8,128)(2,1)S(1)}, u32[]{:S(2)}, u32[]{:S(2)}) %collective-permute-start.4) | collective-permute-done | bytes 524320 | tf_op jit(solution)/shard_map/ppermute | solution.py:322
  138.7 5.0 %collective-permute-done.5.got_down = bf16[16,64,256]{2,1,0:T(8,128)(2,1)S(1)} collective-permute-done((bf16[16,64,256]{2,1,0:T(8,128)(2,1)S(1)}, bf16[16,64,256]{2,1,0:T(8,128)(2,1)S(1)}, u32[]{:S(2)}, u32[]{:S(2)}) %collective-permute-start.5) | collective-permute-done | bytes 524320 | tf_op jit(solution)/shard_map/ppermute | solution.py:323
  143.8 1.1 shard_map.41
Async XLA Ops:
  0.0 1.6 %copy-start = (bf16[16,64,1024]{2,1,0:T(8,128)(2,1)S(1)}, bf16[16,64,1024]{2,1,0:T(8,128)(2,1)}, u32[]{:S(2)}) copy-start(bf16[16,64,1024]{2,1,0:T(8,128)(2,1)} %dens.5) | copy-start | bytes 6291460
  1.6 0.7 copy-start.2
  2.9 30.1 %collective-permute-start = (bf16[17,64,512]{2,1,0:T(8,128)(2,1)S(1)}, bf16[17,64,512]{2,1,0:T(8,128)(2,1)S(1)}, u32[]{:S(2)}, u32[]{:S(2)}) collective-permute-start(bf16[17,64,512]{2,1,0:T(8,128)(2,1)S(1)} %get-tuple-element.14), channel_id=1, source_target_pairs={{1,0},{3,2},{6,3},{5,4},{7,6},{10,7},{9,8},{11,10},{14,11},{13,12}... | collective-permute-start | bytes 3342344 | tf_op jit(solution)/shard_map/ppermute | solution.py:295
  4.2 30.1 %copy-start.1 = (bf16[16,64,1024]{2,1,0:T(8,128)(2,1)S(1)}, bf16[16,64,1024]{2,1,0:T(8,128)(2,1)}, u32[]{:S(2)}) copy-start(bf16[16,64,1024]{2,1,0:T(8,128)(2,1)} %dens.5) | copy-start | bytes 6291460
  4.2 30.1 %copy-start.3 = (s32[16,16]{1,0:T(8,128)S(1)}, s32[16,16]{1,0:T(8,128)}, u32[]{:S(2)}) copy-start(s32[16,16]{1,0:T(8,128)} %pat.5) | copy-start | bytes 3076
  4.2 30.1 %collective-permute-start.1 = (bf16[17,64,512]{2,1,0:T(8,128)(2,1)S(1)}, bf16[17,64,512]{2,1,0:T(8,128)(2,1)S(1)}, u32[]{:S(2)}, u32[]{:S(2)}) collective-permute-start(bf16[17,64,512]{2,1,0:T(8,128)(2,1)S(1)} %get-tuple-element.15), channel_id=1, source_target_pairs={{4,0},{6,2},{7,3},{8,4},{10,6},{11,7},{12,8},{14,10},{15,11},{16,1... | collective-permute-start | bytes 3342344 | tf_op jit(solution)/shard_map/ppermute | solution.py:296
  39.0 79.4 %copy-start.4 = (s32[16,4]{0,1:T(4,128)S(1)}, s32[16,4]{0,1:T(4,128)}, u32[]{:S(2)}) copy-start(s32[16,4]{0,1:T(4,128)} %param.5) | copy-start | bytes 772
  39.0 44.0 %collective-permute-start.2 = (bf16[8,64,256]{2,1,0:T(8,128)(2,1)S(1)}, bf16[8,64,256]{2,1,0:T(8,128)(2,1)S(1)}, u32[]{:S(2)}, u32[]{:S(2)}) collective-permute-start(bf16[8,64,256]{2,1,0:T(8,128)(2,1)S(1)} %get-tuple-element.19), channel_id=1, source_target_pairs={{0,1},{1,2},{2,3},{3,0},{4,5},{5,6},{6,7},{7,4},{8,9},{9,10},{10,1... | collective-permute-start | bytes 786440 | tf_op jit(solution)/shard_map/ppermute | solution.py:317
  40.9 65.4 %collective-permute-start.3 = (bf16[8,64,256]{2,1,0:T(8,128)(2,1)S(1)}, bf16[8,64,256]{2,1,0:T(8,128)(2,1)S(1)}, u32[]{:S(2)}, u32[]{:S(2)}) collective-permute-start(bf16[8,64,256]{2,1,0:T(8,128)(2,1)S(1)} %get-tuple-element.20), channel_id=1, source_target_pairs={{0,3},{1,0},{2,1},{3,2},{4,7},{5,4},{6,5},{7,6},{8,11},{9,8},{10,9... | collective-permute-start | bytes 786440 | tf_op jit(solution)/shard_map/ppermute | solution.py:318
  106.4 32.3 %collective-permute-start.4 = (bf16[16,64,256]{2,1,0:T(8,128)(2,1)S(1)}, bf16[16,64,256]{2,1,0:T(8,128)(2,1)S(1)}, u32[]{:S(2)}, u32[]{:S(2)}) collective-permute-start(bf16[16,64,256]{2,1,0:T(8,128)(2,1)S(1)} %get-tuple-element.21), channel_id=1, source_target_pairs={{0,1},{1,2},{2,3},{3,0},{4,5},{5,6},{6,7},{7,4},{8,9},{9,10},{10,1... | collective-permute-start | bytes 1572872 | tf_op jit(solution)/shard_map/ppermute | solution.py:322
  116.5 27.3 %collective-permute-start.5 = (bf16[16,64,256]{2,1,0:T(8,128)(2,1)S(1)}, bf16[16,64,256]{2,1,0:T(8,128)(2,1)S(1)}, u32[]{:S(2)}, u32[]{:S(2)}) collective-permute-start(bf16[16,64,256]{2,1,0:T(8,128)(2,1)S(1)} %get-tuple-element.22), channel_id=1, source_target_pairs={{0,3},{1,0},{2,1},{3,2},{4,7},{5,4},{6,5},{7,6},{8,11},{9,8},{10,9... | collective-permute-start | bytes 1572872 | tf_op jit(solution)/shard_map/ppermute | solution.py:323

commit v3 on v2

--- a/solution.py
+++ b/solution.py
@@ -32,6 +32,14 @@
     m = jnp.broadcast_to(mask[i : i + 1, lo:hi], (16, hi - lo)).astype(jnp.bfloat16)
     x = dens[i, :, lo:hi].reshape(BS // 16, 16, hi - lo)
     return (x * m[None]).reshape(BS, hi - lo)
+
+
+def group_index():
+    return lax.axis_index("row") * lax.axis_size("col") + lax.axis_index("col")
+
+
+def late_half(groups_half):
+    return group_index() >= groups_half
 
 
 def upper_width(i):
@@ -53,38 +61,52 @@
     return [(2 * row, 0, 0, HALF), (2 * row + 1, 0, HALF, width - HALF)]
 
 
-def pack_kernel(dens, pat, send_a, send_b, mask):
+def pack_kernel(groups_half, dens, pat, send_1, send_2, send_3, mask):
     q = lax.axis_index("depth")
+    late = late_half(groups_half)
     mask[...] = expand(pat[...], WIDE)
-
-    def put(n, lo, hi, part):
-        send_b[n, :, lo:hi] = part
-
-        @pl.when(q != 2)
+    upper_first = (q != 2) | jnp.logical_not(late)
+    upper_second = (q != 2) | late
+
+    def put(n, part):
+        send_3[n] = part
+
+        @pl.when(upper_first)
         def _():
-            send_a[n, :, lo:hi] = part
+            send_1[n] = part
+
+        @pl.when(upper_second)
+        def _():
+            send_2[n] = part
 
     def own(i, lo, hi):
         return masked_lanes(dens, mask, i, lo, hi)
 
-    put(0, 0, HALF, own(0, 0, HALF))
-    put(1, 0, HALF, own(0, HALF, WIDE))
+    put(0, own(0, 0, HALF))
+    put(1, own(0, HALF, WIDE))
     for i in range(1, 8):
-        put(1 + i, 0, HALF, own(i, 0, HALF))
+        put(1 + i, own(i, 0, HALF))
         split = HALF - BS * i
         left = own(i, HALF, WIDE - 128 * (i // 2))[:, :split]
         right = own(ROWS - i, 0, 128 * ((i + 1) // 2))[:, : BS * i]
-        put(9 + i, 0, HALF, jnp.concatenate([left, right], axis=1))
-    put(9, 0, HALF, own(8, 0, HALF))
-
-    @pl.when(q == 2)
-    def _():
+        put(9 + i, jnp.concatenate([left, right], axis=1))
+    put(9, own(8, 0, HALF))
+
+    def put_lower(dst):
         for i in range(1, ROWS):
             width = lower_width(i)
             part = own(i, WIDE - width, WIDE)
             for n, lane, first, lanes in lower_place(i):
-                send_a[n, :, lane : lane + lanes] = part[:, first : first + lanes]
-        send_a[16] = jnp.zeros((BS, HALF), jnp.bfloat16)
+                dst[n, :, lane : lane + lanes] = part[:, first : first + lanes]
+        dst[16] = jnp.zeros((BS, HALF), jnp.bfloat16)
+
+    @pl.when(jnp.logical_not(upper_first))
+    def _():
+        put_lower(send_1)
+
+    @pl.when(jnp.logical_not(upper_second))
+    def _():
+        put_lower(send_2)
 
 
 def own_parts(dens, mask):
@@ -97,23 +119,31 @@
     return lower, upper
 
 
+def chosen(pick, first, second, third=None, pick_third=None):
+    def get(n, lo, hi):
+        part = jnp.where(pick, first[n, :, lo:hi], second[n, :, lo:hi])
+        if third is not None:
+            part = jnp.where(pick_third, third[n, :, lo:hi], part)
+        return part
+
+    return get
+
+
 def sent_upper(buf):
     def get(i):
         if i == 0:
-            return jnp.concatenate([buf[0], buf[1]], axis=1)
+            return jnp.concatenate([buf(0, 0, HALF), buf(1, 0, HALF)], axis=1)
         if i < 8:
             rest = HALF - 128 * (i // 2)
-            if rest == 0:
-                return buf[1 + i]
-            return jnp.concatenate([buf[1 + i], buf[9 + i, :, :rest]], axis=1)
-        return buf[9 + ROWS - i if i > 8 else 9]
+            return jnp.concatenate([buf(1 + i, 0, HALF), buf(9 + i, 0, rest)], axis=1)
+        return buf(9 + ROWS - i if i > 8 else 9, 0, HALF)
 
     return get
 
 
 def sent_lower(buf):
     def get(i):
-        pieces = [buf[n, :, lane : lane + lanes] for n, lane, _, lanes in lower_place(i)]
+        pieces = [buf(n, lane, lane + lanes) for n, lane, _, lanes in lower_place(i)]
         return pieces[0] if len(pieces) == 1 else jnp.concatenate(pieces, axis=1)
 
     return get
@@ -176,8 +206,12 @@
         mirror(y, 0)
 
 
-def main_kernel(dens, pat, y, buf_a, buf_b, own, up1, down1, up2, down2, mask, z):
+def main_kernel(groups, dens, pat, y, got_1, got_2, got_3, own, up1, down1, up2, down2, mask, z):
     q = lax.axis_index("depth")
+    late = late_half(groups // 2)
+    group = group_index()
+    turn = (group == groups - 1) | (group == groups // 2 - 1)
+    next_late = late != turn
     mask[...] = expand(pat[...], WIDE)
     own_lower, own_upper = own_parts(dens, mask)
 
@@ -216,8 +250,8 @@
 
     @pl.when(q == 0)
     def _():
-        build(z, 0, own_lower, sent_upper(buf_a), True)
-        build(z, WIDE, None, sent_upper(buf_b), True)
+        build(z, 0, own_lower, sent_upper(chosen(late, got_1, got_2)), True)
+        build(z, WIDE, None, sent_upper(chosen(late, got_2, got_1)), True)
         products(0)
 
     @pl.when(q == 1)
@@ -227,15 +261,16 @@
 
     @pl.when(q == 2)
     def _():
-        build(z, 0, own_lower, sent_upper(buf_a), True)
-        build(z, WIDE, None, sent_upper(buf_b), True)
+        build(z, 0, own_lower, sent_upper(chosen(late, got_1, got_2)), True)
+        build(z, WIDE, None, sent_upper(chosen(late, got_2, got_1, got_3, turn)), True)
         mirror(z, WIDE)
         products(2)
 
     @pl.when(q == 3)
     def _():
         build(z, 0, own_lower, None)
-        build(z, WIDE, sent_lower(buf_a), sent_upper(buf_b), True)
+        lower = sent_lower(chosen(next_late, got_1, got_2))
+        build(z, WIDE, lower, sent_upper(chosen(next_late, got_2, got_1)), True)
         products(3)
 
 
@@ -280,36 +315,47 @@
     half_share = (ROWS // 2, BS, TILE)
     slot_mask = pltpu.VMEM((ROWS, WIDE), jnp.float32)
 
-    send_a, send_b = call(
-        pack_kernel, (packed,) * 2, [slot_mask], 24, 4_000_000, 4_500_000, density, pattern
+    half = groups // 2
+    sends = call(
+        functools.partial(pack_kernel, half),
+        (packed,) * 3,
+        [slot_mask],
+        24,
+        4_000_000,
+        5_500_000,
+        density,
+        pattern,
     )
 
     def device(g, q):
         return (g % groups) * 4 + q
 
-    route_a, route_b = [], []
+    routes = ([], [], [])
     for g in range(groups):
-        route_a += [(device(g, 1), device(g, 0)), (device(g, 3), device(g, 2))]
-        route_a += [(device(g + 1, 2), device(g, 3))]
-        route_b += [(device(g + 1, q), device(g, q)) for q in (0, 2, 3)]
-    buf_a = lax.ppermute(send_a, AXES, route_a)
-    buf_b = lax.ppermute(send_b, AXES, route_b)
+        late = int(g >= half)
+        over_depth, over_y = routes[1 - late], routes[late]
+        over_depth += [(device(g, 1), device(g, 0)), (device(g, 3), device(g, 2))]
+        over_depth += [(device(g, 2), device(g - 1, 3))]
+        over_y += [(device(g, 3), device(g - 1, 3))]
+        turn = g in (0, half)
+        routes[1 - late if turn else late].append((device(g, 0), device(g - 1, 0)))
+        routes[2 if turn else late].append((device(g, 2), device(g - 1, 2)))
+    got = [lax.ppermute(sent, AXES, route) for sent, route in zip(sends, routes)]
 
     (prepared,) = call(
         prepare_kernel, ((WIDE, WIDE),), [slot_mask], 24, 1_000_000_000, 4_500_000, density, pattern
     )
     own, up1, down1, up2, down2 = call(
-        main_kernel,
+        functools.partial(main_kernel, groups),
         (share, half_share, half_share, share, share),
         [slot_mask, pltpu.VMEM((2 * WIDE, WIDE), jnp.bfloat16)],
         40,
         8_000_000_000,
-        9_000_000,
+        10_000_000,
         density,
         pattern,
         prepared,
-        buf_a,
-        buf_b,
+        *got,
     )
 
     upwards = [(q, (q + 1) % 4) for q in range(4)]

time: 145 us -> 130 us (0.90)
  the two profiles are of different devices: /device:TPU:122 before, /device:TPU:64 now
where the time goes in v3:
time: 130 us
  waiting for transfers between devices  84.5 us (65%)
  starting transfers between devices  35.6 us (27%)
  Pallas kernels  7.09 us (5%)
  local copies, waits for them, and re-layouts  2.39 us (2%)
    ppermute x1, waiting for transfers between devices, per_device(): got_down = lax.ppermute(down1, 'depth', downwards)  44.3 us
    ppermute x3, waiting for transfers between devices, per_device(): lax.ppermute(sent, AXES, route)  22.3 us
    ppermute x1, starting transfers between devices, per_device(): got_up = lax.ppermute(up2, 'depth', upwards)  14 us
    ppermute x1, starting transfers between devices, per_device(): got_down = lax.ppermute(down1, 'depth', downwards)  9.46 us
    ppermute x1, waiting for transfers between devices, per_device(): got_up = lax.ppermute(up2, 'depth', upwards)  8.86 us
    ppermute x3, starting transfers between devices, per_device(): lax.ppermute(sent, AXES, route)  8.26 us
    pallas_call x5, Pallas kernels, call(): pl.pallas_call(kernel, out_shape=tuple((jax.ShapeDtypeStruct(shape, jnp.b...  7.09 us
    ppermute x1, waiting for transfers between devices, per_device(): got_down = lax.ppermute(down2, 'depth', downwards)  6.64 us
  transfers between devices with their start and end apart: 7, of which 5 were waited for; matrix products, arithmetic and copies ran while one was open for 0% of the time, Pallas kernels for 0%

profile of v3, /device:TPU:64, one launch (start us, length us, event | category | flops | bytes accessed | tf_op | source)
XLA Modules:
  0.0 129.7 jit_solution(5395678944204427788)
XLA Ops:
  0.0 0.0 copy-start
  0.0 1.6 %copy-done = bf16[16,64,1024]{2,1,0:T(8,128)(2,1)S(1)} copy-done((bf16[16,64,1024]{2,1,0:T(8,128)(2,1)S(1)}, bf16[16,64,1024]{2,1,0:T(8,128)(2,1)}, u32[]{:S(2)}) %copy-start) | copy-done | bytes 2097176
  1.6 0.0 copy-start.2
  1.6 0.7 copy-done.2
  2.3 0.7 shard_map.38
  3.0 6.1 %collective-permute-start = (bf16[17,64,512]{2,1,0:T(8,128)(2,1)S(1)}, bf16[17,64,512]{2,1,0:T(8,128)(2,1)S(1)}, u32[]{:S(2)}, u32[]{:S(2)}) collective-permute-start(bf16[17,64,512]{2,1,0:T(8,128)(2,1)S(1)} %get-tuple-element.15), channel_id=1, source_target_pairs={{3,511},{7,3},{4,0},{6,2},{11,7},{8,4},{10,6},{15,11},{12,8},{14,1... | collective-permute-start | bytes 3342344 | tf_op jit(solution)/shard_map/ppermute | solution.py:343
  9.1 1.3 collective-permute-start.1
  10.4 0.0 copy-start.1
  10.4 0.0 copy-start.3
  10.4 0.9 collective-permute-start.2
  11.3 0.4 shard_map.37.y
  11.7 22.3 %collective-permute-done.got_1 = bf16[17,64,512]{2,1,0:T(8,128)(2,1)S(1)} collective-permute-done((bf16[17,64,512]{2,1,0:T(8,128)(2,1)S(1)}, bf16[17,64,512]{2,1,0:T(8,128)(2,1)S(1)}, u32[]{:S(2)}, u32[]{:S(2)}) %collective-permute-start) | collective-permute-done | bytes 1114144 | tf_op jit(solution)/shard_map/ppermute | solution.py:343
  34.0 0.0 collective-permute-done.1.got_2
  34.0 0.0 collective-permute-done.2.got_3
  34.0 0.0 copy-done.1
  34.0 0.0 copy-done.3
  34.0 4.8 %shard_map.39 = (bf16[16,64,256]{2,1,0:T(8,128)(2,1)S(1)}, bf16[8,64,256]{2,1,0:T(8,128)(2,1)S(1)}, bf16[8,64,256]{2,1,0:T(8,128)(2,1)S(1)}, bf16[16,64,256]{2,1,0:T(8,128)(2,1)S(1)}, bf16[16,64,256]{2,1,0:T(8,128)(2,1)S(1)}) custom-call(bf16[16,64,1024]{2,1,0:T(8,128)(2,1)S(1)} %copy-done.1, s32[16,16]{1,0:T(8,128)S(1)} %copy-done.3, ...), custom_call_target="tpu_custom_call" | custom-call | flops 8000000000 | bytes 10000000 | tf_op jit(solution)/shard_map/pallas_call | solution.py:303
  38.8 0.0 copy-start.4
  38.8 1.9 %collective-permute-start.3 = (bf16[8,64,256]{2,1,0:T(8,128)(2,1)S(1)}, bf16[8,64,256]{2,1,0:T(8,128)(2,1)S(1)}, u32[]{:S(2)}, u32[]{:S(2)}) collective-permute-start(bf16[8,64,256]{2,1,0:T(8,128)(2,1)S(1)} %get-tuple-element.21), channel_id=1, source_target_pairs={{0,1},{1,2},{2,3},{3,0},{4,5},{5,6},{6,7},{7,4},{8,9},{9,10},{10,1... | collective-permute-start | bytes 786440 | tf_op jit(solution)/shard_map/ppermute | solution.py:363
  40.8 9.5 %collective-permute-start.4 = (bf16[8,64,256]{2,1,0:T(8,128)(2,1)S(1)}, bf16[8,64,256]{2,1,0:T(8,128)(2,1)S(1)}, u32[]{:S(2)}, u32[]{:S(2)}) collective-permute-start(bf16[8,64,256]{2,1,0:T(8,128)(2,1)S(1)} %get-tuple-element.22), channel_id=1, source_target_pairs={{0,3},{1,0},{2,1},{3,2},{4,7},{5,4},{6,5},{7,6},{8,11},{9,8},{10,9... | collective-permute-start | bytes 786440 | tf_op jit(solution)/shard_map/ppermute | solution.py:364
  50.2 2.4 %collective-permute-done.3.got_up = bf16[8,64,256]{2,1,0:T(8,128)(2,1)S(1)} collective-permute-done((bf16[8,64,256]{2,1,0:T(8,128)(2,1)S(1)}, bf16[8,64,256]{2,1,0:T(8,128)(2,1)S(1)}, u32[]{:S(2)}, u32[]{:S(2)}) %collective-permute-start.3) | collective-permute-done | bytes 262176 | tf_op jit(solution)/shard_map/ppermute | solution.py:363
  52.6 44.3 %collective-permute-done.4.got_down = bf16[8,64,256]{2,1,0:T(8,128)(2,1)S(1)} collective-permute-done((bf16[8,64,256]{2,1,0:T(8,128)(2,1)S(1)}, bf16[8,64,256]{2,1,0:T(8,128)(2,1)S(1)}, u32[]{:S(2)}, u32[]{:S(2)}) %collective-permute-start.4) | collective-permute-done | bytes 262176 | tf_op jit(solution)/shard_map/ppermute | solution.py:364
  96.9 0.1 shard_map.40
  97.1 14.0 %collective-permute-start.5 = (bf16[16,64,256]{2,1,0:T(8,128)(2,1)S(1)}, bf16[16,64,256]{2,1,0:T(8,128)(2,1)S(1)}, u32[]{:S(2)}, u32[]{:S(2)}) collective-permute-start(bf16[16,64,256]{2,1,0:T(8,128)(2,1)S(1)} %get-tuple-element.23), channel_id=1, source_target_pairs={{0,1},{1,2},{2,3},{3,0},{4,5},{5,6},{6,7},{7,4},{8,9},{9,10},{10,1... | collective-permute-start | bytes 1572872 | tf_op jit(solution)/shard_map/ppermute | solution.py:368
  111.1 1.9 %collective-permute-start.6 = (bf16[16,64,256]{2,1,0:T(8,128)(2,1)S(1)}, bf16[16,64,256]{2,1,0:T(8,128)(2,1)S(1)}, u32[]{:S(2)}, u32[]{:S(2)}) collective-permute-start(bf16[16,64,256]{2,1,0:T(8,128)(2,1)S(1)} %get-tuple-element.24), channel_id=1, source_target_pairs={{0,3},{1,0},{2,1},{3,2},{4,7},{5,4},{6,5},{7,6},{8,11},{9,8},{10,9... | collective-permute-start | bytes 1572872 | tf_op jit(solution)/shard_map/ppermute | solution.py:369
  113.0 0.0 copy-done.4
  113.0 0.1 copy.4.keep
  113.1 8.9 %collective-permute-done.5.got_up = bf16[16,64,256]{2,1,0:T(8,128)(2,1)S(1)} collective-permute-done((bf16[16,64,256]{2,1,0:T(8,128)(2,1)S(1)}, bf16[16,64,256]{2,1,0:T(8,128)(2,1)S(1)}, u32[]{:S(2)}, u32[]{:S(2)}) %collective-permute-start.5) | collective-permute-done | bytes 524320 | tf_op jit(solution)/shard_map/ppermute | solution.py:368
  122.0 6.6 %collective-permute-done.6.got_down = bf16[16,64,256]{2,1,0:T(8,128)(2,1)S(1)} collective-permute-done((bf16[16,64,256]{2,1,0:T(8,128)(2,1)S(1)}, bf16[16,64,256]{2,1,0:T(8,128)(2,1)S(1)}, u32[]{:S(2)}, u32[]{:S(2)}) %collective-permute-start.6) | collective-permute-done | bytes 524320 | tf_op jit(solution)/shard_map/ppermute | solution.py:369
  128.6 1.1 shard_map.41
Async XLA Ops:
  0.0 1.6 %copy-start = (bf16[16,64,1024]{2,1,0:T(8,128)(2,1)S(1)}, bf16[16,64,1024]{2,1,0:T(8,128)(2,1)}, u32[]{:S(2)}) copy-start(bf16[16,64,1024]{2,1,0:T(8,128)(2,1)} %dens.5) | copy-start | bytes 6291460
  1.6 0.7 copy-start.2
  3.0 31.0 %collective-permute-start = (bf16[17,64,512]{2,1,0:T(8,128)(2,1)S(1)}, bf16[17,64,512]{2,1,0:T(8,128)(2,1)S(1)}, u32[]{:S(2)}, u32[]{:S(2)}) collective-permute-start(bf16[17,64,512]{2,1,0:T(8,128)(2,1)S(1)} %get-tuple-element.15), channel_id=1, source_target_pairs={{3,511},{7,3},{4,0},{6,2},{11,7},{8,4},{10,6},{15,11},{12,8},{14,1... | collective-permute-start | bytes 3342344 | tf_op jit(solution)/shard_map/ppermute | solution.py:343
  9.1 24.9 %collective-permute-start.1 = (bf16[17,64,512]{2,1,0:T(8,128)(2,1)S(1)}, bf16[17,64,512]{2,1,0:T(8,128)(2,1)S(1)}, u32[]{:S(2)}, u32[]{:S(2)}) collective-permute-start(bf16[17,64,512]{2,1,0:T(8,128)(2,1)S(1)} %get-tuple-element.16), channel_id=1, source_target_pairs={{1,0},{3,2},{2,511},{0,508},{5,4},{7,6},{6,3},{9,8},{11,10},{10,7}... | collective-permute-start | bytes 3342344 | tf_op jit(solution)/shard_map/ppermute | solution.py:343
  10.4 23.6 %copy-start.1 = (bf16[16,64,1024]{2,1,0:T(8,128)(2,1)S(1)}, bf16[16,64,1024]{2,1,0:T(8,128)(2,1)}, u32[]{:S(2)}) copy-start(bf16[16,64,1024]{2,1,0:T(8,128)(2,1)} %dens.5) | copy-start | bytes 6291460
  10.4 23.6 %copy-start.3 = (s32[16,16]{1,0:T(8,128)S(1)}, s32[16,16]{1,0:T(8,128)}, u32[]{:S(2)}) copy-start(s32[16,16]{1,0:T(8,128)} %pat.5) | copy-start | bytes 3076
  10.4 23.6 %collective-permute-start.2 = (bf16[17,64,512]{2,1,0:T(8,128)(2,1)S(1)}, bf16[17,64,512]{2,1,0:T(8,128)(2,1)S(1)}, u32[]{:S(2)}, u32[]{:S(2)}) collective-permute-start(bf16[17,64,512]{2,1,0:T(8,128)(2,1)S(1)} %get-tuple-element.17), channel_id=1, source_target_pairs={{2,510},{258,254}} | collective-permute-start | bytes 3342344 | tf_op jit(solution)/shard_map/ppermute | solution.py:343
  38.8 74.2 %copy-start.4 = (s32[16,4]{0,1:T(4,128)S(1)}, s32[16,4]{0,1:T(4,128)}, u32[]{:S(2)}) copy-start(s32[16,4]{0,1:T(4,128)} %param.5) | copy-start | bytes 772
  38.8 13.8 %collective-permute-start.3 = (bf16[8,64,256]{2,1,0:T(8,128)(2,1)S(1)}, bf16[8,64,256]{2,1,0:T(8,128)(2,1)S(1)}, u32[]{:S(2)}, u32[]{:S(2)}) collective-permute-start(bf16[8,64,256]{2,1,0:T(8,128)(2,1)S(1)} %get-tuple-element.21), channel_id=1, source_target_pairs={{0,1},{1,2},{2,3},{3,0},{4,5},{5,6},{6,7},{7,4},{8,9},{9,10},{10,1... | collective-permute-start | bytes 786440 | tf_op jit(solution)/shard_map/ppermute | solution.py:363
  40.8 56.2 %collective-permute-start.4 = (bf16[8,64,256]{2,1,0:T(8,128)(2,1)S(1)}, bf16[8,64,256]{2,1,0:T(8,128)(2,1)S(1)}, u32[]{:S(2)}, u32[]{:S(2)}) collective-permute-start(bf16[8,64,256]{2,1,0:T(8,128)(2,1)S(1)} %get-tuple-element.22), channel_id=1, source_target_pairs={{0,3},{1,0},{2,1},{3,2},{4,7},{5,4},{6,5},{7,6},{8,11},{9,8},{10,9... | collective-permute-start | bytes 786440 | tf_op jit(solution)/shard_map/ppermute | solution.py:364
  97.1 24.9 %collective-permute-start.5 = (bf16[16,64,256]{2,1,0:T(8,128)(2,1)S(1)}, bf16[16,64,256]{2,1,0:T(8,128)(2,1)S(1)}, u32[]{:S(2)}, u32[]{:S(2)}) collective-permute-start(bf16[16,64,256]{2,1,0:T(8,128)(2,1)S(1)} %get-tuple-element.23), channel_id=1, source_target_pairs={{0,1},{1,2},{2,3},{3,0},{4,5},{5,6},{6,7},{7,4},{8,9},{9,10},{10,1... | collective-permute-start | bytes 1572872 | tf_op jit(solution)/shard_map/ppermute | solution.py:368
  111.1 17.5 %collective-permute-start.6 = (bf16[16,64,256]{2,1,0:T(8,128)(2,1)S(1)}, bf16[16,64,256]{2,1,0:T(8,128)(2,1)S(1)}, u32[]{:S(2)}, u32[]{:S(2)}) collective-permute-start(bf16[16,64,256]{2,1,0:T(8,128)(2,1)S(1)} %get-tuple-element.24), channel_id=1, source_target_pairs={{0,3},{1,0},{2,1},{3,2},{4,7},{5,4},{6,5},{7,6},{8,11},{9,8},{10,9... | collective-permute-start | bytes 1572872 | tf_op jit(solution)/shard_map/ppermute | solution.py:369

commit v4 on v3

--- a/solution.py
+++ b/solution.py
@@ -61,16 +61,14 @@
     return [(2 * row, 0, 0, HALF), (2 * row + 1, 0, HALF, width - HALF)]
 
 
-def pack_kernel(groups_half, dens, pat, send_1, send_2, send_3, mask):
+def pack_kernel(groups_half, dens, pat, send_1, send_2, mask):
     q = lax.axis_index("depth")
     late = late_half(groups_half)
     mask[...] = expand(pat[...], WIDE)
-    upper_first = (q != 2) | jnp.logical_not(late)
-    upper_second = (q != 2) | late
+    upper_first = (q != 2) | late
+    upper_second = (q != 2) | jnp.logical_not(late)
 
     def put(n, part):
-        send_3[n] = part
-
         @pl.when(upper_first)
         def _():
             send_1[n] = part
@@ -119,12 +117,9 @@
     return lower, upper
 
 
-def chosen(pick, first, second, third=None, pick_third=None):
+def chosen(pick, first, second):
     def get(n, lo, hi):
-        part = jnp.where(pick, first[n, :, lo:hi], second[n, :, lo:hi])
-        if third is not None:
-            part = jnp.where(pick_third, third[n, :, lo:hi], part)
-        return part
+        return jnp.where(pick, first[n, :, lo:hi], second[n, :, lo:hi])
 
     return get
 
@@ -206,7 +201,9 @@
         mirror(y, 0)
 
 
-def main_kernel(groups, dens, pat, y, got_1, got_2, got_3, own, up1, down1, up2, down2, mask, z):
+def main_kernel(
+    groups, dens, pat, y, got_a1, got_a2, got_b1, got_b2, own, first1, second1, first2, second2, mask, z
+):
     q = lax.axis_index("depth")
     late = late_half(groups // 2)
     group = group_index()
@@ -225,12 +222,12 @@
                 return row[:, p * TILE : (p + 1) * TILE]
 
             own[i] = share(static_q)
-            up2[i] = share(static_q + 1)
-            down2[i] = share(static_q - 1)
+            first2[i] = jnp.where(late, share(static_q - 1), share(static_q + 1))
+            second2[i] = jnp.where(late, share(static_q + 1), share(static_q - 1))
             if i < 8:
-                up1[i] = share(static_q + 2)
+                first1[i] = share(static_q + 2)
             else:
-                down1[i - 8] = share(static_q + 2)
+                second1[i - 8] = share(static_q + 2)
 
     def products(static_q):
         for t in range(WIDE // TILE):
@@ -250,45 +247,45 @@
 
     @pl.when(q == 0)
     def _():
-        build(z, 0, own_lower, sent_upper(chosen(late, got_1, got_2)), True)
-        build(z, WIDE, None, sent_upper(chosen(late, got_2, got_1)), True)
+        build(z, 0, own_lower, sent_upper(chosen(late, got_a1, got_a2)), True)
+        build(z, WIDE, None, sent_upper(chosen(late, got_a2, got_a1)), True)
         products(0)
 
     @pl.when(q == 1)
     def _():
-        for ref in (own, up1, down1, up2, down2):
+        for ref in (own, first1, second1, first2, second2):
             ref[...] = jnp.zeros_like(ref)
 
     @pl.when(q == 2)
     def _():
-        build(z, 0, own_lower, sent_upper(chosen(late, got_1, got_2)), True)
-        build(z, WIDE, None, sent_upper(chosen(late, got_2, got_1, got_3, turn)), True)
+        build(z, 0, own_lower, sent_upper(chosen(late, got_a1, got_a2)), True)
+        build(z, WIDE, None, sent_upper(chosen(next_late, got_b1, got_b2)), True)
         mirror(z, WIDE)
         products(2)
 
     @pl.when(q == 3)
     def _():
         build(z, 0, own_lower, None)
-        lower = sent_lower(chosen(next_late, got_1, got_2))
-        build(z, WIDE, lower, sent_upper(chosen(next_late, got_2, got_1)), True)
+        lower = sent_lower(chosen(next_late, got_b2, got_b1))
+        build(z, WIDE, lower, sent_upper(chosen(next_late, got_a2, got_a1)), True)
         products(3)
 
 
-def add_kernel(up2, down2, got_up, got_down, up_out, down_out):
+def add_kernel(first, second, got_first, got_second, first_out, second_out):
     for i in range(8):
-        total = up2[i].astype(jnp.float32) + got_up[i].astype(jnp.float32)
-        up_out[i] = total.astype(jnp.bfloat16)
-        down_out[i] = down2[i]
-        total = down2[8 + i].astype(jnp.float32) + got_down[i].astype(jnp.float32)
-        down_out[8 + i] = total.astype(jnp.bfloat16)
-        up_out[8 + i] = up2[8 + i]
-
-
-def final_kernel(own, got_up, got_down, keep, out, mask):
+        total = first[i].astype(jnp.float32) + got_first[i].astype(jnp.float32)
+        first_out[i] = total.astype(jnp.bfloat16)
+        second_out[i] = second[i]
+        total = second[8 + i].astype(jnp.float32) + got_second[i].astype(jnp.float32)
+        second_out[8 + i] = total.astype(jnp.bfloat16)
+        first_out[8 + i] = first[8 + i]
+
+
+def final_kernel(own, got_first, got_second, keep, out, mask):
     mask[...] = expand(keep[...], TILE)
     for i in range(ROWS):
-        total = own[i].astype(jnp.float32) + got_up[i].astype(jnp.float32)
-        total = total + got_down[i].astype(jnp.float32)
+        total = own[i].astype(jnp.float32) + got_first[i].astype(jnp.float32)
+        total = total + got_second[i].astype(jnp.float32)
         out[i] = (total * mask[i : i + 1, :]).astype(jnp.bfloat16)
 
 
@@ -316,9 +313,9 @@
     slot_mask = pltpu.VMEM((ROWS, WIDE), jnp.float32)
 
     half = groups // 2
-    sends = call(
+    send_1, send_2 = call(
         functools.partial(pack_kernel, half),
-        (packed,) * 3,
+        (packed,) * 2,
         [slot_mask],
         24,
         4_000_000,
@@ -330,22 +327,26 @@
     def device(g, q):
         return (g % groups) * 4 + q
 
-    routes = ([], [], [])
+    routes_a, routes_b = ([], []), ([], [])
     for g in range(groups):
         late = int(g >= half)
-        over_depth, over_y = routes[1 - late], routes[late]
-        over_depth += [(device(g, 1), device(g, 0)), (device(g, 3), device(g, 2))]
-        over_depth += [(device(g, 2), device(g - 1, 3))]
-        over_y += [(device(g, 3), device(g - 1, 3))]
-        turn = g in (0, half)
-        routes[1 - late if turn else late].append((device(g, 0), device(g - 1, 0)))
-        routes[2 if turn else late].append((device(g, 2), device(g - 1, 2)))
-    got = [lax.ppermute(sent, AXES, route) for sent, route in zip(sends, routes)]
+        routes_a[1 - late].extend([(device(g, 1), device(g, 0)), (device(g, 3), device(g, 2))])
+        routes_a[late].append((device(g, 3), device(g - 1, 3)))
+        routes_a[int((g - 1) % groups >= half)].append((device(g, 0), device(g - 1, 0)))
+        routes_b[late].append((device(g, 2), device(g - 1, 3)))
+        routes_b[1 - late].append((device(g, 2), device(g - 1, 2)))
+    got = [
+        lax.ppermute(send_1, AXES, routes_a[0]),
+        lax.ppermute(send_1, AXES, routes_b[0]),
+        lax.ppermute(send_1, AXES, routes_a[1]),
+        lax.ppermute(send_2, AXES, routes_b[1]),
+    ]
+    got = [got[0], got[2], got[1], got[3]]
 
     (prepared,) = call(
         prepare_kernel, ((WIDE, WIDE),), [slot_mask], 24, 1_000_000_000, 4_500_000, density, pattern
     )
-    own, up1, down1, up2, down2 = call(
+    own, first1, second1, first2, second2 = call(
         functools.partial(main_kernel, groups),
         (share, half_share, half_share, share, share),
         [slot_mask, pltpu.VMEM((2 * WIDE, WIDE), jnp.bfloat16)],
@@ -358,15 +359,29 @@
         *got,
     )
 
-    upwards = [(q, (q + 1) % 4) for q in range(4)]
-    downwards = [(q, (q - 1) % 4) for q in range(4)]
-    got_up = lax.ppermute(up1, "depth", upwards)
-    got_down = lax.ppermute(down1, "depth", downwards)
-    up2, down2 = call(
-        add_kernel, (share,) * 2, [], 16, 1_000_000, 3_000_000, up2, down2, got_up, got_down
-    )
-    got_up = lax.ppermute(up2, "depth", upwards)
-    got_down = lax.ppermute(down2, "depth", downwards)
+    first_route, second_route = [], []
+    for g in range(groups):
+        for q in range(4):
+            up = (device(g, q), device(g, (q + 1) % 4))
+            down = (device(g, q), device(g, (q - 1) % 4))
+            first_route.append(down if g >= half else up)
+            second_route.append(up if g >= half else down)
+    got_first = lax.ppermute(first1, AXES, first_route)
+    got_second = lax.ppermute(second1, AXES, second_route)
+    first2, second2 = call(
+        add_kernel,
+        (share,) * 2,
+        [],
+        16,
+        1_000_000,
+        3_000_000,
+        first2,
+        second2,
+        got_first,
+        got_second,
+    )
+    got_first = lax.ppermute(first2, AXES, first_route)
+    got_second = lax.ppermute(second2, AXES, second_route)
     (out,) = call(
         final_kernel,
         (share,),
@@ -375,8 +390,8 @@
         1_500_000,
         2_700_000,
         own,
-        got_up,
-        got_down,
+        got_first,
+        got_second,
         keep_filter,
     )
     return out

time: 130 us -> 123 us (0.946)
  the two profiles are of different devices: /device:TPU:64 before, /device:TPU:67 now
where the time goes in v4:
time: 123 us
  starting transfers between devices  59.2 us (48%)
  waiting for transfers between devices  53.8 us (44%)
  Pallas kernels  7.11 us (6%)
  local copies, waits for them, and re-layouts  2.39 us (2%)
    ppermute x1, starting transfers between devices, per_device(): got_first = lax.ppermute(first1, AXES, first_route)  36.2 us
    ppermute x1, waiting for transfers between devices, per_device(): lax.ppermute(send_1, AXES, routes_a[0])  20.5 us
    ppermute x1, waiting for transfers between devices, per_device(): got_first = lax.ppermute(first2, AXES, first_route)  19.2 us
    ppermute x1, starting transfers between devices, per_device(): got_first = lax.ppermute(first2, AXES, first_route)  10.6 us
    ppermute x1, waiting for transfers between devices, per_device(): got_second = lax.ppermute(second1, AXES, second_route)  7.43 us
    pallas_call x5, Pallas kernels, call(): pl.pallas_call(kernel, out_shape=tuple((jax.ShapeDtypeStruct(shape, jnp.b...  7.11 us
    ppermute x1, starting transfers between devices, per_device(): lax.ppermute(send_1, AXES, routes_a[1])  5.66 us
    ppermute x1, waiting for transfers between devices, per_device(): got_second = lax.ppermute(second2, AXES, second_route)  2.82 us
  transfers between devices with their start and end apart: 8, of which 6 were waited for; matrix products, arithmetic and copies ran while one was open for 0% of the time, Pallas kernels for 0%

profile of v4, /device:TPU:67, one launch (start us, length us, event | category | flops | bytes accessed | tf_op | source)
XLA Modules:
  0.0 122.6 jit_solution(124005277128852242)
XLA Ops:
  0.0 0.0 copy-start
  0.0 1.6 %copy-done = bf16[16,64,1024]{2,1,0:T(8,128)(2,1)S(1)} copy-done((bf16[16,64,1024]{2,1,0:T(8,128)(2,1)S(1)}, bf16[16,64,1024]{2,1,0:T(8,128)(2,1)}, u32[]{:S(2)}) %copy-start) | copy-done | bytes 2097176
  1.6 0.0 copy-start.2
  1.6 0.7 copy-done.2
  2.3 0.6 shard_map.38
  2.9 1.3 %collective-permute-start = (bf16[17,64,512]{2,1,0:T(8,128)(2,1)S(1)}, bf16[17,64,512]{2,1,0:T(8,128)(2,1)S(1)}, u32[]{:S(2)}, u32[]{:S(2)}) collective-permute-start(bf16[17,64,512]{2,1,0:T(8,128)(2,1)S(1)} %get-tuple-element.14), channel_id=1, source_target_pairs={{3,511},{7,3},{4,0},{11,7},{8,4},{15,11},{12,8},{19,15},{16,12},{2... | collective-permute-start | bytes 3342344 | tf_op jit(solution)/shard_map/ppermute | solution.py:339
  4.2 5.7 %collective-permute-start.1 = (bf16[17,64,512]{2,1,0:T(8,128)(2,1)S(1)}, bf16[17,64,512]{2,1,0:T(8,128)(2,1)S(1)}, u32[]{:S(2)}, u32[]{:S(2)}) collective-permute-start(bf16[17,64,512]{2,1,0:T(8,128)(2,1)S(1)} %get-tuple-element.14), channel_id=1, source_target_pairs={{1,0},{3,2},{0,508},{5,4},{7,6},{9,8},{11,10},{13,12},{15,14},{17,... | collective-permute-start | bytes 3342344 | tf_op jit(solution)/shard_map/ppermute | solution.py:341
  9.9 0.7 collective-permute-start.2
  10.6 0.0 copy-start.1
  10.6 0.0 copy-start.3
  10.7 0.9 collective-permute-start.3
  11.5 0.4 shard_map.37.y
  12.0 20.5 %collective-permute-done.got_a1 = bf16[17,64,512]{2,1,0:T(8,128)(2,1)S(1)} collective-permute-done((bf16[17,64,512]{2,1,0:T(8,128)(2,1)S(1)}, bf16[17,64,512]{2,1,0:T(8,128)(2,1)S(1)}, u32[]{:S(2)}, u32[]{:S(2)}) %collective-permute-start) | collective-permute-done | bytes 1114144 | tf_op jit(solution)/shard_map/ppermute | solution.py:339
  32.4 1.8 %collective-permute-done.1.got_a2 = bf16[17,64,512]{2,1,0:T(8,128)(2,1)S(1)} collective-permute-done((bf16[17,64,512]{2,1,0:T(8,128)(2,1)S(1)}, bf16[17,64,512]{2,1,0:T(8,128)(2,1)S(1)}, u32[]{:S(2)}, u32[]{:S(2)}) %collective-permute-start.1) | collective-permute-done | bytes 1114144 | tf_op jit(solution)/shard_map/ppermute | solution.py:341
  34.3 0.0 collective-permute-done.2.got_b1
  34.3 0.0 collective-permute-done.3.got_b2
  34.3 0.0 copy-done.1
  34.3 0.0 copy-done.3
  34.3 4.8 %shard_map.39 = (bf16[16,64,256]{2,1,0:T(8,128)(2,1)S(1)}, bf16[8,64,256]{2,1,0:T(8,128)(2,1)S(1)}, bf16[8,64,256]{2,1,0:T(8,128)(2,1)S(1)}, bf16[16,64,256]{2,1,0:T(8,128)(2,1)S(1)}, bf16[16,64,256]{2,1,0:T(8,128)(2,1)S(1)}) custom-call(bf16[16,64,1024]{2,1,0:T(8,128)(2,1)S(1)} %copy-done.1, s32[16,16]{1,0:T(8,128)S(1)} %copy-done.3, ...), custom_call_target="tpu_custom_call" | custom-call | flops 8000000000 | bytes 10000000 | tf_op jit(solution)/shard_map/pallas_call | solution.py:300
  39.1 0.0 copy-start.4
  39.1 36.2 %collective-permute-start.4 = (bf16[8,64,256]{2,1,0:T(8,128)(2,1)S(1)}, bf16[8,64,256]{2,1,0:T(8,128)(2,1)S(1)}, u32[]{:S(2)}, u32[]{:S(2)}) collective-permute-start(bf16[8,64,256]{2,1,0:T(8,128)(2,1)S(1)} %get-tuple-element.19), channel_id=1, source_target_pairs={{0,1},{1,2},{2,3},{3,0},{4,5},{5,6},{6,7},{7,4},{8,9},{9,10},{10,1... | collective-permute-start | bytes 786440 | tf_op jit(solution)/shard_map/ppermute | solution.py:369
  75.3 1.9 %collective-permute-start.5 = (bf16[8,64,256]{2,1,0:T(8,128)(2,1)S(1)}, bf16[8,64,256]{2,1,0:T(8,128)(2,1)S(1)}, u32[]{:S(2)}, u32[]{:S(2)}) collective-permute-start(bf16[8,64,256]{2,1,0:T(8,128)(2,1)S(1)} %get-tuple-element.20), channel_id=1, source_target_pairs={{0,3},{1,0},{2,1},{3,2},{4,7},{5,4},{6,5},{7,6},{8,11},{9,8},{10,9... | collective-permute-start | bytes 786440 | tf_op jit(solution)/shard_map/ppermute | solution.py:370
  77.3 2.1 %collective-permute-done.4.got_first = bf16[8,64,256]{2,1,0:T(8,128)(2,1)S(1)} collective-permute-done((bf16[8,64,256]{2,1,0:T(8,128)(2,1)S(1)}, bf16[8,64,256]{2,1,0:T(8,128)(2,1)S(1)}, u32[]{:S(2)}, u32[]{:S(2)}) %collective-permute-start.4) | collective-permute-done | bytes 262176 | tf_op jit(solution)/shard_map/ppermute | solution.py:369
  79.4 7.4 %collective-permute-done.5.got_second = bf16[8,64,256]{2,1,0:T(8,128)(2,1)S(1)} collective-permute-done((bf16[8,64,256]{2,1,0:T(8,128)(2,1)S(1)}, bf16[8,64,256]{2,1,0:T(8,128)(2,1)S(1)}, u32[]{:S(2)}, u32[]{:S(2)}) %collective-permute-start.5) | collective-permute-done | bytes 262176 | tf_op jit(solution)/shard_map/ppermute | solution.py:370
  86.8 0.1 shard_map.40
  87.0 10.6 %collective-permute-start.6 = (bf16[16,64,256]{2,1,0:T(8,128)(2,1)S(1)}, bf16[16,64,256]{2,1,0:T(8,128)(2,1)S(1)}, u32[]{:S(2)}, u32[]{:S(2)}) collective-permute-start(bf16[16,64,256]{2,1,0:T(8,128)(2,1)S(1)} %get-tuple-element.21), channel_id=1, source_target_pairs={{0,1},{1,2},{2,3},{3,0},{4,5},{5,6},{6,7},{7,4},{8,9},{9,10},{10,1... | collective-permute-start | bytes 1572872 | tf_op jit(solution)/shard_map/ppermute | solution.py:383
  97.6 1.9 %collective-permute-start.7 = (bf16[16,64,256]{2,1,0:T(8,128)(2,1)S(1)}, bf16[16,64,256]{2,1,0:T(8,128)(2,1)S(1)}, u32[]{:S(2)}, u32[]{:S(2)}) collective-permute-start(bf16[16,64,256]{2,1,0:T(8,128)(2,1)S(1)} %get-tuple-element.22), channel_id=1, source_target_pairs={{0,3},{1,0},{2,1},{3,2},{4,7},{5,4},{6,5},{7,6},{8,11},{9,8},{10,9... | collective-permute-start | bytes 1572872 | tf_op jit(solution)/shard_map/ppermute | solution.py:384
  99.5 0.0 copy-done.4
  99.5 0.1 copy.4.keep
  99.6 19.2 %collective-permute-done.6.got_first = bf16[16,64,256]{2,1,0:T(8,128)(2,1)S(1)} collective-permute-done((bf16[16,64,256]{2,1,0:T(8,128)(2,1)S(1)}, bf16[16,64,256]{2,1,0:T(8,128)(2,1)S(1)}, u32[]{:S(2)}, u32[]{:S(2)}) %collective-permute-start.6) | collective-permute-done | bytes 524320 | tf_op jit(solution)/shard_map/ppermute | solution.py:383
  118.8 2.8 %collective-permute-done.7.got_second = bf16[16,64,256]{2,1,0:T(8,128)(2,1)S(1)} collective-permute-done((bf16[16,64,256]{2,1,0:T(8,128)(2,1)S(1)}, bf16[16,64,256]{2,1,0:T(8,128)(2,1)S(1)}, u32[]{:S(2)}, u32[]{:S(2)}) %collective-permute-start.7) | collective-permute-done | bytes 524320 | tf_op jit(solution)/shard_map/ppermute | solution.py:384
  121.6 1.1 shard_map.41
Async XLA Ops:
  0.0 1.6 %copy-start = (bf16[16,64,1024]{2,1,0:T(8,128)(2,1)S(1)}, bf16[16,64,1024]{2,1,0:T(8,128)(2,1)}, u32[]{:S(2)}) copy-start(bf16[16,64,1024]{2,1,0:T(8,128)(2,1)} %dens.5) | copy-start | bytes 6291460
  1.6 0.7 copy-start.2
  2.9 29.5 %collective-permute-start = (bf16[17,64,512]{2,1,0:T(8,128)(2,1)S(1)}, bf16[17,64,512]{2,1,0:T(8,128)(2,1)S(1)}, u32[]{:S(2)}, u32[]{:S(2)}) collective-permute-start(bf16[17,64,512]{2,1,0:T(8,128)(2,1)S(1)} %get-tuple-element.14), channel_id=1, source_target_pairs={{3,511},{7,3},{4,0},{11,7},{8,4},{15,11},{12,8},{19,15},{16,12},{2... | collective-permute-start | bytes 3342344 | tf_op jit(solution)/shard_map/ppermute | solution.py:339
  4.2 30.0 %collective-permute-start.1 = (bf16[17,64,512]{2,1,0:T(8,128)(2,1)S(1)}, bf16[17,64,512]{2,1,0:T(8,128)(2,1)S(1)}, u32[]{:S(2)}, u32[]{:S(2)}) collective-permute-start(bf16[17,64,512]{2,1,0:T(8,128)(2,1)S(1)} %get-tuple-element.14), channel_id=1, source_target_pairs={{1,0},{3,2},{0,508},{5,4},{7,6},{9,8},{11,10},{13,12},{15,14},{17,... | collective-permute-start | bytes 3342344 | tf_op jit(solution)/shard_map/ppermute | solution.py:341
  9.9 24.4 %collective-permute-start.2 = (bf16[17,64,512]{2,1,0:T(8,128)(2,1)S(1)}, bf16[17,64,512]{2,1,0:T(8,128)(2,1)S(1)}, u32[]{:S(2)}, u32[]{:S(2)}) collective-permute-start(bf16[17,64,512]{2,1,0:T(8,128)(2,1)S(1)} %get-tuple-element.14), channel_id=1, source_target_pairs={{2,511},{6,3},{10,7},{14,11},{18,15},{22,19},{26,23},{30,27},{34,3... | collective-permute-start | bytes 3342344 | tf_op jit(solution)/shard_map/ppermute | solution.py:340
  10.6 23.6 %copy-start.1 = (bf16[16,64,1024]{2,1,0:T(8,128)(2,1)S(1)}, bf16[16,64,1024]{2,1,0:T(8,128)(2,1)}, u32[]{:S(2)}) copy-start(bf16[16,64,1024]{2,1,0:T(8,128)(2,1)} %dens.5) | copy-start | bytes 6291460
  10.6 23.6 %copy-start.3 = (s32[16,16]{1,0:T(8,128)S(1)}, s32[16,16]{1,0:T(8,128)}, u32[]{:S(2)}) copy-start(s32[16,16]{1,0:T(8,128)} %pat.5) | copy-start | bytes 3076
  10.7 23.6 %collective-permute-start.3 = (bf16[17,64,512]{2,1,0:T(8,128)(2,1)S(1)}, bf16[17,64,512]{2,1,0:T(8,128)(2,1)S(1)}, u32[]{:S(2)}, u32[]{:S(2)}) collective-permute-start(bf16[17,64,512]{2,1,0:T(8,128)(2,1)S(1)} %get-tuple-element.15), channel_id=1, source_target_pairs={{2,510},{6,2},{10,6},{14,10},{18,14},{22,18},{26,22},{30,26},{34,3... | collective-permute-start | bytes 3342344 | tf_op jit(solution)/shard_map/ppermute | solution.py:342
  39.1 60.4 %copy-start.4 = (s32[16,4]{0,1:T(4,128)S(1)}, s32[16,4]{0,1:T(4,128)}, u32[]{:S(2)}) copy-start(s32[16,4]{0,1:T(4,128)} %param.5) | copy-start | bytes 772
  39.1 40.3 %collective-permute-start.4 = (bf16[8,64,256]{2,1,0:T(8,128)(2,1)S(1)}, bf16[8,64,256]{2,1,0:T(8,128)(2,1)S(1)}, u32[]{:S(2)}, u32[]{:S(2)}) collective-permute-start(bf16[8,64,256]{2,1,0:T(8,128)(2,1)S(1)} %get-tuple-element.19), channel_id=1, source_target_pairs={{0,1},{1,2},{2,3},{3,0},{4,5},{5,6},{6,7},{7,4},{8,9},{9,10},{10,1... | collective-permute-start | bytes 786440 | tf_op jit(solution)/shard_map/ppermute | solution.py:369
  75.3 11.5 %collective-permute-start.5 = (bf16[8,64,256]{2,1,0:T(8,128)(2,1)S(1)}, bf16[8,64,256]{2,1,0:T(8,128)(2,1)S(1)}, u32[]{:S(2)}, u32[]{:S(2)}) collective-permute-start(bf16[8,64,256]{2,1,0:T(8,128)(2,1)S(1)} %get-tuple-element.20), channel_id=1, source_target_pairs={{0,3},{1,0},{2,1},{3,2},{4,7},{5,4},{6,5},{7,6},{8,11},{9,8},{10,9... | collective-permute-start | bytes 786440 | tf_op jit(solution)/shard_map/ppermute | solution.py:370
  87.0 31.8 %collective-permute-start.6 = (bf16[16,64,256]{2,1,0:T(8,128)(2,1)S(1)}, bf16[16,64,256]{2,1,0:T(8,128)(2,1)S(1)}, u32[]{:S(2)}, u32[]{:S(2)}) collective-permute-start(bf16[16,64,256]{2,1,0:T(8,128)(2,1)S(1)} %get-tuple-element.21), channel_id=1, source_target_pairs={{0,1},{1,2},{2,3},{3,0},{4,5},{5,6},{6,7},{7,4},{8,9},{9,10},{10,1... | collective-permute-start | bytes 1572872 | tf_op jit(solution)/shard_map/ppermute | solution.py:383
  97.6 24.0 %collective-permute-start.7 = (bf16[16,64,256]{2,1,0:T(8,128)(2,1)S(1)}, bf16[16,64,256]{2,1,0:T(8,128)(2,1)S(1)}, u32[]{:S(2)}, u32[]{:S(2)}) collective-permute-start(bf16[16,64,256]{2,1,0:T(8,128)(2,1)S(1)} %get-tuple-element.22), channel_id=1, source_target_pairs={{0,3},{1,0},{2,1},{3,2},{4,7},{5,4},{6,5},{7,6},{8,11},{9,8},{10,9... | collective-permute-start | bytes 1572872 | tf_op jit(solution)/shard_map/ppermute | solution.py:384

commit v5 on v4

--- a/solution.py
+++ b/solution.py
@@ -61,50 +61,48 @@
     return [(2 * row, 0, 0, HALF), (2 * row + 1, 0, HALF, width - HALF)]
 
 
-def pack_kernel(groups_half, dens, pat, send_1, send_2, mask):
-    q = lax.axis_index("depth")
+def put_upper(own, put):
+    put(0, own(0, 0, HALF))
+    put(1, own(0, HALF, WIDE))
+    for i in range(1, 9):
+        put(1 + i, own(i, 0, HALF))
+    for i in range(1, 8):
+        left = own(i, HALF, WIDE - 128 * (i // 2))[:, : HALF - BS * i]
+        right = own(ROWS - i, 0, 128 * ((i + 1) // 2))[:, : BS * i]
+        put(9 + i, jnp.concatenate([left, right], axis=1))
+
+
+def pack(groups_half, dens, mask, send, lower_if_late):
     late = late_half(groups_half)
-    mask[...] = expand(pat[...], WIDE)
-    upper_first = (q != 2) | late
-    upper_second = (q != 2) | jnp.logical_not(late)
-
-    def put(n, part):
-        @pl.when(upper_first)
-        def _():
-            send_1[n] = part
-
-        @pl.when(upper_second)
-        def _():
-            send_2[n] = part
+    send_lower = (lax.axis_index("depth") == 2) & (late == lower_if_late)
 
     def own(i, lo, hi):
         return masked_lanes(dens, mask, i, lo, hi)
 
-    put(0, own(0, 0, HALF))
-    put(1, own(0, HALF, WIDE))
-    for i in range(1, 8):
-        put(1 + i, own(i, 0, HALF))
-        split = HALF - BS * i
-        left = own(i, HALF, WIDE - 128 * (i // 2))[:, :split]
-        right = own(ROWS - i, 0, 128 * ((i + 1) // 2))[:, : BS * i]
-        put(9 + i, jnp.concatenate([left, right], axis=1))
-    put(9, own(8, 0, HALF))
-
-    def put_lower(dst):
+    def put(n, part):
+        send[n] = part
+
+    @pl.when(jnp.logical_not(send_lower))
+    def _():
+        put_upper(own, put)
+
+    @pl.when(send_lower)
+    def _():
         for i in range(1, ROWS):
             width = lower_width(i)
             part = own(i, WIDE - width, WIDE)
             for n, lane, first, lanes in lower_place(i):
-                dst[n, :, lane : lane + lanes] = part[:, first : first + lanes]
-        dst[16] = jnp.zeros((BS, HALF), jnp.bfloat16)
-
-    @pl.when(jnp.logical_not(upper_first))
-    def _():
-        put_lower(send_1)
-
-    @pl.when(jnp.logical_not(upper_second))
-    def _():
-        put_lower(send_2)
+                send[n, :, lane : lane + lanes] = part[:, first : first + lanes]
+        send[16] = jnp.zeros((BS, HALF), jnp.bfloat16)
+
+
+def pack_kernel(groups_half, dens, pat, send, mask):
+    mask[...] = expand(pat[...], WIDE)
+    pack(groups_half, dens, mask, send, True)
+
+
+def pack_first_kernel(groups_half, dens, mask, send):
+    pack(groups_half, dens, mask, send, False)
 
 
 def own_parts(dens, mask):
@@ -188,28 +186,37 @@
             dst[base + m * TILE : base + (m + 1) * TILE, cols] = turned
 
 
-def prepare_kernel(dens, pat, y, mask):
+def prepare_kernel(dens, mask, y, acc):
     q = lax.axis_index("depth")
+    own_lower, own_upper = own_parts(dens, mask)
 
     @pl.when((q == 0) | (q == 2))
     def _():
-        mask[...] = expand(pat[...], WIDE)
-        build(y, 0, None, own_parts(dens, mask)[1])
+        build(y, 0, None, own_upper)
 
     @pl.when(q == 2)
     def _():
         mirror(y, 0)
 
+    @pl.when(q == 3)
+    def _():
+        build(y, 0, own_lower, None)
+
+    @pl.when(q != 1)
+    def _():
+        for t in range(WIDE // TILE):
+            lo, hi = t * TILE, (t + 1) * TILE
+            acc[t, :, : WIDE - lo] = dot(y[lo:hi, :], y[lo:, :], NT)
+
 
 def main_kernel(
-    groups, dens, pat, y, got_a1, got_a2, got_b1, got_b2, own, first1, second1, first2, second2, mask, z
+    groups, dens, mask, y, acc, got_a1, got_a2, got_b1, got_b2, own, first1, second1, first2, second2, z
 ):
     q = lax.axis_index("depth")
     late = late_half(groups // 2)
     group = group_index()
     turn = (group == groups - 1) | (group == groups // 2 - 1)
     next_late = late != turn
-    mask[...] = expand(pat[...], WIDE)
     own_lower, own_upper = own_parts(dens, mask)
 
     def finish(static_q, tile_row, window):
@@ -232,17 +239,16 @@
     def products(static_q):
         for t in range(WIDE // TILE):
             lo, hi = t * TILE, (t + 1) * TILE
-            depth_hi = hi if static_q == 3 else WIDE
-            window = dot(z[lo:hi, :depth_hi], z[lo : lo + WIDE + TILE, :depth_hi], NT)
-            if static_q == 0:
-                first = dot(y[lo:hi, lo:], y[lo:, lo:], NT)
-                window = jnp.concatenate(
-                    [window[:, : WIDE - lo] + first, window[:, WIDE - lo :]], axis=1
-                )
-            if static_q == 2:
-                first = dot(y[lo:hi, :], y[lo:, :], NT)
-                second = dot(y[lo:hi, :], z[:WIDE, :hi], NN)
-                window = window + jnp.concatenate([first, second], axis=1)
+            ahead = acc[t, :, : WIDE - lo]
+            if static_q == 3:
+                later = dot(y[lo:hi, :hi], z[WIDE : WIDE + hi, :hi], NT)
+                window = jnp.concatenate([ahead, later], axis=1)
+            else:
+                window = dot(z[lo:hi, :], z[lo : lo + WIDE + TILE, :], NT)
+                later = window[:, WIDE - lo :]
+                if static_q == 2:
+                    later = later + dot(y[lo:hi, :], z[:WIDE, :hi], NN)
+                window = jnp.concatenate([window[:, : WIDE - lo] + ahead, later], axis=1)
             finish(static_q, t, window)
 
     @pl.when(q == 0)
@@ -265,7 +271,6 @@
 
     @pl.when(q == 3)
     def _():
-        build(z, 0, own_lower, None)
         lower = sent_lower(chosen(next_late, got_b2, got_b1))
         build(z, WIDE, lower, sent_upper(chosen(next_late, got_a2, got_a1)), True)
         products(3)
@@ -295,11 +300,17 @@
 
 def per_device(groups, density, pattern, keep_filter):
     mib = 1024 * 1024
+    window_rows = (WIDE // TILE, TILE, WIDE)
+    slot_mask = (ROWS, WIDE)
+    wide_types = (window_rows, slot_mask)
 
     def call(kernel, outs, scratch, limit, flops, moved, *operands):
         return pl.pallas_call(
             kernel,
-            out_shape=tuple(jax.ShapeDtypeStruct(shape, jnp.bfloat16) for shape in outs),
+            out_shape=tuple(
+                jax.ShapeDtypeStruct(shape, jnp.float32 if shape in wide_types else jnp.bfloat16)
+                for shape in outs
+            ),
             in_specs=vmem(len(operands)),
             out_specs=tuple(vmem(len(outs))),
             scratch_shapes=scratch,
@@ -310,18 +321,37 @@
     packed = (17, BS, HALF)
     share = (ROWS, BS, TILE)
     half_share = (ROWS // 2, BS, TILE)
-    slot_mask = pltpu.VMEM((ROWS, WIDE), jnp.float32)
 
     half = groups // 2
-    send_1, send_2 = call(
+    send_2, mask = call(
         functools.partial(pack_kernel, half),
-        (packed,) * 2,
-        [slot_mask],
-        24,
+        (packed, slot_mask),
+        [],
+        16,
         4_000_000,
-        5_500_000,
+        3_500_000,
         density,
         pattern,
+    )
+    (send_1,) = call(
+        functools.partial(pack_first_kernel, half),
+        (packed,),
+        [],
+        16,
+        4_000_000,
+        3_500_000,
+        density,
+        mask,
+    )
+    prepared, ahead = call(
+        prepare_kernel,
+        ((WIDE, WIDE), window_rows),
+        [],
+        16,
+        3_000_000_000,
+        9_500_000,
+        density,
+        mask,
     )
 
     def device(g, q):
@@ -335,28 +365,26 @@
         routes_a[int((g - 1) % groups >= half)].append((device(g, 0), device(g - 1, 0)))
         routes_b[late].append((device(g, 2), device(g - 1, 3)))
         routes_b[1 - late].append((device(g, 2), device(g - 1, 2)))
-    got = [
-        lax.ppermute(send_1, AXES, routes_a[0]),
-        lax.ppermute(send_1, AXES, routes_b[0]),
-        lax.ppermute(send_1, AXES, routes_a[1]),
-        lax.ppermute(send_2, AXES, routes_b[1]),
-    ]
-    got = [got[0], got[2], got[1], got[3]]
-
-    (prepared,) = call(
-        prepare_kernel, ((WIDE, WIDE),), [slot_mask], 24, 1_000_000_000, 4_500_000, density, pattern
-    )
+    got_a1 = lax.ppermute(send_1, AXES, routes_a[0])
+    got_b1 = lax.ppermute(send_1, AXES, routes_b[0])
+    got_a2 = lax.ppermute(send_2, AXES, routes_a[1])
+    got_b2 = lax.ppermute(send_2, AXES, routes_b[1])
+
     own, first1, second1, first2, second2 = call(
         functools.partial(main_kernel, groups),
         (share, half_share, half_share, share, share),
-        [slot_mask, pltpu.VMEM((2 * WIDE, WIDE), jnp.bfloat16)],
-        40,
-        8_000_000_000,
-        10_000_000,
+        [pltpu.VMEM((2 * WIDE, WIDE), jnp.bfloat16)],
+        20,
+        6_000_000_000,
+        14_000_000,
         density,
-        pattern,
+        mask,
         prepared,
-        *got,
+        ahead,
+        got_a1,
+        got_a2,
+        got_b1,
+        got_b2,
     )
 
     first_route, second_route = [], []
@@ -366,8 +394,8 @@
             down = (device(g, q), device(g, (q - 1) % 4))
             first_route.append(down if g >= half else up)
             second_route.append(up if g >= half else down)
-    got_first = lax.ppermute(first1, AXES, first_route)
-    got_second = lax.ppermute(second1, AXES, second_route)
+    got_first = lax.ppermute(first1, AXES, [r for r in first_route if r[0] % 4 != 1])
+    got_second = lax.ppermute(second1, AXES, [r for r in second_route if r[0] % 4 != 1])
     first2, second2 = call(
         add_kernel,
         (share,) * 2,

time: 123 us -> 119 us (0.967)
  the two profiles are of different devices: /device:TPU:67 before, /device:TPU:68 now
where the time goes in v5:
time: 119 us
  starting transfers between devices  57.4 us (48%)
  waiting for transfers between devices  51.8 us (44%)
  Pallas kernels  6.82 us (6%)
  local copies, waits for them, and re-layouts  2.38 us (2%)
    ppermute x1, starting transfers between devices, per_device(): lax.ppermute(first1, AXES, [r for r in first_route if r[0] % 4 != 1])  36 us
    ppermute x1, waiting for transfers between devices, per_device(): got_a1 = lax.ppermute(send_1, AXES, routes_a[0])  20.5 us
    ppermute x1, waiting for transfers between devices, per_device(): got_first = lax.ppermute(first2, AXES, first_route)  20.5 us
    ppermute x1, starting transfers between devices, per_device(): got_first = lax.ppermute(first2, AXES, first_route)  9.91 us
    pallas_call x6, Pallas kernels, call(): pl.pallas_call(kernel, out_shape=tuple((jax.ShapeDtypeStruct(shape, jnp.f...  6.82 us
    ppermute x1, waiting for transfers between devices, per_device(): lax.ppermute(second1, AXES, [r for r in second_route if r[0] % 4 != 1])  6.4 us
    ppermute x1, starting transfers between devices, per_device(): got_a2 = lax.ppermute(send_2, AXES, routes_a[1])  4.92 us
    ppermute x1, waiting for transfers between devices, per_device(): lax.ppermute(first1, AXES, [r for r in first_route if r[0] % 4 != 1])  2.62 us
  transfers between devices with their start and end apart: 8, of which 5 were waited for; matrix products, arithmetic and copies ran while one was open for 0% of the time, Pallas kernels for 2%

profile of v5, /device:TPU:68, one launch (start us, length us, event | category | flops | bytes accessed | tf_op | source)
XLA Modules:
  0.0 118.5 jit_solution(15587424181273437655)
XLA Ops:
  0.0 0.0 copy-start
  0.0 1.6 %copy-done = bf16[16,64,1024]{2,1,0:T(8,128)(2,1)S(1)} copy-done((bf16[16,64,1024]{2,1,0:T(8,128)(2,1)S(1)}, bf16[16,64,1024]{2,1,0:T(8,128)(2,1)}, u32[]{:S(2)}) %copy-start) | copy-done | bytes 2097176
  1.6 0.0 copy-start.2
  1.6 0.7 copy-done.2
  2.3 0.2 shard_map.37
  2.5 0.1 shard_map.39
  2.7 1.3 %collective-permute-start = (bf16[17,64,512]{2,1,0:T(8,128)(2,1)S(1)}, bf16[17,64,512]{2,1,0:T(8,128)(2,1)S(1)}, u32[]{:S(2)}, u32[]{:S(2)}) collective-permute-start(bf16[17,64,512]{2,1,0:T(8,128)(2,1)S(1)} %shard_map.39), channel_id=1, source_target_pairs={{3,511},{7,3},{4,0},{11,7},{8,4},{15,11},{12,8},{19,15},{16,12},{2... | collective-permute-start | bytes 3342344 | tf_op jit(solution)/shard_map/ppermute | solution.py:368
  4.0 0.7 collective-permute-start.2
  4.7 0.0 copy-start.1
  4.7 4.9 %collective-permute-start.1 = (bf16[17,64,512]{2,1,0:T(8,128)(2,1)S(1)}, bf16[17,64,512]{2,1,0:T(8,128)(2,1)S(1)}, u32[]{:S(2)}, u32[]{:S(2)}) collective-permute-start(bf16[17,64,512]{2,1,0:T(8,128)(2,1)S(1)} %get-tuple-element.19), channel_id=1, source_target_pairs={{1,0},{3,2},{0,508},{5,4},{7,6},{9,8},{11,10},{13,12},{15,14},{17,... | collective-permute-start | bytes 3342344 | tf_op jit(solution)/shard_map/ppermute | solution.py:370
  9.7 0.7 collective-permute-start.3
  10.4 1.9 %shard_map.38 = (bf16[1024,1024]{1,0:T(8,128)(2,1)S(1)}, f32[4,256,1024]{2,1,0:T(8,128)S(1)}) custom-call(bf16[16,64,1024]{2,1,0:T(8,128)(2,1)S(1)} %copy-done, f32[16,1024]{1,0:T(8,128)S(1)} %get-tuple-element.16.mask), custom_call_target="tpu_custom_call" | custom-call | flops 3000000000 | bytes 9500000 | tf_op jit(solution)/shard_map/pallas_call | solution.py:308
  12.3 20.5 %collective-permute-done.got_a1 = bf16[17,64,512]{2,1,0:T(8,128)(2,1)S(1)} collective-permute-done((bf16[17,64,512]{2,1,0:T(8,128)(2,1)S(1)}, bf16[17,64,512]{2,1,0:T(8,128)(2,1)S(1)}, u32[]{:S(2)}, u32[]{:S(2)}) %collective-permute-start) | collective-permute-done | bytes 1114144 | tf_op jit(solution)/shard_map/ppermute | solution.py:368
  32.8 0.0 collective-permute-done.2.got_b1
  32.8 1.8 %collective-permute-done.1.got_a2 = bf16[17,64,512]{2,1,0:T(8,128)(2,1)S(1)} collective-permute-done((bf16[17,64,512]{2,1,0:T(8,128)(2,1)S(1)}, bf16[17,64,512]{2,1,0:T(8,128)(2,1)S(1)}, u32[]{:S(2)}, u32[]{:S(2)}) %collective-permute-start.1) | collective-permute-done | bytes 1114144 | tf_op jit(solution)/shard_map/ppermute | solution.py:370
  34.6 0.0 collective-permute-done.3.got_b2
  34.6 0.0 copy-done.1
  34.6 3.4 %shard_map.40 = (bf16[16,64,256]{2,1,0:T(8,128)(2,1)S(1)}, bf16[8,64,256]{2,1,0:T(8,128)(2,1)S(1)}, bf16[8,64,256]{2,1,0:T(8,128)(2,1)S(1)}, bf16[16,64,256]{2,1,0:T(8,128)(2,1)S(1)}, bf16[16,64,256]{2,1,0:T(8,128)(2,1)S(1)}) custom-call(bf16[16,64,1024]{2,1,0:T(8,128)(2,1)S(1)} %copy-done.1, f32[16,1024]{1,0:T(8,128)S(1)} %get-tuple-element.16.mask, ...), custom_call_target="tpu_custom_call" | custom-call | flops 6000000000 | bytes 14000000 | tf_op jit(solution)/shard_map/pallas_call | solution.py:308
  38.0 0.0 copy-start.3
  38.0 36.0 %collective-permute-start.4 = (bf16[8,64,256]{2,1,0:T(8,128)(2,1)S(1)}, bf16[8,64,256]{2,1,0:T(8,128)(2,1)S(1)}, u32[]{:S(2)}, u32[]{:S(2)}) collective-permute-start(bf16[8,64,256]{2,1,0:T(8,128)(2,1)S(1)} %get-tuple-element.23), channel_id=1, source_target_pairs={{0,1},{2,3},{3,0},{4,5},{6,7},{7,4},{8,9},{10,11},{11,8},{12,13},{... | collective-permute-start | bytes 786440 | tf_op jit(solution)/shard_map/ppermute | solution.py:397
  74.0 1.9 %collective-permute-start.5 = (bf16[8,64,256]{2,1,0:T(8,128)(2,1)S(1)}, bf16[8,64,256]{2,1,0:T(8,128)(2,1)S(1)}, u32[]{:S(2)}, u32[]{:S(2)}) collective-permute-start(bf16[8,64,256]{2,1,0:T(8,128)(2,1)S(1)} %get-tuple-element.24), channel_id=1, source_target_pairs={{0,3},{2,1},{3,2},{4,7},{6,5},{7,6},{8,11},{10,9},{11,10},{12,15},... | collective-permute-start | bytes 786440 | tf_op jit(solution)/shard_map/ppermute | solution.py:398
  75.9 2.6 %collective-permute-done.4.got_first = bf16[8,64,256]{2,1,0:T(8,128)(2,1)S(1)} collective-permute-done((bf16[8,64,256]{2,1,0:T(8,128)(2,1)S(1)}, bf16[8,64,256]{2,1,0:T(8,128)(2,1)S(1)}, u32[]{:S(2)}, u32[]{:S(2)}) %collective-permute-start.4) | collective-permute-done | bytes 262176 | tf_op jit(solution)/shard_map/ppermute | solution.py:397
  78.5 6.4 %collective-permute-done.5.got_second = bf16[8,64,256]{2,1,0:T(8,128)(2,1)S(1)} collective-permute-done((bf16[8,64,256]{2,1,0:T(8,128)(2,1)S(1)}, bf16[8,64,256]{2,1,0:T(8,128)(2,1)S(1)}, u32[]{:S(2)}, u32[]{:S(2)}) %collective-permute-start.5) | collective-permute-done | bytes 262176 | tf_op jit(solution)/shard_map/ppermute | solution.py:398
  84.9 0.1 shard_map.41
  85.1 9.9 %collective-permute-start.6 = (bf16[16,64,256]{2,1,0:T(8,128)(2,1)S(1)}, bf16[16,64,256]{2,1,0:T(8,128)(2,1)S(1)}, u32[]{:S(2)}, u32[]{:S(2)}) collective-permute-start(bf16[16,64,256]{2,1,0:T(8,128)(2,1)S(1)} %get-tuple-element.25), channel_id=1, source_target_pairs={{0,1},{1,2},{2,3},{3,0},{4,5},{5,6},{6,7},{7,4},{8,9},{9,10},{10,1... | collective-permute-start | bytes 1572872 | tf_op jit(solution)/shard_map/ppermute | solution.py:411
  95.0 1.9 %collective-permute-start.7 = (bf16[16,64,256]{2,1,0:T(8,128)(2,1)S(1)}, bf16[16,64,256]{2,1,0:T(8,128)(2,1)S(1)}, u32[]{:S(2)}, u32[]{:S(2)}) collective-permute-start(bf16[16,64,256]{2,1,0:T(8,128)(2,1)S(1)} %get-tuple-element.26), channel_id=1, source_target_pairs={{0,3},{1,0},{2,1},{3,2},{4,7},{5,4},{6,5},{7,6},{8,11},{9,8},{10,9... | collective-permute-start | bytes 1572872 | tf_op jit(solution)/shard_map/ppermute | solution.py:412
  96.9 0.0 copy-done.3
  96.9 0.1 copy.4.keep
  97.0 20.5 %collective-permute-done.6.got_first = bf16[16,64,256]{2,1,0:T(8,128)(2,1)S(1)} collective-permute-done((bf16[16,64,256]{2,1,0:T(8,128)(2,1)S(1)}, bf16[16,64,256]{2,1,0:T(8,128)(2,1)S(1)}, u32[]{:S(2)}, u32[]{:S(2)}) %collective-permute-start.6) | collective-permute-done | bytes 524320 | tf_op jit(solution)/shard_map/ppermute | solution.py:411
  117.5 0.0 collective-permute-done.7.got_second
  117.5 1.1 shard_map.42
Async XLA Ops:
  0.0 1.6 %copy-start = (bf16[16,64,1024]{2,1,0:T(8,128)(2,1)S(1)}, bf16[16,64,1024]{2,1,0:T(8,128)(2,1)}, u32[]{:S(2)}) copy-start(bf16[16,64,1024]{2,1,0:T(8,128)(2,1)} %dens.7) | copy-start | bytes 6291460
  1.6 0.7 copy-start.2
  2.7 30.1 %collective-permute-start = (bf16[17,64,512]{2,1,0:T(8,128)(2,1)S(1)}, bf16[17,64,512]{2,1,0:T(8,128)(2,1)S(1)}, u32[]{:S(2)}, u32[]{:S(2)}) collective-permute-start(bf16[17,64,512]{2,1,0:T(8,128)(2,1)S(1)} %shard_map.39), channel_id=1, source_target_pairs={{3,511},{7,3},{4,0},{11,7},{8,4},{15,11},{12,8},{19,15},{16,12},{2... | collective-permute-start | bytes 3342344 | tf_op jit(solution)/shard_map/ppermute | solution.py:368
  4.0 28.8 %collective-permute-start.2 = (bf16[17,64,512]{2,1,0:T(8,128)(2,1)S(1)}, bf16[17,64,512]{2,1,0:T(8,128)(2,1)S(1)}, u32[]{:S(2)}, u32[]{:S(2)}) collective-permute-start(bf16[17,64,512]{2,1,0:T(8,128)(2,1)S(1)} %shard_map.39), channel_id=1, source_target_pairs={{2,511},{6,3},{10,7},{14,11},{18,15},{22,19},{26,23},{30,27},{34,3... | collective-permute-start | bytes 3342344 | tf_op jit(solution)/shard_map/ppermute | solution.py:369
  4.7 29.9 %copy-start.1 = (bf16[16,64,1024]{2,1,0:T(8,128)(2,1)S(1)}, bf16[16,64,1024]{2,1,0:T(8,128)(2,1)}, u32[]{:S(2)}) copy-start(bf16[16,64,1024]{2,1,0:T(8,128)(2,1)} %dens.7) | copy-start | bytes 6291460
  4.7 29.8 %collective-permute-start.1 = (bf16[17,64,512]{2,1,0:T(8,128)(2,1)S(1)}, bf16[17,64,512]{2,1,0:T(8,128)(2,1)S(1)}, u32[]{:S(2)}, u32[]{:S(2)}) collective-permute-start(bf16[17,64,512]{2,1,0:T(8,128)(2,1)S(1)} %get-tuple-element.19), channel_id=1, source_target_pairs={{1,0},{3,2},{0,508},{5,4},{7,6},{9,8},{11,10},{13,12},{15,14},{17,... | collective-permute-start | bytes 3342344 | tf_op jit(solution)/shard_map/ppermute | solution.py:370
  9.7 24.9 %collective-permute-start.3 = (bf16[17,64,512]{2,1,0:T(8,128)(2,1)S(1)}, bf16[17,64,512]{2,1,0:T(8,128)(2,1)S(1)}, u32[]{:S(2)}, u32[]{:S(2)}) collective-permute-start(bf16[17,64,512]{2,1,0:T(8,128)(2,1)S(1)} %get-tuple-element.19), channel_id=1, source_target_pairs={{2,510},{6,2},{10,6},{14,10},{18,14},{22,18},{26,22},{30,26},{34,3... | collective-permute-start | bytes 3342344 | tf_op jit(solution)/shard_map/ppermute | solution.py:371
  38.0 58.9 %copy-start.3 = (s32[16,4]{0,1:T(4,128)S(1)}, s32[16,4]{0,1:T(4,128)}, u32[]{:S(2)}) copy-start(s32[16,4]{0,1:T(4,128)} %param.5) | copy-start | bytes 772
  38.0 40.5 %collective-permute-start.4 = (bf16[8,64,256]{2,1,0:T(8,128)(2,1)S(1)}, bf16[8,64,256]{2,1,0:T(8,128)(2,1)S(1)}, u32[]{:S(2)}, u32[]{:S(2)}) collective-permute-start(bf16[8,64,256]{2,1,0:T(8,128)(2,1)S(1)} %get-tuple-element.23), channel_id=1, source_target_pairs={{0,1},{2,3},{3,0},{4,5},{6,7},{7,4},{8,9},{10,11},{11,8},{12,13},{... | collective-permute-start | bytes 786440 | tf_op jit(solution)/shard_map/ppermute | solution.py:397
  74.0 11.0 %collective-permute-start.5 = (bf16[8,64,256]{2,1,0:T(8,128)(2,1)S(1)}, bf16[8,64,256]{2,1,0:T(8,128)(2,1)S(1)}, u32[]{:S(2)}, u32[]{:S(2)}) collective-permute-start(bf16[8,64,256]{2,1,0:T(8,128)(2,1)S(1)} %get-tuple-element.24), channel_id=1, source_target_pairs={{0,3},{2,1},{3,2},{4,7},{6,5},{7,6},{8,11},{10,9},{11,10},{12,15},... | collective-permute-start | bytes 786440 | tf_op jit(solution)/shard_map/ppermute | solution.py:398
  85.1 32.4 %collective-permute-start.6 = (bf16[16,64,256]{2,1,0:T(8,128)(2,1)S(1)}, bf16[16,64,256]{2,1,0:T(8,128)(2,1)S(1)}, u32[]{:S(2)}, u32[]{:S(2)}) collective-permute-start(bf16[16,64,256]{2,1,0:T(8,128)(2,1)S(1)} %get-tuple-element.25), channel_id=1, source_target_pairs={{0,1},{1,2},{2,3},{3,0},{4,5},{5,6},{6,7},{7,4},{8,9},{9,10},{10,1... | collective-permute-start | bytes 1572872 | tf_op jit(solution)/shard_map/ppermute | solution.py:411
  95.0 22.5 %collective-permute-start.7 = (bf16[16,64,256]{2,1,0:T(8,128)(2,1)S(1)}, bf16[16,64,256]{2,1,0:T(8,128)(2,1)S(1)}, u32[]{:S(2)}, u32[]{:S(2)}) collective-permute-start(bf16[16,64,256]{2,1,0:T(8,128)(2,1)S(1)} %get-tuple-element.26), channel_id=1, source_target_pairs={{0,3},{1,0},{2,1},{3,2},{4,7},{5,4},{6,5},{7,6},{8,11},{9,8},{10,9... | collective-permute-start | bytes 1572872 | tf_op jit(solution)/shard_map/ppermute | solution.py:412

commit v6 on v5

--- a/solution.py
+++ b/solution.py
@@ -34,12 +34,9 @@
     return (x * m[None]).reshape(BS, hi - lo)
 
 
-def group_index():
-    return lax.axis_index("row") * lax.axis_size("col") + lax.axis_index("col")
-
-
 def late_half(groups_half):
-    return group_index() >= groups_half
+    group = lax.axis_index("row") * lax.axis_size("col") + lax.axis_index("col")
+    return group >= groups_half
 
 
 def upper_width(i):
@@ -72,37 +69,41 @@
         put(9 + i, jnp.concatenate([left, right], axis=1))
 
 
-def pack(groups_half, dens, mask, send, lower_if_late):
-    late = late_half(groups_half)
-    send_lower = (lax.axis_index("depth") == 2) & (late == lower_if_late)
+def put_lower(own, put):
+    for i in range(1, ROWS):
+        width = lower_width(i)
+        part = own(i, WIDE - width, WIDE)
+        for n, lane, first, lanes in lower_place(i):
+            put(n, lane, part[:, first : first + lanes])
+
+
+def pack_kernel(dens, pat, upper, diag, mask):
+    mask[...] = expand(pat[...], WIDE)
 
     def own(i, lo, hi):
         return masked_lanes(dens, mask, i, lo, hi)
 
     def put(n, part):
-        send[n] = part
-
-    @pl.when(jnp.logical_not(send_lower))
-    def _():
-        put_upper(own, put)
-
-    @pl.when(send_lower)
-    def _():
-        for i in range(1, ROWS):
-            width = lower_width(i)
-            part = own(i, WIDE - width, WIDE)
-            for n, lane, first, lanes in lower_place(i):
-                send[n, :, lane : lane + lanes] = part[:, first : first + lanes]
-        send[16] = jnp.zeros((BS, HALF), jnp.bfloat16)
-
-
-def pack_kernel(groups_half, dens, pat, send, mask):
-    mask[...] = expand(pat[...], WIDE)
-    pack(groups_half, dens, mask, send, True)
-
-
-def pack_first_kernel(groups_half, dens, mask, send):
-    pack(groups_half, dens, mask, send, False)
+        upper[n] = part
+
+    put_upper(own, put)
+    for a in range(ROWS // 2):
+        pair = [own(2 * a + e, 0, 2 * BS)[:, :BS] for e in range(2)]
+        diag[a] = jnp.concatenate(pair, axis=1)
+
+
+def pack_first_kernel(dens, mask, upper, lower):
+    def own(i, lo, hi):
+        return masked_lanes(dens, mask, i, lo, hi)
+
+    def put(n, part):
+        upper[n] = part
+
+    def put_at(n, lane, part):
+        lower[n, :, lane : lane + part.shape[1]] = part
+
+    put_upper(own, put)
+    put_lower(own, put_at)
 
 
 def own_parts(dens, mask):
@@ -115,28 +116,21 @@
     return lower, upper
 
 
-def chosen(pick, first, second):
-    def get(n, lo, hi):
-        return jnp.where(pick, first[n, :, lo:hi], second[n, :, lo:hi])
-
-    return get
-
-
 def sent_upper(buf):
     def get(i):
         if i == 0:
-            return jnp.concatenate([buf(0, 0, HALF), buf(1, 0, HALF)], axis=1)
+            return jnp.concatenate([buf[0], buf[1]], axis=1)
         if i < 8:
             rest = HALF - 128 * (i // 2)
-            return jnp.concatenate([buf(1 + i, 0, HALF), buf(9 + i, 0, rest)], axis=1)
-        return buf(9 + ROWS - i if i > 8 else 9, 0, HALF)
+            return jnp.concatenate([buf[1 + i], buf[9 + i, :, :rest]], axis=1)
+        return buf[9 + ROWS - i if i > 8 else 9]
 
     return get
 
 
 def sent_lower(buf):
     def get(i):
-        pieces = [buf(n, lane, lane + lanes) for n, lane, _, lanes in lower_place(i)]
+        pieces = [buf[n, :, lane : lane + lanes] for n, lane, _, lanes in lower_place(i)]
         return pieces[0] if len(pieces) == 1 else jnp.concatenate(pieces, axis=1)
 
     return get
@@ -169,21 +163,34 @@
             dst[rows, :] = both
 
 
-def mirror(dst, base):
+def put_diagonal(dst, base, diag):
+    lane = lax.broadcasted_iota(jnp.int32, (BS, 2 * BS), 1)
+    for i in range(ROWS):
+        a = i // 2
+        at = (slice(base + i * BS, base + (i + 1) * BS), slice(2 * BS * a, 2 * BS * (a + 1)))
+        mine = lane >= BS if i % 2 else lane < BS
+        dst[at] = jnp.where(mine, diag[a], dst[at])
+
+
+def mirror(dst, base, from_lower=False):
     r = lax.broadcasted_iota(jnp.int32, (TILE, TILE), 0)
     c = lax.broadcasted_iota(jnp.int32, (TILE, TILE), 1)
     eye = jnp.where(r == c, 1.0, 0.0).astype(jnp.bfloat16)
-    above = lax.shift_right_logical(r, 6) < lax.shift_right_logical(c, 6)
-    strict = jnp.where(above, 1.0, 0.0).astype(jnp.bfloat16)
+    block_r, block_c = lax.shift_right_logical(r, 6), lax.shift_right_logical(c, 6)
+    given = block_r > block_c if from_lower else block_r < block_c
+    strict = jnp.where(given, 1.0, 0.0).astype(jnp.bfloat16)
+
+    def tile_at(n, m):
+        return (slice(base + n * TILE, base + (n + 1) * TILE), slice(m * TILE, (m + 1) * TILE))
+
     for n in range(WIDE // TILE):
-        rows = slice(base + n * TILE, base + (n + 1) * TILE)
-        cols = slice(n * TILE, (n + 1) * TILE)
-        diag = dst[rows, cols]
-        dst[rows, cols] = diag + dot(eye, diag * strict, NT).astype(jnp.bfloat16)
+        diag = dst[tile_at(n, n)]
+        dst[tile_at(n, n)] = diag + dot(eye, diag * strict, NT).astype(jnp.bfloat16)
         for m in range(n + 1, WIDE // TILE):
-            tile = dst[rows, m * TILE : (m + 1) * TILE]
-            turned = dot(eye, tile, NT).astype(jnp.bfloat16)
-            dst[base + m * TILE : base + (m + 1) * TILE, cols] = turned
+            source, target = (tile_at(m, n), tile_at(n, m))
+            if not from_lower:
+                source, target = target, source
+            dst[target] = dot(eye, dst[source], NT).astype(jnp.bfloat16)
 
 
 def prepare_kernel(dens, mask, y, acc):
@@ -210,13 +217,26 @@
 
 
 def main_kernel(
-    groups, dens, mask, y, acc, got_a1, got_a2, got_b1, got_b2, own, first1, second1, first2, second2, z
+    groups_half,
+    dens,
+    mask,
+    y,
+    acc,
+    got_depth,
+    got_y,
+    got_lower,
+    got_diag,
+    own,
+    first1,
+    second1,
+    first_free,
+    second_free,
+    first_due,
+    second_due,
+    z,
 ):
     q = lax.axis_index("depth")
-    late = late_half(groups // 2)
-    group = group_index()
-    turn = (group == groups - 1) | (group == groups // 2 - 1)
-    next_late = late != turn
+    late = late_half(groups_half)
     own_lower, own_upper = own_parts(dens, mask)
 
     def finish(static_q, tile_row, window):
@@ -229,12 +249,16 @@
                 return row[:, p * TILE : (p + 1) * TILE]
 
             own[i] = share(static_q)
-            first2[i] = jnp.where(late, share(static_q - 1), share(static_q + 1))
-            second2[i] = jnp.where(late, share(static_q + 1), share(static_q - 1))
+            first = jnp.where(late, share(static_q - 1), share(static_q + 1))
+            second = jnp.where(late, share(static_q + 1), share(static_q - 1))
             if i < 8:
                 first1[i] = share(static_q + 2)
+                first_due[i] = first
+                second_free[i] = second
             else:
                 second1[i - 8] = share(static_q + 2)
+                first_free[i - 8] = first
+                second_due[i - 8] = second
 
     def products(static_q):
         for t in range(WIDE // TILE):
@@ -253,26 +277,26 @@
 
     @pl.when(q == 0)
     def _():
-        build(z, 0, own_lower, sent_upper(chosen(late, got_a1, got_a2)), True)
-        build(z, WIDE, None, sent_upper(chosen(late, got_a2, got_a1)), True)
+        build(z, 0, own_lower, sent_upper(got_depth), True)
+        build(z, WIDE, None, sent_upper(got_y), True)
         products(0)
 
     @pl.when(q == 1)
     def _():
-        for ref in (own, first1, second1, first2, second2):
+        for ref in (own, first_free, second_free, first_due, second_due):
             ref[...] = jnp.zeros_like(ref)
 
     @pl.when(q == 2)
     def _():
-        build(z, 0, own_lower, sent_upper(chosen(late, got_a1, got_a2)), True)
-        build(z, WIDE, None, sent_upper(chosen(next_late, got_b1, got_b2)), True)
-        mirror(z, WIDE)
+        build(z, 0, own_lower, sent_upper(got_depth), True)
+        build(z, WIDE, sent_lower(got_lower), None)
+        put_diagonal(z, WIDE, got_diag)
+        mirror(z, WIDE, True)
         products(2)
 
     @pl.when(q == 3)
     def _():
-        lower = sent_lower(chosen(next_late, got_b2, got_b1))
-        build(z, WIDE, lower, sent_upper(chosen(next_late, got_a2, got_a1)), True)
+        build(z, WIDE, sent_lower(got_lower), sent_upper(got_y), True)
         products(3)
 
 
@@ -280,17 +304,16 @@
     for i in range(8):
         total = first[i].astype(jnp.float32) + got_first[i].astype(jnp.float32)
         first_out[i] = total.astype(jnp.bfloat16)
-        second_out[i] = second[i]
-        total = second[8 + i].astype(jnp.float32) + got_second[i].astype(jnp.float32)
-        second_out[8 + i] = total.astype(jnp.bfloat16)
-        first_out[8 + i] = first[8 + i]
-
-
-def final_kernel(own, got_first, got_second, keep, out, mask):
+        total = second[i].astype(jnp.float32) + got_second[i].astype(jnp.float32)
+        second_out[i] = total.astype(jnp.bfloat16)
+
+
+def final_kernel(own, first_free, second_free, first_due, second_due, keep, out, mask):
     mask[...] = expand(keep[...], TILE)
     for i in range(ROWS):
-        total = own[i].astype(jnp.float32) + got_first[i].astype(jnp.float32)
-        total = total + got_second[i].astype(jnp.float32)
+        one, other = (first_due, second_free) if i < 8 else (first_free, second_due)
+        total = own[i].astype(jnp.float32) + one[i % 8].astype(jnp.float32)
+        total = total + other[i % 8].astype(jnp.float32)
         out[i] = (total * mask[i : i + 1, :]).astype(jnp.bfloat16)
 
 
@@ -318,14 +341,15 @@
             cost_estimate=pl.CostEstimate(flops=flops, bytes_accessed=moved, transcendentals=0),
         )(*operands)
 
-    packed = (17, BS, HALF)
+    upper_part = (17, BS, HALF)
+    lower_part = (16, BS, HALF)
     share = (ROWS, BS, TILE)
     half_share = (ROWS // 2, BS, TILE)
-
     half = groups // 2
-    send_2, mask = call(
-        functools.partial(pack_kernel, half),
-        (packed, slot_mask),
+
+    upper, diag, mask = call(
+        pack_kernel,
+        (upper_part, (ROWS // 2, BS, 2 * BS), slot_mask),
         [],
         16,
         4_000_000,
@@ -333,13 +357,13 @@
         density,
         pattern,
     )
-    (send_1,) = call(
-        functools.partial(pack_first_kernel, half),
-        (packed,),
+    upper_first, lower = call(
+        pack_first_kernel,
+        (upper_part, lower_part),
         [],
         16,
         4_000_000,
-        3_500_000,
+        4_500_000,
         density,
         mask,
     )
@@ -357,22 +381,25 @@
     def device(g, q):
         return (g % groups) * 4 + q
 
-    routes_a, routes_b = ([], []), ([], [])
+    by_depth, by_y, of_lower, of_diag, first_route, second_route = [], [], [], [], [], []
     for g in range(groups):
-        late = int(g >= half)
-        routes_a[1 - late].extend([(device(g, 1), device(g, 0)), (device(g, 3), device(g, 2))])
-        routes_a[late].append((device(g, 3), device(g - 1, 3)))
-        routes_a[int((g - 1) % groups >= half)].append((device(g, 0), device(g - 1, 0)))
-        routes_b[late].append((device(g, 2), device(g - 1, 3)))
-        routes_b[1 - late].append((device(g, 2), device(g - 1, 2)))
-    got_a1 = lax.ppermute(send_1, AXES, routes_a[0])
-    got_b1 = lax.ppermute(send_1, AXES, routes_b[0])
-    got_a2 = lax.ppermute(send_2, AXES, routes_a[1])
-    got_b2 = lax.ppermute(send_2, AXES, routes_b[1])
-
-    own, first1, second1, first2, second2 = call(
-        functools.partial(main_kernel, groups),
-        (share, half_share, half_share, share, share),
+        by_depth += [(device(g, 1), device(g, 0)), (device(g, 3), device(g, 2))]
+        by_y += [(device(g, 0), device(g - 1, 0)), (device(g, 3), device(g - 1, 3))]
+        of_lower += [(device(g, 1), device(g - 1, 2)), (device(g, 2), device(g - 1, 3))]
+        of_diag.append((device(g, 2), device(g - 1, 2)))
+        for q in range(4):
+            up = (device(g, q), device(g, (q + 1) % 4))
+            down = (device(g, q), device(g, (q - 1) % 4))
+            first_route.append(down if g >= half else up)
+            second_route.append(up if g >= half else down)
+    got_depth = lax.ppermute(upper_first, AXES, by_depth)
+    got_lower = lax.ppermute(lower, AXES, of_lower)
+    got_y = lax.ppermute(upper, AXES, by_y)
+    got_diag = lax.ppermute(diag, AXES, of_diag)
+
+    own, first1, second1, first_free, second_free, first_due, second_due = call(
+        functools.partial(main_kernel, half),
+        (share,) + (half_share,) * 6,
         [pltpu.VMEM((2 * WIDE, WIDE), jnp.bfloat16)],
         20,
         6_000_000_000,
@@ -381,35 +408,30 @@
         mask,
         prepared,
         ahead,
-        got_a1,
-        got_a2,
-        got_b1,
-        got_b2,
-    )
-
-    first_route, second_route = [], []
-    for g in range(groups):
-        for q in range(4):
-            up = (device(g, q), device(g, (q + 1) % 4))
-            down = (device(g, q), device(g, (q - 1) % 4))
-            first_route.append(down if g >= half else up)
-            second_route.append(up if g >= half else down)
+        got_depth,
+        got_y,
+        got_lower,
+        got_diag,
+    )
+
     got_first = lax.ppermute(first1, AXES, [r for r in first_route if r[0] % 4 != 1])
     got_second = lax.ppermute(second1, AXES, [r for r in second_route if r[0] % 4 != 1])
-    first2, second2 = call(
+    first_free = lax.ppermute(first_free, AXES, [r for r in first_route if r[0] % 4 != 1])
+    second_free = lax.ppermute(second_free, AXES, [r for r in second_route if r[0] % 4 != 1])
+    first_due, second_due = call(
         add_kernel,
-        (share,) * 2,
+        (half_share,) * 2,
         [],
         16,
         1_000_000,
         3_000_000,
-        first2,
-        second2,
+        first_due,
+        second_due,
         got_first,
         got_second,
     )
-    got_first = lax.ppermute(first2, AXES, first_route)
-    got_second = lax.ppermute(second2, AXES, second_route)
+    first_due = lax.ppermute(first_due, AXES, first_route)
+    second_due = lax.ppermute(second_due, AXES, second_route)
     (out,) = call(
         final_kernel,
         (share,),
@@ -418,8 +440,10 @@
         1_500_000,
         2_700_000,
         own,
-        got_first,
-        got_second,
+        first_free,
+        second_free,
+        first_due,
+        second_due,
         keep_filter,
     )
     return out

time: 119 us -> 116 us (0.975)
  the two profiles are of different devices: /device:TPU:68 before, /device:TPU:70 now
where the time goes in v6:
time: 116 us
  starting transfers between devices  63.7 us (55%)
  waiting for transfers between devices  42.5 us (37%)
  Pallas kernels  6.92 us (6%)
  local copies, waits for them, and re-layouts  2.38 us (2%)
    ppermute x1, starting transfers between devices, per_device(): lax.ppermute(first1, AXES, [r for r in first_route if r[0] % 4 != 1])  36.7 us
    ppermute x1, waiting for transfers between devices, per_device(): got_depth = lax.ppermute(upper_first, AXES, by_depth)  20.3 us
    ppermute x1, waiting for transfers between devices, per_device(): lax.ppermute(second1, AXES, [r for r in second_route if r[0] % 4 != 1])  11.8 us
    ppermute x1, starting transfers between devices, per_device(): lax.ppermute(first_free, AXES, [r for r in first_route if r[0] % 4 != 1])  8.51 us
    pallas_call x6, Pallas kernels, call(): pl.pallas_call(kernel, out_shape=tuple((jax.ShapeDtypeStruct(shape, jnp.f...  6.92 us
    ppermute x1, waiting for transfers between devices, per_device(): second_due = lax.ppermute(second_due, AXES, second_route)  6 us
    ppermute x1, starting transfers between devices, per_device(): got_y = lax.ppermute(upper, AXES, by_y)  5.08 us
    ppermute x1, starting transfers between devices, per_device(): first_due = lax.ppermute(first_due, AXES, first_route)  4.49 us
  transfers between devices with their start and end apart: 10, of which 5 were waited for; matrix products, arithmetic and copies ran while one was open for 0% of the time, Pallas kernels for 2%

profile of v6, /device:TPU:70, one launch (start us, length us, event | category | flops | bytes accessed | tf_op | source)
XLA Modules:
  0.0 115.7 jit_solution(16989816421844246682)
XLA Ops:
  0.0 1.6 %copy-done = bf16[16,64,1024]{2,1,0:T(8,128)(2,1)S(1)} copy-done((bf16[16,64,1024]{2,1,0:T(8,128)(2,1)S(1)}, bf16[16,64,1024]{2,1,0:T(8,128)(2,1)}, u32[]{:S(2)}) %copy-start) | copy-done | bytes 2097176
  1.6 0.7 copy-done.2
  2.3 0.3 shard_map.37
  2.6 0.3 shard_map.39
  2.9 1.3 %collective-permute-start = (bf16[17,64,512]{2,1,0:T(8,128)(2,1)S(1)}, bf16[17,64,512]{2,1,0:T(8,128)(2,1)S(1)}, u32[]{:S(2)}, u32[]{:S(2)}) collective-permute-start(bf16[17,64,512]{2,1,0:T(8,128)(2,1)S(1)} %get-tuple-element.24), channel_id=1, source_target_pairs={{1,0},{3,2},{5,4},{7,6},{9,8},{11,10},{13,12},{15,14},{17,16},{19,... | collective-permute-start | bytes 3342344 | tf_op jit(solution)/shard_map/ppermute | solution.py:395
  4.2 5.1 %collective-permute-start.1 = (bf16[17,64,512]{2,1,0:T(8,128)(2,1)S(1)}, bf16[17,64,512]{2,1,0:T(8,128)(2,1)S(1)}, u32[]{:S(2)}, u32[]{:S(2)}) collective-permute-start(bf16[17,64,512]{2,1,0:T(8,128)(2,1)S(1)} %get-tuple-element.25), channel_id=1, source_target_pairs={{0,508},{3,511},{4,0},{7,3},{8,4},{11,7},{12,8},{15,11},{16,12},{1... | collective-permute-start | bytes 3342344 | tf_op jit(solution)/shard_map/ppermute | solution.py:397
  9.3 0.7 collective-permute-start.2
  10.0 0.0 copy-start.1
  10.0 0.8 collective-permute-start.3
  10.8 1.9 %shard_map.38 = (bf16[1024,1024]{1,0:T(8,128)(2,1)S(1)}, f32[4,256,1024]{2,1,0:T(8,128)S(1)}) custom-call(bf16[16,64,1024]{2,1,0:T(8,128)(2,1)S(1)} %copy-done, f32[16,1024]{1,0:T(8,128)S(1)} %get-tuple-element.21.mask), custom_call_target="tpu_custom_call" | custom-call | flops 3000000000 | bytes 9500000 | tf_op jit(solution)/shard_map/pallas_call | solution.py:331
  12.7 0.0 collective-permute-done.3.got_diag
  12.7 0.0 collective-permute-done.2.got_lower
  12.7 20.3 %collective-permute-done.got_depth = bf16[17,64,512]{2,1,0:T(8,128)(2,1)S(1)} collective-permute-done((bf16[17,64,512]{2,1,0:T(8,128)(2,1)S(1)}, bf16[17,64,512]{2,1,0:T(8,128)(2,1)S(1)}, u32[]{:S(2)}, u32[]{:S(2)}) %collective-permute-start) | collective-permute-done | bytes 1114144 | tf_op jit(solution)/shard_map/ppermute | solution.py:395
  33.0 0.9 collective-permute-done.1.got_y
  33.9 0.0 copy-done.1
  33.9 3.3 %shard_map.40 = (bf16[16,64,256]{2,1,0:T(8,128)(2,1)S(1)}, bf16[8,64,256]{2,1,0:T(8,128)(2,1)S(1)}, bf16[8,64,256]{2,1,0:T(8,128)(2,1)S(1)}, bf16[8,64,256]{2,1,...) custom-call(bf16[16,64,1024]{2,1,0:T(8,128)(2,1)S(1)} %copy-done.1, ...), custom_call_target="tpu_custom_call" | custom-call | flops 6000000000 | bytes 14000000 | tf_op jit(solution)/shard_map/pallas_call | solution.py:331
  37.2 36.7 %collective-permute-start.6 = (bf16[8,64,256]{2,1,0:T(8,128)(2,1)S(1)}, bf16[8,64,256]{2,1,0:T(8,128)(2,1)S(1)}, u32[]{:S(2)}, u32[]{:S(2)}) collective-permute-start(bf16[8,64,256]{2,1,0:T(8,128)(2,1)S(1)} %get-tuple-element.33), channel_id=1, source_target_pairs={{0,1},{2,3},{3,0},{4,5},{6,7},{7,4},{8,9},{10,11},{11,8},{12,13},{... | collective-permute-start | bytes 786440 | tf_op jit(solution)/shard_map/ppermute | solution.py:417
  74.0 1.9 %collective-permute-start.7 = (bf16[8,64,256]{2,1,0:T(8,128)(2,1)S(1)}, bf16[8,64,256]{2,1,0:T(8,128)(2,1)S(1)}, u32[]{:S(2)}, u32[]{:S(2)}) collective-permute-start(bf16[8,64,256]{2,1,0:T(8,128)(2,1)S(1)} %get-tuple-element.34), channel_id=1, source_target_pairs={{0,3},{2,1},{3,2},{4,7},{6,5},{7,6},{8,11},{10,9},{11,10},{12,15},... | collective-permute-start | bytes 786440 | tf_op jit(solution)/shard_map/ppermute | solution.py:418
  75.9 8.5 %collective-permute-start.4 = (bf16[8,64,256]{2,1,0:T(8,128)(2,1)S(1)}, bf16[8,64,256]{2,1,0:T(8,128)(2,1)S(1)}, u32[]{:S(2)}, u32[]{:S(2)}) collective-permute-start(bf16[8,64,256]{2,1,0:T(8,128)(2,1)S(1)} %get-tuple-element.29), channel_id=1, source_target_pairs={{0,1},{2,3},{3,0},{4,5},{6,7},{7,4},{8,9},{10,11},{11,8},{12,13},{... | collective-permute-start | bytes 786440 | tf_op jit(solution)/shard_map/ppermute | solution.py:419
  84.4 1.9 %collective-permute-start.5 = (bf16[8,64,256]{2,1,0:T(8,128)(2,1)S(1)}, bf16[8,64,256]{2,1,0:T(8,128)(2,1)S(1)}, u32[]{:S(2)}, u32[]{:S(2)}) collective-permute-start(bf16[8,64,256]{2,1,0:T(8,128)(2,1)S(1)} %get-tuple-element.30), channel_id=1, source_target_pairs={{0,3},{2,1},{3,2},{4,7},{6,5},{7,6},{8,11},{10,9},{11,10},{12,15},... | collective-permute-start | bytes 786440 | tf_op jit(solution)/shard_map/ppermute | solution.py:420
  86.4 0.0 collective-permute-done.6.got_first
  86.4 11.8 %collective-permute-done.7.got_second = bf16[8,64,256]{2,1,0:T(8,128)(2,1)S(1)} collective-permute-done((bf16[8,64,256]{2,1,0:T(8,128)(2,1)S(1)}, bf16[8,64,256]{2,1,0:T(8,128)(2,1)S(1)}, u32[]{:S(2)}, u32[]{:S(2)}) %collective-permute-start.7) | collective-permute-done | bytes 262176 | tf_op jit(solution)/shard_map/ppermute | solution.py:418
  98.1 0.1 shard_map.41
  98.3 4.5 %collective-permute-start.8 = (bf16[8,64,256]{2,1,0:T(8,128)(2,1)S(1)}, bf16[8,64,256]{2,1,0:T(8,128)(2,1)S(1)}, u32[]{:S(2)}, u32[]{:S(2)}) collective-permute-start(bf16[8,64,256]{2,1,0:T(8,128)(2,1)S(1)} %get-tuple-element.35), channel_id=1, source_target_pairs={{0,1},{1,2},{2,3},{3,0},{4,5},{5,6},{6,7},{7,4},{8,9},{9,10},{10,1... | collective-permute-start | bytes 786440 | tf_op jit(solution)/shard_map/ppermute | solution.py:433
  102.8 2.3 %collective-permute-start.9 = (bf16[8,64,256]{2,1,0:T(8,128)(2,1)S(1)}, bf16[8,64,256]{2,1,0:T(8,128)(2,1)S(1)}, u32[]{:S(2)}, u32[]{:S(2)}) collective-permute-start(bf16[8,64,256]{2,1,0:T(8,128)(2,1)S(1)} %get-tuple-element.36), channel_id=1, source_target_pairs={{0,3},{1,0},{2,1},{3,2},{4,7},{5,4},{6,5},{7,6},{8,11},{9,8},{10,9... | collective-permute-start | bytes 786440 | tf_op jit(solution)/shard_map/ppermute | solution.py:434
  105.0 0.0 copy-done.3
  105.0 0.1 copy.4.keep
  105.1 0.0 collective-permute-done.4.first_free
  105.1 0.0 collective-permute-done.5.second_free
  105.1 3.5 %collective-permute-done.8.first_due = bf16[8,64,256]{2,1,0:T(8,128)(2,1)S(1)} collective-permute-done((bf16[8,64,256]{2,1,0:T(8,128)(2,1)S(1)}, bf16[8,64,256]{2,1,0:T(8,128)(2,1)S(1)}, u32[]{:S(2)}, u32[]{:S(2)}) %collective-permute-start.8) | collective-permute-done | bytes 262176 | tf_op jit(solution)/shard_map/ppermute | solution.py:433
  108.6 6.0 %collective-permute-done.9.second_due = bf16[8,64,256]{2,1,0:T(8,128)(2,1)S(1)} collective-permute-done((bf16[8,64,256]{2,1,0:T(8,128)(2,1)S(1)}, bf16[8,64,256]{2,1,0:T(8,128)(2,1)S(1)}, u32[]{:S(2)}, u32[]{:S(2)}) %collective-permute-start.9) | collective-permute-done | bytes 262176 | tf_op jit(solution)/shard_map/ppermute | solution.py:434
  114.6 1.1 shard_map.42
  (3 shorter events, 0.0 us)
Async XLA Ops:
  0.0 1.6 %copy-start = (bf16[16,64,1024]{2,1,0:T(8,128)(2,1)S(1)}, bf16[16,64,1024]{2,1,0:T(8,128)(2,1)}, u32[]{:S(2)}) copy-start(bf16[16,64,1024]{2,1,0:T(8,128)(2,1)} %dens.7) | copy-start | bytes 6291460
  1.6 0.7 copy-start.2
  2.9 30.1 %collective-permute-start = (bf16[17,64,512]{2,1,0:T(8,128)(2,1)S(1)}, bf16[17,64,512]{2,1,0:T(8,128)(2,1)S(1)}, u32[]{:S(2)}, u32[]{:S(2)}) collective-permute-start(bf16[17,64,512]{2,1,0:T(8,128)(2,1)S(1)} %get-tuple-element.24), channel_id=1, source_target_pairs={{1,0},{3,2},{5,4},{7,6},{9,8},{11,10},{13,12},{15,14},{17,16},{19,... | collective-permute-start | bytes 3342344 | tf_op jit(solution)/shard_map/ppermute | solution.py:395
  4.2 29.7 %collective-permute-start.1 = (bf16[17,64,512]{2,1,0:T(8,128)(2,1)S(1)}, bf16[17,64,512]{2,1,0:T(8,128)(2,1)S(1)}, u32[]{:S(2)}, u32[]{:S(2)}) collective-permute-start(bf16[17,64,512]{2,1,0:T(8,128)(2,1)S(1)} %get-tuple-element.25), channel_id=1, source_target_pairs={{0,508},{3,511},{4,0},{7,3},{8,4},{11,7},{12,8},{15,11},{16,12},{1... | collective-permute-start | bytes 3342344 | tf_op jit(solution)/shard_map/ppermute | solution.py:397
  9.3 3.4 %collective-permute-start.2 = (bf16[16,64,512]{2,1,0:T(8,128)(2,1)S(1)}, bf16[16,64,512]{2,1,0:T(8,128)(2,1)S(1)}, u32[]{:S(2)}, u32[]{:S(2)}) collective-permute-start(bf16[16,64,512]{2,1,0:T(8,128)(2,1)S(1)} %get-tuple-element.26), channel_id=1, source_target_pairs={{1,510},{2,511},{5,2},{6,3},{9,6},{10,7},{13,10},{14,11},{17,14},{... | collective-permute-start | bytes 3145736 | tf_op jit(solution)/shard_map/ppermute | solution.py:396
  10.0 23.9 %copy-start.1 = (bf16[16,64,1024]{2,1,0:T(8,128)(2,1)S(1)}, bf16[16,64,1024]{2,1,0:T(8,128)(2,1)}, u32[]{:S(2)}) copy-start(bf16[16,64,1024]{2,1,0:T(8,128)(2,1)} %dens.7) | copy-start | bytes 6291460
  10.0 2.7 %collective-permute-start.3 = (bf16[8,64,128]{2,1,0:T(8,128)(2,1)S(1)}, bf16[8,64,128]{2,1,0:T(8,128)(2,1)S(1)}, u32[]{:S(2)}, u32[]{:S(2)}) collective-permute-start(bf16[8,64,128]{2,1,0:T(8,128)(2,1)S(1)} %get-tuple-element.27), channel_id=1, source_target_pairs={{2,510},{6,2},{10,6},{14,10},{18,14},{22,18},{26,22},{30,26},{34,3... | collective-permute-start | bytes 393224 | tf_op jit(solution)/shard_map/ppermute | solution.py:398
  33.9 71.1 %copy-start.3 = (s32[16,4]{0,1:T(4,128)S(1)}, s32[16,4]{0,1:T(4,128)}, u32[]{:S(2)}) copy-start(s32[16,4]{0,1:T(4,128)} %param.5) | copy-start | bytes 772
  37.2 49.1 %collective-permute-start.6 = (bf16[8,64,256]{2,1,0:T(8,128)(2,1)S(1)}, bf16[8,64,256]{2,1,0:T(8,128)(2,1)S(1)}, u32[]{:S(2)}, u32[]{:S(2)}) collective-permute-start(bf16[8,64,256]{2,1,0:T(8,128)(2,1)S(1)} %get-tuple-element.33), channel_id=1, source_target_pairs={{0,1},{2,3},{3,0},{4,5},{6,7},{7,4},{8,9},{10,11},{11,8},{12,13},{... | collective-permute-start | bytes 786440 | tf_op jit(solution)/shard_map/ppermute | solution.py:417
  74.0 24.2 %collective-permute-start.7 = (bf16[8,64,256]{2,1,0:T(8,128)(2,1)S(1)}, bf16[8,64,256]{2,1,0:T(8,128)(2,1)S(1)}, u32[]{:S(2)}, u32[]{:S(2)}) collective-permute-start(bf16[8,64,256]{2,1,0:T(8,128)(2,1)S(1)} %get-tuple-element.34), channel_id=1, source_target_pairs={{0,3},{2,1},{3,2},{4,7},{6,5},{7,6},{8,11},{10,9},{11,10},{12,15},... | collective-permute-start | bytes 786440 | tf_op jit(solution)/shard_map/ppermute | solution.py:418
  75.9 29.2 %collective-permute-start.4 = (bf16[8,64,256]{2,1,0:T(8,128)(2,1)S(1)}, bf16[8,64,256]{2,1,0:T(8,128)(2,1)S(1)}, u32[]{:S(2)}, u32[]{:S(2)}) collective-permute-start(bf16[8,64,256]{2,1,0:T(8,128)(2,1)S(1)} %get-tuple-element.29), channel_id=1, source_target_pairs={{0,1},{2,3},{3,0},{4,5},{6,7},{7,4},{8,9},{10,11},{11,8},{12,13},{... | collective-permute-start | bytes 786440 | tf_op jit(solution)/shard_map/ppermute | solution.py:419
  84.4 20.7 %collective-permute-start.5 = (bf16[8,64,256]{2,1,0:T(8,128)(2,1)S(1)}, bf16[8,64,256]{2,1,0:T(8,128)(2,1)S(1)}, u32[]{:S(2)}, u32[]{:S(2)}) collective-permute-start(bf16[8,64,256]{2,1,0:T(8,128)(2,1)S(1)} %get-tuple-element.30), channel_id=1, source_target_pairs={{0,3},{2,1},{3,2},{4,7},{6,5},{7,6},{8,11},{10,9},{11,10},{12,15},... | collective-permute-start | bytes 786440 | tf_op jit(solution)/shard_map/ppermute | solution.py:420
  98.3 10.4 %collective-permute-start.8 = (bf16[8,64,256]{2,1,0:T(8,128)(2,1)S(1)}, bf16[8,64,256]{2,1,0:T(8,128)(2,1)S(1)}, u32[]{:S(2)}, u32[]{:S(2)}) collective-permute-start(bf16[8,64,256]{2,1,0:T(8,128)(2,1)S(1)} %get-tuple-element.35), channel_id=1, source_target_pairs={{0,1},{1,2},{2,3},{3,0},{4,5},{5,6},{6,7},{7,4},{8,9},{9,10},{10,1... | collective-permute-start | bytes 786440 | tf_op jit(solution)/shard_map/ppermute | solution.py:433
  102.8 11.9 %collective-permute-start.9 = (bf16[8,64,256]{2,1,0:T(8,128)(2,1)S(1)}, bf16[8,64,256]{2,1,0:T(8,128)(2,1)S(1)}, u32[]{:S(2)}, u32[]{:S(2)}) collective-permute-start(bf16[8,64,256]{2,1,0:T(8,128)(2,1)S(1)} %get-tuple-element.36), channel_id=1, source_target_pairs={{0,3},{1,0},{2,1},{3,2},{4,7},{5,4},{6,5},{7,6},{8,11},{9,8},{10,9... | collective-permute-start | bytes 786440 | tf_op jit(solution)/shard_map/ppermute | solution.py:434

commit v7 on v6

--- a/solution.py
+++ b/solution.py
@@ -69,41 +69,39 @@
         put(9 + i, jnp.concatenate([left, right], axis=1))
 
 
-def put_lower(own, put):
-    for i in range(1, ROWS):
-        width = lower_width(i)
-        part = own(i, WIDE - width, WIDE)
-        for n, lane, first, lanes in lower_place(i):
-            put(n, lane, part[:, first : first + lanes])
-
-
-def pack_kernel(dens, pat, upper, diag, mask):
-    mask[...] = expand(pat[...], WIDE)
+def pack(dens, mask, send, lower_at):
+    q = lax.axis_index("depth")
 
     def own(i, lo, hi):
         return masked_lanes(dens, mask, i, lo, hi)
 
     def put(n, part):
-        upper[n] = part
-
-    put_upper(own, put)
+        send[n] = part
+
+    @pl.when(q != lower_at)
+    def _():
+        put_upper(own, put)
+
+    @pl.when(q == lower_at)
+    def _():
+        for i in range(1, ROWS):
+            width = lower_width(i)
+            part = own(i, WIDE - width, WIDE)
+            for n, lane, first, lanes in lower_place(i):
+                send[n, :, lane : lane + lanes] = part[:, first : first + lanes]
+        send[16] = jnp.zeros((BS, HALF), jnp.bfloat16)
+
+
+def pack_kernel(dens, pat, send, diag, mask):
+    mask[...] = expand(pat[...], WIDE)
+    pack(dens, mask, send, 1)
     for a in range(ROWS // 2):
-        pair = [own(2 * a + e, 0, 2 * BS)[:, :BS] for e in range(2)]
+        pair = [masked_lanes(dens, mask, 2 * a + e, 0, 2 * BS)[:, :BS] for e in range(2)]
         diag[a] = jnp.concatenate(pair, axis=1)
 
 
-def pack_first_kernel(dens, mask, upper, lower):
-    def own(i, lo, hi):
-        return masked_lanes(dens, mask, i, lo, hi)
-
-    def put(n, part):
-        upper[n] = part
-
-    def put_at(n, lane, part):
-        lower[n, :, lane : lane + part.shape[1]] = part
-
-    put_upper(own, put)
-    put_lower(own, put_at)
+def pack_first_kernel(dens, mask, send):
+    pack(dens, mask, send, 2)
 
 
 def own_parts(dens, mask):
@@ -222,9 +220,8 @@
     mask,
     y,
     acc,
-    got_depth,
-    got_y,
-    got_lower,
+    got_a,
+    got_b,
     got_diag,
     own,
     first1,
@@ -277,8 +274,8 @@
 
     @pl.when(q == 0)
     def _():
-        build(z, 0, own_lower, sent_upper(got_depth), True)
-        build(z, WIDE, None, sent_upper(got_y), True)
+        build(z, 0, own_lower, sent_upper(got_a), True)
+        build(z, WIDE, None, sent_upper(got_b), True)
         products(0)
 
     @pl.when(q == 1)
@@ -288,15 +285,15 @@
 
     @pl.when(q == 2)
     def _():
-        build(z, 0, own_lower, sent_upper(got_depth), True)
-        build(z, WIDE, sent_lower(got_lower), None)
+        build(z, 0, own_lower, sent_upper(got_a), True)
+        build(z, WIDE, sent_lower(got_b), None)
         put_diagonal(z, WIDE, got_diag)
         mirror(z, WIDE, True)
         products(2)
 
     @pl.when(q == 3)
     def _():
-        build(z, WIDE, sent_lower(got_lower), sent_upper(got_y), True)
+        build(z, WIDE, sent_lower(got_a), sent_upper(got_b), True)
         products(3)
 
 
@@ -341,15 +338,14 @@
             cost_estimate=pl.CostEstimate(flops=flops, bytes_accessed=moved, transcendentals=0),
         )(*operands)
 
-    upper_part = (17, BS, HALF)
-    lower_part = (16, BS, HALF)
+    packed = (17, BS, HALF)
     share = (ROWS, BS, TILE)
     half_share = (ROWS // 2, BS, TILE)
     half = groups // 2
 
-    upper, diag, mask = call(
+    send_b, diag, mask = call(
         pack_kernel,
-        (upper_part, (ROWS // 2, BS, 2 * BS), slot_mask),
+        (packed, (ROWS // 2, BS, 2 * BS), slot_mask),
         [],
         16,
         4_000_000,
@@ -357,9 +353,9 @@
         density,
         pattern,
     )
-    upper_first, lower = call(
+    (send_a,) = call(
         pack_first_kernel,
-        (upper_part, lower_part),
+        (packed,),
         [],
         16,
         4_000_000,
@@ -381,21 +377,21 @@
     def device(g, q):
         return (g % groups) * 4 + q
 
-    by_depth, by_y, of_lower, of_diag, first_route, second_route = [], [], [], [], [], []
+    route_a, route_b, route_diag, first_route, second_route = [], [], [], [], []
     for g in range(groups):
-        by_depth += [(device(g, 1), device(g, 0)), (device(g, 3), device(g, 2))]
-        by_y += [(device(g, 0), device(g - 1, 0)), (device(g, 3), device(g - 1, 3))]
-        of_lower += [(device(g, 1), device(g - 1, 2)), (device(g, 2), device(g - 1, 3))]
-        of_diag.append((device(g, 2), device(g - 1, 2)))
+        route_a += [(device(g, 1), device(g, 0)), (device(g, 3), device(g, 2))]
+        route_a.append((device(g, 2), device(g - 1, 3)))
+        route_b += [(device(g, 0), device(g - 1, 0)), (device(g, 3), device(g - 1, 3))]
+        route_b.append((device(g, 1), device(g - 1, 2)))
+        route_diag.append((device(g, 2), device(g - 1, 2)))
         for q in range(4):
             up = (device(g, q), device(g, (q + 1) % 4))
             down = (device(g, q), device(g, (q - 1) % 4))
             first_route.append(down if g >= half else up)
             second_route.append(up if g >= half else down)
-    got_depth = lax.ppermute(upper_first, AXES, by_depth)
-    got_lower = lax.ppermute(lower, AXES, of_lower)
-    got_y = lax.ppermute(upper, AXES, by_y)
-    got_diag = lax.ppermute(diag, AXES, of_diag)
+    got_a = lax.ppermute(send_a, AXES, route_a)
+    got_b = lax.ppermute(send_b, AXES, route_b)
+    got_diag = lax.ppermute(diag, AXES, route_diag)
 
     own, first1, second1, first_free, second_free, first_due, second_due = call(
         functools.partial(main_kernel, half),
@@ -408,9 +404,8 @@
         mask,
         prepared,
         ahead,
-        got_depth,
-        got_y,
-        got_lower,
+        got_a,
+        got_b,
         got_diag,
     )
 

time: 116 us -> 116 us (level)
  the two profiles are of different devices: /device:TPU:70 before, /device:TPU:61 now
where the time goes in v7:
time: 116 us; the launch traced here: 115 us
  waiting for transfers between devices  57.1 us (49%)
  starting transfers between devices  48.9 us (42%)
  Pallas kernels  6.83 us (6%)
  local copies, waits for them, and re-layouts  2.38 us (2%)
    ppermute x1, waiting for transfers between devices, per_device(): got_a = lax.ppermute(send_a, AXES, route_a)  46.3 us
    ppermute x1, starting transfers between devices, per_device(): first_due = lax.ppermute(first_due, AXES, first_route)  14.9 us
    ppermute x1, starting transfers between devices, per_device(): lax.ppermute(second1, AXES, [r for r in second_route if r[0] % 4 != 1])  11.8 us
    ppermute x1, starting transfers between devices, per_device(): lax.ppermute(second_free, AXES, [r for r in second_route if r[0] % 4 != 1])  11.3 us
    pallas_call x6, Pallas kernels, call(): pl.pallas_call(kernel, out_shape=tuple((jax.ShapeDtypeStruct(shape, jnp.f...  6.83 us
    ppermute x1, waiting for transfers between devices, per_device(): second_due = lax.ppermute(second_due, AXES, second_route)  5.84 us
    ppermute x1, waiting for transfers between devices, per_device(): first_due = lax.ppermute(first_due, AXES, first_route)  4.88 us
    ppermute x1, starting transfers between devices, per_device(): got_b = lax.ppermute(send_b, AXES, route_b)  2.98 us
  transfers between devices with their start and end apart: 9, of which 3 were waited for; matrix products, arithmetic and copies ran while one was open for 0% of the time, Pallas kernels for 2%

profile of v7, /device:TPU:61, one launch (start us, length us, event | category | flops | bytes accessed | tf_op | source)
XLA Modules:
  0.0 115.3 jit_solution(1567839171890846599)
XLA Ops:
  0.0 0.0 copy-start
  0.0 1.6 %copy-done = bf16[16,64,1024]{2,1,0:T(8,128)(2,1)S(1)} copy-done((bf16[16,64,1024]{2,1,0:T(8,128)(2,1)S(1)}, bf16[16,64,1024]{2,1,0:T(8,128)(2,1)}, u32[]{:S(2)}) %copy-start) | copy-done | bytes 2097176
  1.6 0.0 copy-start.2
  1.6 0.7 copy-done.2
  2.3 0.4 shard_map.37
  2.6 0.1 shard_map.39
  2.8 1.3 %collective-permute-start = (bf16[17,64,512]{2,1,0:T(8,128)(2,1)S(1)}, bf16[17,64,512]{2,1,0:T(8,128)(2,1)S(1)}, u32[]{:S(2)}, u32[]{:S(2)}) collective-permute-start(bf16[17,64,512]{2,1,0:T(8,128)(2,1)S(1)} %shard_map.39), channel_id=1, source_target_pairs={{1,0},{3,2},{2,511},{5,4},{7,6},{6,3},{9,8},{11,10},{10,7},{13,12}... | collective-permute-start | bytes 3342344 | tf_op jit(solution)/shard_map/ppermute | solution.py:392
  4.1 3.0 %collective-permute-start.1 = (bf16[17,64,512]{2,1,0:T(8,128)(2,1)S(1)}, bf16[17,64,512]{2,1,0:T(8,128)(2,1)S(1)}, u32[]{:S(2)}, u32[]{:S(2)}) collective-permute-start(bf16[17,64,512]{2,1,0:T(8,128)(2,1)S(1)} %get-tuple-element.22), channel_id=1, source_target_pairs={{0,508},{3,511},{1,510},{4,0},{7,3},{5,2},{8,4},{11,7},{9,6},{12,8... | collective-permute-start | bytes 3342344 | tf_op jit(solution)/shard_map/ppermute | solution.py:393
  7.1 0.0 copy-start.1
  7.1 0.8 collective-permute-start.2
  7.9 1.9 %shard_map.38 = (bf16[1024,1024]{1,0:T(8,128)(2,1)S(1)}, f32[4,256,1024]{2,1,0:T(8,128)S(1)}) custom-call(bf16[16,64,1024]{2,1,0:T(8,128)(2,1)S(1)} %copy-done, f32[16,1024]{1,0:T(8,128)S(1)} %get-tuple-element.19.mask), custom_call_target="tpu_custom_call" | custom-call | flops 3000000000 | bytes 9500000 | tf_op jit(solution)/shard_map/pallas_call | solution.py:328
  9.8 0.0 collective-permute-done.2.got_diag
  9.8 46.3 %collective-permute-done.got_a = bf16[17,64,512]{2,1,0:T(8,128)(2,1)S(1)} collective-permute-done((bf16[17,64,512]{2,1,0:T(8,128)(2,1)S(1)}, bf16[17,64,512]{2,1,0:T(8,128)(2,1)S(1)}, u32[]{:S(2)}, u32[]{:S(2)}) %collective-permute-start) | collective-permute-done | bytes 1114144 | tf_op jit(solution)/shard_map/ppermute | solution.py:392
  56.1 0.0 collective-permute-done.1.got_b
  56.1 0.0 copy-done.1
  56.1 3.3 %shard_map.40 = (bf16[16,64,256]{2,1,0:T(8,128)(2,1)S(1)}, bf16[8,64,256]{2,1,0:T(8,128)(2,1)S(1)}, bf16[8,64,256]{2,1,0:T(8,128)(2,1)S(1)}, bf16[8,64,256]{2,1,...) custom-call(bf16[16,64,1024]{2,1,0:T(8,128)(2,1)S(1)} %copy-done.1, ...), custom_call_target="tpu_custom_call" | custom-call | flops 6000000000 | bytes 14000000 | tf_op jit(solution)/shard_map/pallas_call | solution.py:328
  59.4 1.9 %collective-permute-start.5 = (bf16[8,64,256]{2,1,0:T(8,128)(2,1)S(1)}, bf16[8,64,256]{2,1,0:T(8,128)(2,1)S(1)}, u32[]{:S(2)}, u32[]{:S(2)}) collective-permute-start(bf16[8,64,256]{2,1,0:T(8,128)(2,1)S(1)} %get-tuple-element.29), channel_id=1, source_target_pairs={{0,1},{2,3},{3,0},{4,5},{6,7},{7,4},{8,9},{10,11},{11,8},{12,13},{... | collective-permute-start | bytes 786440 | tf_op jit(solution)/shard_map/ppermute | solution.py:412
  61.4 11.8 %collective-permute-start.6 = (bf16[8,64,256]{2,1,0:T(8,128)(2,1)S(1)}, bf16[8,64,256]{2,1,0:T(8,128)(2,1)S(1)}, u32[]{:S(2)}, u32[]{:S(2)}) collective-permute-start(bf16[8,64,256]{2,1,0:T(8,128)(2,1)S(1)} %get-tuple-element.30), channel_id=1, source_target_pairs={{0,3},{2,1},{3,2},{4,7},{6,5},{7,6},{8,11},{10,9},{11,10},{12,15},... | collective-permute-start | bytes 786440 | tf_op jit(solution)/shard_map/ppermute | solution.py:413
  73.2 1.9 %collective-permute-start.3 = (bf16[8,64,256]{2,1,0:T(8,128)(2,1)S(1)}, bf16[8,64,256]{2,1,0:T(8,128)(2,1)S(1)}, u32[]{:S(2)}, u32[]{:S(2)}) collective-permute-start(bf16[8,64,256]{2,1,0:T(8,128)(2,1)S(1)} %get-tuple-element.25), channel_id=1, source_target_pairs={{0,1},{2,3},{3,0},{4,5},{6,7},{7,4},{8,9},{10,11},{11,8},{12,13},{... | collective-permute-start | bytes 786440 | tf_op jit(solution)/shard_map/ppermute | solution.py:414
  75.1 11.3 %collective-permute-start.4 = (bf16[8,64,256]{2,1,0:T(8,128)(2,1)S(1)}, bf16[8,64,256]{2,1,0:T(8,128)(2,1)S(1)}, u32[]{:S(2)}, u32[]{:S(2)}) collective-permute-start(bf16[8,64,256]{2,1,0:T(8,128)(2,1)S(1)} %get-tuple-element.26), channel_id=1, source_target_pairs={{0,3},{2,1},{3,2},{4,7},{6,5},{7,6},{8,11},{10,9},{11,10},{12,15},... | collective-permute-start | bytes 786440 | tf_op jit(solution)/shard_map/ppermute | solution.py:415
  86.5 0.0 collective-permute-done.5.got_first
  86.5 0.0 collective-permute-done.6.got_second
  86.5 0.1 shard_map.41
  86.6 14.9 %collective-permute-start.7 = (bf16[8,64,256]{2,1,0:T(8,128)(2,1)S(1)}, bf16[8,64,256]{2,1,0:T(8,128)(2,1)S(1)}, u32[]{:S(2)}, u32[]{:S(2)}) collective-permute-start(bf16[8,64,256]{2,1,0:T(8,128)(2,1)S(1)} %get-tuple-element.31), channel_id=1, source_target_pairs={{0,1},{1,2},{2,3},{3,0},{4,5},{5,6},{6,7},{7,4},{8,9},{9,10},{10,1... | collective-permute-start | bytes 786440 | tf_op jit(solution)/shard_map/ppermute | solution.py:428
  101.5 1.9 %collective-permute-start.8 = (bf16[8,64,256]{2,1,0:T(8,128)(2,1)S(1)}, bf16[8,64,256]{2,1,0:T(8,128)(2,1)S(1)}, u32[]{:S(2)}, u32[]{:S(2)}) collective-permute-start(bf16[8,64,256]{2,1,0:T(8,128)(2,1)S(1)} %get-tuple-element.32), channel_id=1, source_target_pairs={{0,3},{1,0},{2,1},{3,2},{4,7},{5,4},{6,5},{7,6},{8,11},{9,8},{10,9... | collective-permute-start | bytes 786440 | tf_op jit(solution)/shard_map/ppermute | solution.py:429
  103.4 0.0 copy-done.3
  103.4 0.1 copy.4.keep
  103.5 0.0 collective-permute-done.3.first_free
  103.5 0.0 collective-permute-done.4.second_free
  103.5 4.9 %collective-permute-done.7.first_due = bf16[8,64,256]{2,1,0:T(8,128)(2,1)S(1)} collective-permute-done((bf16[8,64,256]{2,1,0:T(8,128)(2,1)S(1)}, bf16[8,64,256]{2,1,0:T(8,128)(2,1)S(1)}, u32[]{:S(2)}, u32[]{:S(2)}) %collective-permute-start.7) | collective-permute-done | bytes 262176 | tf_op jit(solution)/shard_map/ppermute | solution.py:428
  108.4 5.8 %collective-permute-done.8.second_due = bf16[8,64,256]{2,1,0:T(8,128)(2,1)S(1)} collective-permute-done((bf16[8,64,256]{2,1,0:T(8,128)(2,1)S(1)}, bf16[8,64,256]{2,1,0:T(8,128)(2,1)S(1)}, u32[]{:S(2)}, u32[]{:S(2)}) %collective-permute-start.8) | collective-permute-done | bytes 262176 | tf_op jit(solution)/shard_map/ppermute | solution.py:429
  114.3 1.1 shard_map.42
  (1 shorter events, 0.0 us)
Async XLA Ops:
  0.0 1.6 %copy-start = (bf16[16,64,1024]{2,1,0:T(8,128)(2,1)S(1)}, bf16[16,64,1024]{2,1,0:T(8,128)(2,1)}, u32[]{:S(2)}) copy-start(bf16[16,64,1024]{2,1,0:T(8,128)(2,1)} %dens.7) | copy-start | bytes 6291460
  1.6 0.7 copy-start.2
  2.8 53.3 %collective-permute-start = (bf16[17,64,512]{2,1,0:T(8,128)(2,1)S(1)}, bf16[17,64,512]{2,1,0:T(8,128)(2,1)S(1)}, u32[]{:S(2)}, u32[]{:S(2)}) collective-permute-start(bf16[17,64,512]{2,1,0:T(8,128)(2,1)S(1)} %shard_map.39), channel_id=1, source_target_pairs={{1,0},{3,2},{2,511},{5,4},{7,6},{6,3},{9,8},{11,10},{10,7},{13,12}... | collective-permute-start | bytes 3342344 | tf_op jit(solution)/shard_map/ppermute | solution.py:392
  4.1 52.0 %collective-permute-start.1 = (bf16[17,64,512]{2,1,0:T(8,128)(2,1)S(1)}, bf16[17,64,512]{2,1,0:T(8,128)(2,1)S(1)}, u32[]{:S(2)}, u32[]{:S(2)}) collective-permute-start(bf16[17,64,512]{2,1,0:T(8,128)(2,1)S(1)} %get-tuple-element.22), channel_id=1, source_target_pairs={{0,508},{3,511},{1,510},{4,0},{7,3},{5,2},{8,4},{11,7},{9,6},{12,8... | collective-permute-start | bytes 3342344 | tf_op jit(solution)/shard_map/ppermute | solution.py:393
  7.1 49.0 %copy-start.1 = (bf16[16,64,1024]{2,1,0:T(8,128)(2,1)S(1)}, bf16[16,64,1024]{2,1,0:T(8,128)(2,1)}, u32[]{:S(2)}) copy-start(bf16[16,64,1024]{2,1,0:T(8,128)(2,1)} %dens.7) | copy-start | bytes 6291460
  7.1 2.7 %collective-permute-start.2 = (bf16[8,64,128]{2,1,0:T(8,128)(2,1)S(1)}, bf16[8,64,128]{2,1,0:T(8,128)(2,1)S(1)}, u32[]{:S(2)}, u32[]{:S(2)}) collective-permute-start(bf16[8,64,128]{2,1,0:T(8,128)(2,1)S(1)} %get-tuple-element.23), channel_id=1, source_target_pairs={{2,510},{6,2},{10,6},{14,10},{18,14},{22,18},{26,22},{30,26},{34,3... | collective-permute-start | bytes 393224 | tf_op jit(solution)/shard_map/ppermute | solution.py:394
  56.1 47.3 %copy-start.3 = (s32[16,4]{0,1:T(4,128)S(1)}, s32[16,4]{0,1:T(4,128)}, u32[]{:S(2)}) copy-start(s32[16,4]{0,1:T(4,128)} %param.5) | copy-start | bytes 772
  59.4 27.0 %collective-permute-start.5 = (bf16[8,64,256]{2,1,0:T(8,128)(2,1)S(1)}, bf16[8,64,256]{2,1,0:T(8,128)(2,1)S(1)}, u32[]{:S(2)}, u32[]{:S(2)}) collective-permute-start(bf16[8,64,256]{2,1,0:T(8,128)(2,1)S(1)} %get-tuple-element.29), channel_id=1, source_target_pairs={{0,1},{2,3},{3,0},{4,5},{6,7},{7,4},{8,9},{10,11},{11,8},{12,13},{... | collective-permute-start | bytes 786440 | tf_op jit(solution)/shard_map/ppermute | solution.py:412
  61.4 25.1 %collective-permute-start.6 = (bf16[8,64,256]{2,1,0:T(8,128)(2,1)S(1)}, bf16[8,64,256]{2,1,0:T(8,128)(2,1)S(1)}, u32[]{:S(2)}, u32[]{:S(2)}) collective-permute-start(bf16[8,64,256]{2,1,0:T(8,128)(2,1)S(1)} %get-tuple-element.30), channel_id=1, source_target_pairs={{0,3},{2,1},{3,2},{4,7},{6,5},{7,6},{8,11},{10,9},{11,10},{12,15},... | collective-permute-start | bytes 786440 | tf_op jit(solution)/shard_map/ppermute | solution.py:413
  73.2 30.3 %collective-permute-start.3 = (bf16[8,64,256]{2,1,0:T(8,128)(2,1)S(1)}, bf16[8,64,256]{2,1,0:T(8,128)(2,1)S(1)}, u32[]{:S(2)}, u32[]{:S(2)}) collective-permute-start(bf16[8,64,256]{2,1,0:T(8,128)(2,1)S(1)} %get-tuple-element.25), channel_id=1, source_target_pairs={{0,1},{2,3},{3,0},{4,5},{6,7},{7,4},{8,9},{10,11},{11,8},{12,13},{... | collective-permute-start | bytes 786440 | tf_op jit(solution)/shard_map/ppermute | solution.py:414
  75.1 28.4 %collective-permute-start.4 = (bf16[8,64,256]{2,1,0:T(8,128)(2,1)S(1)}, bf16[8,64,256]{2,1,0:T(8,128)(2,1)S(1)}, u32[]{:S(2)}, u32[]{:S(2)}) collective-permute-start(bf16[8,64,256]{2,1,0:T(8,128)(2,1)S(1)} %get-tuple-element.26), channel_id=1, source_target_pairs={{0,3},{2,1},{3,2},{4,7},{6,5},{7,6},{8,11},{10,9},{11,10},{12,15},... | collective-permute-start | bytes 786440 | tf_op jit(solution)/shard_map/ppermute | solution.py:415
  86.6 21.8 %collective-permute-start.7 = (bf16[8,64,256]{2,1,0:T(8,128)(2,1)S(1)}, bf16[8,64,256]{2,1,0:T(8,128)(2,1)S(1)}, u32[]{:S(2)}, u32[]{:S(2)}) collective-permute-start(bf16[8,64,256]{2,1,0:T(8,128)(2,1)S(1)} %get-tuple-element.31), channel_id=1, source_target_pairs={{0,1},{1,2},{2,3},{3,0},{4,5},{5,6},{6,7},{7,4},{8,9},{9,10},{10,1... | collective-permute-start | bytes 786440 | tf_op jit(solution)/shard_map/ppermute | solution.py:428
  101.5 12.8 %collective-permute-start.8 = (bf16[8,64,256]{2,1,0:T(8,128)(2,1)S(1)}, bf16[8,64,256]{2,1,0:T(8,128)(2,1)S(1)}, u32[]{:S(2)}, u32[]{:S(2)}) collective-permute-start(bf16[8,64,256]{2,1,0:T(8,128)(2,1)S(1)} %get-tuple-element.32), channel_id=1, source_target_pairs={{0,3},{1,0},{2,1},{3,2},{4,7},{5,4},{6,5},{7,6},{8,11},{9,8},{10,9... | collective-permute-start | bytes 786440 | tf_op jit(solution)/shard_map/ppermute | solution.py:429

commit v8 on v6

--- a/solution.py
+++ b/solution.py
@@ -45,17 +45,6 @@
 
 def lower_width(i):
     return 128 * ((i - 1) // 2 + 1)
-
-
-def lower_place(i):
-    a, e = (i - 1) // 2, (i - 1) % 2
-    width = lower_width(i)
-    if a < 3:
-        return [(2 * (2 * a + e) + 1, HALF - width, 0, width)]
-    if a == 3:
-        return [(12 + e, 0, 0, width)]
-    row = 7 if i == ROWS - 1 else 2 * (6 - a) + e
-    return [(2 * row, 0, 0, HALF), (2 * row + 1, 0, HALF, width - HALF)]
 
 
 def put_upper(own, put):
@@ -70,11 +59,13 @@
 
 
 def put_lower(own, put):
-    for i in range(1, ROWS):
-        width = lower_width(i)
-        part = own(i, WIDE - width, WIDE)
-        for n, lane, first, lanes in lower_place(i):
-            put(n, lane, part[:, first : first + lanes])
+    for i in range(8, ROWS):
+        put(i - 8, own(i, HALF, WIDE))
+    for r in range(1, 8):
+        odd = BS * (r % 2)
+        left = own(8 - r, HALF + 128 * (r // 2), WIDE)[:, odd:]
+        right = own(8 + r, HALF - 128 * ((r + 1) // 2), HALF)[:, odd:]
+        put(7 + r, jnp.concatenate([left, right], axis=1))
 
 
 def pack_kernel(dens, pat, upper, diag, mask):
@@ -92,18 +83,18 @@
         diag[a] = jnp.concatenate(pair, axis=1)
 
 
-def pack_first_kernel(dens, mask, upper, lower):
+def pack_first_kernel(dens, mask, lower, upper):
     def own(i, lo, hi):
         return masked_lanes(dens, mask, i, lo, hi)
 
-    def put(n, part):
+    def put_low(n, part):
+        lower[n] = part
+
+    def put_up(n, part):
         upper[n] = part
 
-    def put_at(n, lane, part):
-        lower[n, :, lane : lane + part.shape[1]] = part
-
-    put_upper(own, put)
-    put_lower(own, put_at)
+    put_lower(own, put_low)
+    put_upper(own, put_up)
 
 
 def own_parts(dens, mask):
@@ -130,37 +121,43 @@
 
 def sent_lower(buf):
     def get(i):
-        pieces = [buf[n, :, lane : lane + lanes] for n, lane, _, lanes in lower_place(i)]
-        return pieces[0] if len(pieces) == 1 else jnp.concatenate(pieces, axis=1)
+        if i < 8:
+            return buf[15 - i]
+        if i == 8:
+            return buf[0]
+        return jnp.concatenate([buf[i - 1, :, HALF - 128 * ((i - 7) // 2) :], buf[i - 8]], axis=1)
 
     return get
 
 
-def build(dst, base, lower, upper, packed=False):
+def build(dst, base, lower, upper, packed_lower=False, packed_upper=False):
     lane = lax.broadcasted_iota(jnp.int32, (BS, WIDE), 1)
     for i in range(ROWS):
         rows = slice(base + i * BS, base + (i + 1) * BS)
+        low_placed = packed_lower and 0 < i < 8
+        up_placed = packed_upper and i >= 8
+        shifted_lower = lower and not low_placed
+        shifted_upper = upper and not up_placed
         parts = []
         if i > 0:
-            parts.append(lower(i) if lower else jnp.zeros((BS, lower_width(i)), jnp.bfloat16))
-        placed = packed and i >= 8
-        if upper and not placed:
-            parts.append(upper(i))
-        else:
-            parts.append(jnp.zeros((BS, upper_width(i)), jnp.bfloat16))
+            zeros = jnp.zeros((BS, lower_width(i)), jnp.bfloat16)
+            parts.append(lower(i) if shifted_lower else zeros)
+        zeros = jnp.zeros((BS, upper_width(i)), jnp.bfloat16)
+        parts.append(upper(i) if shifted_upper else zeros)
         both = jnp.concatenate(parts, axis=1) if i > 0 else parts[0]
         if i % 2:
             both = both[:, BS : BS + WIDE]
-            if not lower:
+            if not shifted_lower:
                 both = jnp.where(lane >= i * BS, both, jnp.zeros_like(both))
-            if not upper or placed:
+            if not shifted_upper:
                 both = jnp.where(lane < i * BS, both, jnp.zeros_like(both))
-        if placed:
-            dst[rows, :HALF] = both[:, :HALF]
-            right = jnp.where(lane[:, HALF:] >= i * BS, upper(i), both[:, HALF:])
-            dst[rows, HALF:] = right
-        else:
-            dst[rows, :] = both
+        left, right = both[:, :HALF], both[:, HALF:]
+        if low_placed:
+            left = jnp.where(lane[:, :HALF] < i * BS, lower(i), left)
+        if up_placed:
+            right = jnp.where(lane[:, HALF:] >= i * BS, upper(i), right)
+        dst[rows, :HALF] = left
+        dst[rows, HALF:] = right
 
 
 def put_diagonal(dst, base, diag):
@@ -222,9 +219,9 @@
     mask,
     y,
     acc,
+    got_lower,
     got_depth,
     got_y,
-    got_lower,
     got_diag,
     own,
     first1,
@@ -277,8 +274,8 @@
 
     @pl.when(q == 0)
     def _():
-        build(z, 0, own_lower, sent_upper(got_depth), True)
-        build(z, WIDE, None, sent_upper(got_y), True)
+        build(z, 0, own_lower, sent_upper(got_depth), packed_upper=True)
+        build(z, WIDE, None, sent_upper(got_y), packed_upper=True)
         products(0)
 
     @pl.when(q == 1)
@@ -288,15 +285,15 @@
 
     @pl.when(q == 2)
     def _():
-        build(z, 0, own_lower, sent_upper(got_depth), True)
-        build(z, WIDE, sent_lower(got_lower), None)
+        build(z, 0, own_lower, sent_upper(got_depth), packed_upper=True)
+        build(z, WIDE, sent_lower(got_lower), None, packed_lower=True)
         put_diagonal(z, WIDE, got_diag)
         mirror(z, WIDE, True)
         products(2)
 
     @pl.when(q == 3)
     def _():
-        build(z, WIDE, sent_lower(got_lower), sent_upper(got_y), True)
+        build(z, WIDE, sent_lower(got_lower), sent_upper(got_y), True, True)
         products(3)
 
 
@@ -342,7 +339,7 @@
         )(*operands)
 
     upper_part = (17, BS, HALF)
-    lower_part = (16, BS, HALF)
+    lower_part = (15, BS, HALF)
     share = (ROWS, BS, TILE)
     half_share = (ROWS // 2, BS, TILE)
     half = groups // 2
@@ -357,9 +354,9 @@
         density,
         pattern,
     )
-    upper_first, lower = call(
+    lower, upper_first = call(
         pack_first_kernel,
-        (upper_part, lower_part),
+        (lower_part, upper_part),
         [],
         16,
         4_000_000,
@@ -381,19 +378,19 @@
     def device(g, q):
         return (g % groups) * 4 + q
 
-    by_depth, by_y, of_lower, of_diag, first_route, second_route = [], [], [], [], [], []
+    of_lower, by_depth, by_y, of_diag, first_route, second_route = [], [], [], [], [], []
     for g in range(groups):
+        of_lower += [(device(g, 1), device(g - 1, 2)), (device(g, 2), device(g - 1, 3))]
         by_depth += [(device(g, 1), device(g, 0)), (device(g, 3), device(g, 2))]
         by_y += [(device(g, 0), device(g - 1, 0)), (device(g, 3), device(g - 1, 3))]
-        of_lower += [(device(g, 1), device(g - 1, 2)), (device(g, 2), device(g - 1, 3))]
         of_diag.append((device(g, 2), device(g - 1, 2)))
         for q in range(4):
             up = (device(g, q), device(g, (q + 1) % 4))
             down = (device(g, q), device(g, (q - 1) % 4))
             first_route.append(down if g >= half else up)
             second_route.append(up if g >= half else down)
+    got_lower = lax.ppermute(lower, AXES, of_lower)
     got_depth = lax.ppermute(upper_first, AXES, by_depth)
-    got_lower = lax.ppermute(lower, AXES, of_lower)
     got_y = lax.ppermute(upper, AXES, by_y)
     got_diag = lax.ppermute(diag, AXES, of_diag)
 
@@ -408,9 +405,9 @@
         mask,
         prepared,
         ahead,
+        got_lower,
         got_depth,
         got_y,
-        got_lower,
         got_diag,
     )
 

time: 116 us -> 113 us (0.974)
  waiting for transfers between devices: 42.5 us -> 40.1 us
    ppermute x1, starting transfers between devices: 36.7 us -> 33.9 us  [per_device(): lax.ppermute(first1, AXES, [r for r in first_route if r[0] % 4 != 1])]
    ppermute x1, waiting for transfers between devices: 11.8 us -> 9.01 us  [per_device(): lax.ppermute(second1, AXES, [r for r in second_route if r[0] % 4 != 1])]
    ppermute x1, starting transfers between devices: 4.49 us -> 7.2 us  [per_device(): first_due = lax.ppermute(first_due, AXES, first_route)]
where the time goes in v8:
time: 113 us
  starting transfers between devices  63.3 us (56%)
  waiting for transfers between devices  40.1 us (35%)
  Pallas kernels  6.89 us (6%)
  local copies, waits for them, and re-layouts  2.38 us (2%)
    ppermute x1, starting transfers between devices, per_device(): lax.ppermute(first1, AXES, [r for r in first_route if r[0] % 4 != 1])  33.9 us
    ppermute x1, waiting for transfers between devices, per_device(): got_depth = lax.ppermute(upper_first, AXES, by_depth)  20.3 us
    ppermute x1, waiting for transfers between devices, per_device(): lax.ppermute(second1, AXES, [r for r in second_route if r[0] % 4 != 1])  9.01 us
    ppermute x1, starting transfers between devices, per_device(): lax.ppermute(first_free, AXES, [r for r in first_route if r[0] % 4 != 1])  8.5 us
    ppermute x1, starting transfers between devices, per_device(): first_due = lax.ppermute(first_due, AXES, first_route)  7.2 us
    pallas_call x6, Pallas kernels, call(): pl.pallas_call(kernel, out_shape=tuple((jax.ShapeDtypeStruct(shape, jnp.f...  6.89 us
    ppermute x1, waiting for transfers between devices, per_device(): second_due = lax.ppermute(second_due, AXES, second_route)  5.98 us
    ppermute x1, starting transfers between devices, per_device(): got_y = lax.ppermute(upper, AXES, by_y)  5.08 us
  transfers between devices with their start and end apart: 10, of which 5 were waited for; matrix products, arithmetic and copies ran while one was open for 0% of the time, Pallas kernels for 2%

profile of v8, /device:TPU:70, one launch (start us, length us, event | category | flops | bytes accessed | tf_op | source)
XLA Modules:
  0.0 112.8 jit_solution(3654018817818692682)
XLA Ops:
  0.0 1.6 %copy-done = bf16[16,64,1024]{2,1,0:T(8,128)(2,1)S(1)} copy-done((bf16[16,64,1024]{2,1,0:T(8,128)(2,1)S(1)}, bf16[16,64,1024]{2,1,0:T(8,128)(2,1)}, u32[]{:S(2)}) %copy-start) | copy-done | bytes 2097176
  1.6 0.7 copy-done.2
  2.3 0.3 shard_map.37
  2.6 0.2 shard_map.39
  2.9 1.3 %collective-permute-start.1 = (bf16[17,64,512]{2,1,0:T(8,128)(2,1)S(1)}, bf16[17,64,512]{2,1,0:T(8,128)(2,1)S(1)}, u32[]{:S(2)}, u32[]{:S(2)}) collective-permute-start(bf16[17,64,512]{2,1,0:T(8,128)(2,1)S(1)} %get-tuple-element.25), channel_id=1, source_target_pairs={{1,0},{3,2},{5,4},{7,6},{9,8},{11,10},{13,12},{15,14},{17,16},{19,... | collective-permute-start | bytes 3342344 | tf_op jit(solution)/shard_map/ppermute | solution.py:393
  4.2 5.1 %collective-permute-start.2 = (bf16[17,64,512]{2,1,0:T(8,128)(2,1)S(1)}, bf16[17,64,512]{2,1,0:T(8,128)(2,1)S(1)}, u32[]{:S(2)}, u32[]{:S(2)}) collective-permute-start(bf16[17,64,512]{2,1,0:T(8,128)(2,1)S(1)} %get-tuple-element.26), channel_id=1, source_target_pairs={{0,508},{3,511},{4,0},{7,3},{8,4},{11,7},{12,8},{15,11},{16,12},{1... | collective-permute-start | bytes 3342344 | tf_op jit(solution)/shard_map/ppermute | solution.py:394
  9.2 0.7 collective-permute-start
  10.0 0.0 copy-start.1
  10.0 0.8 collective-permute-start.3
  10.8 1.9 %shard_map.38 = (bf16[1024,1024]{1,0:T(8,128)(2,1)S(1)}, f32[4,256,1024]{2,1,0:T(8,128)S(1)}) custom-call(bf16[16,64,1024]{2,1,0:T(8,128)(2,1)S(1)} %copy-done, f32[16,1024]{1,0:T(8,128)S(1)} %get-tuple-element.21.mask), custom_call_target="tpu_custom_call" | custom-call | flops 3000000000 | bytes 9500000 | tf_op jit(solution)/shard_map/pallas_call | solution.py:328
  12.7 0.0 collective-permute-done.3.got_diag
  12.7 0.0 collective-permute-done.got_lower
  12.7 20.3 %collective-permute-done.1.got_depth = bf16[17,64,512]{2,1,0:T(8,128)(2,1)S(1)} collective-permute-done((bf16[17,64,512]{2,1,0:T(8,128)(2,1)S(1)}, bf16[17,64,512]{2,1,0:T(8,128)(2,1)S(1)}, u32[]{:S(2)}, u32[]{:S(2)}) %collective-permute-start.1) | collective-permute-done | bytes 1114144 | tf_op jit(solution)/shard_map/ppermute | solution.py:393
  33.0 0.9 collective-permute-done.2.got_y
  33.9 0.0 copy-done.1
  33.9 3.3 %shard_map.40 = (bf16[16,64,256]{2,1,0:T(8,128)(2,1)S(1)}, bf16[8,64,256]{2,1,0:T(8,128)(2,1)S(1)}, bf16[8,64,256]{2,1,0:T(8,128)(2,1)S(1)}, bf16[8,64,256]{2,1,...) custom-call(bf16[16,64,1024]{2,1,0:T(8,128)(2,1)S(1)} %copy-done.1, ...), custom_call_target="tpu_custom_call" | custom-call | flops 6000000000 | bytes 14000000 | tf_op jit(solution)/shard_map/pallas_call | solution.py:328
  37.2 33.9 %collective-permute-start.6 = (bf16[8,64,256]{2,1,0:T(8,128)(2,1)S(1)}, bf16[8,64,256]{2,1,0:T(8,128)(2,1)S(1)}, u32[]{:S(2)}, u32[]{:S(2)}) collective-permute-start(bf16[8,64,256]{2,1,0:T(8,128)(2,1)S(1)} %get-tuple-element.33), channel_id=1, source_target_pairs={{0,1},{2,3},{3,0},{4,5},{6,7},{7,4},{8,9},{10,11},{11,8},{12,13},{... | collective-permute-start | bytes 786440 | tf_op jit(solution)/shard_map/ppermute | solution.py:414
  71.1 1.9 %collective-permute-start.7 = (bf16[8,64,256]{2,1,0:T(8,128)(2,1)S(1)}, bf16[8,64,256]{2,1,0:T(8,128)(2,1)S(1)}, u32[]{:S(2)}, u32[]{:S(2)}) collective-permute-start(bf16[8,64,256]{2,1,0:T(8,128)(2,1)S(1)} %get-tuple-element.34), channel_id=1, source_target_pairs={{0,3},{2,1},{3,2},{4,7},{6,5},{7,6},{8,11},{10,9},{11,10},{12,15},... | collective-permute-start | bytes 786440 | tf_op jit(solution)/shard_map/ppermute | solution.py:415
  73.0 8.5 %collective-permute-start.4 = (bf16[8,64,256]{2,1,0:T(8,128)(2,1)S(1)}, bf16[8,64,256]{2,1,0:T(8,128)(2,1)S(1)}, u32[]{:S(2)}, u32[]{:S(2)}) collective-permute-start(bf16[8,64,256]{2,1,0:T(8,128)(2,1)S(1)} %get-tuple-element.29), channel_id=1, source_target_pairs={{0,1},{2,3},{3,0},{4,5},{6,7},{7,4},{8,9},{10,11},{11,8},{12,13},{... | collective-permute-start | bytes 786440 | tf_op jit(solution)/shard_map/ppermute | solution.py:416
  81.6 1.9 %collective-permute-start.5 = (bf16[8,64,256]{2,1,0:T(8,128)(2,1)S(1)}, bf16[8,64,256]{2,1,0:T(8,128)(2,1)S(1)}, u32[]{:S(2)}, u32[]{:S(2)}) collective-permute-start(bf16[8,64,256]{2,1,0:T(8,128)(2,1)S(1)} %get-tuple-element.30), channel_id=1, source_target_pairs={{0,3},{2,1},{3,2},{4,7},{6,5},{7,6},{8,11},{10,9},{11,10},{12,15},... | collective-permute-start | bytes 786440 | tf_op jit(solution)/shard_map/ppermute | solution.py:417
  83.5 0.0 collective-permute-done.6.got_first
  83.5 9.0 %collective-permute-done.7.got_second = bf16[8,64,256]{2,1,0:T(8,128)(2,1)S(1)} collective-permute-done((bf16[8,64,256]{2,1,0:T(8,128)(2,1)S(1)}, bf16[8,64,256]{2,1,0:T(8,128)(2,1)S(1)}, u32[]{:S(2)}, u32[]{:S(2)}) %collective-permute-start.7) | collective-permute-done | bytes 262176 | tf_op jit(solution)/shard_map/ppermute | solution.py:415
  92.5 0.1 shard_map.41
  92.6 7.2 %collective-permute-start.8 = (bf16[8,64,256]{2,1,0:T(8,128)(2,1)S(1)}, bf16[8,64,256]{2,1,0:T(8,128)(2,1)S(1)}, u32[]{:S(2)}, u32[]{:S(2)}) collective-permute-start(bf16[8,64,256]{2,1,0:T(8,128)(2,1)S(1)} %get-tuple-element.35), channel_id=1, source_target_pairs={{0,1},{1,2},{2,3},{3,0},{4,5},{5,6},{6,7},{7,4},{8,9},{9,10},{10,1... | collective-permute-start | bytes 786440 | tf_op jit(solution)/shard_map/ppermute | solution.py:430
  99.8 1.9 %collective-permute-start.9 = (bf16[8,64,256]{2,1,0:T(8,128)(2,1)S(1)}, bf16[8,64,256]{2,1,0:T(8,128)(2,1)S(1)}, u32[]{:S(2)}, u32[]{:S(2)}) collective-permute-start(bf16[8,64,256]{2,1,0:T(8,128)(2,1)S(1)} %get-tuple-element.36), channel_id=1, source_target_pairs={{0,3},{1,0},{2,1},{3,2},{4,7},{5,4},{6,5},{7,6},{8,11},{9,8},{10,9... | collective-permute-start | bytes 786440 | tf_op jit(solution)/shard_map/ppermute | solution.py:431
  101.8 0.0 copy-done.3
  101.8 0.1 copy.4.keep
  101.9 0.0 collective-permute-done.4.first_free
  101.9 0.0 collective-permute-done.5.second_free
  101.9 3.8 %collective-permute-done.8.first_due = bf16[8,64,256]{2,1,0:T(8,128)(2,1)S(1)} collective-permute-done((bf16[8,64,256]{2,1,0:T(8,128)(2,1)S(1)}, bf16[8,64,256]{2,1,0:T(8,128)(2,1)S(1)}, u32[]{:S(2)}, u32[]{:S(2)}) %collective-permute-start.8) | collective-permute-done | bytes 262176 | tf_op jit(solution)/shard_map/ppermute | solution.py:430
  105.7 6.0 %collective-permute-done.9.second_due = bf16[8,64,256]{2,1,0:T(8,128)(2,1)S(1)} collective-permute-done((bf16[8,64,256]{2,1,0:T(8,128)(2,1)S(1)}, bf16[8,64,256]{2,1,0:T(8,128)(2,1)S(1)}, u32[]{:S(2)}, u32[]{:S(2)}) %collective-permute-start.9) | collective-permute-done | bytes 262176 | tf_op jit(solution)/shard_map/ppermute | solution.py:431
  111.7 1.1 shard_map.42
  (3 shorter events, 0.0 us)
Async XLA Ops:
  0.0 1.6 %copy-start = (bf16[16,64,1024]{2,1,0:T(8,128)(2,1)S(1)}, bf16[16,64,1024]{2,1,0:T(8,128)(2,1)}, u32[]{:S(2)}) copy-start(bf16[16,64,1024]{2,1,0:T(8,128)(2,1)} %dens.7) | copy-start | bytes 6291460
  1.6 0.7 copy-start.2
  2.9 30.1 %collective-permute-start.1 = (bf16[17,64,512]{2,1,0:T(8,128)(2,1)S(1)}, bf16[17,64,512]{2,1,0:T(8,128)(2,1)S(1)}, u32[]{:S(2)}, u32[]{:S(2)}) collective-permute-start(bf16[17,64,512]{2,1,0:T(8,128)(2,1)S(1)} %get-tuple-element.25), channel_id=1, source_target_pairs={{1,0},{3,2},{5,4},{7,6},{9,8},{11,10},{13,12},{15,14},{17,16},{19,... | collective-permute-start | bytes 3342344 | tf_op jit(solution)/shard_map/ppermute | solution.py:393
  4.2 29.7 %collective-permute-start.2 = (bf16[17,64,512]{2,1,0:T(8,128)(2,1)S(1)}, bf16[17,64,512]{2,1,0:T(8,128)(2,1)S(1)}, u32[]{:S(2)}, u32[]{:S(2)}) collective-permute-start(bf16[17,64,512]{2,1,0:T(8,128)(2,1)S(1)} %get-tuple-element.26), channel_id=1, source_target_pairs={{0,508},{3,511},{4,0},{7,3},{8,4},{11,7},{12,8},{15,11},{16,12},{1... | collective-permute-start | bytes 3342344 | tf_op jit(solution)/shard_map/ppermute | solution.py:394
  9.2 3.4 %collective-permute-start = (bf16[15,64,512]{2,1,0:T(8,128)(2,1)S(1)}, bf16[15,64,512]{2,1,0:T(8,128)(2,1)S(1)}, u32[]{:S(2)}, u32[]{:S(2)}) collective-permute-start(bf16[15,64,512]{2,1,0:T(8,128)(2,1)S(1)} %get-tuple-element.24), channel_id=1, source_target_pairs={{1,510},{2,511},{5,2},{6,3},{9,6},{10,7},{13,10},{14,11},{17,14},{... | collective-permute-start | bytes 2949128 | tf_op jit(solution)/shard_map/ppermute | solution.py:392
  10.0 23.9 %copy-start.1 = (bf16[16,64,1024]{2,1,0:T(8,128)(2,1)S(1)}, bf16[16,64,1024]{2,1,0:T(8,128)(2,1)}, u32[]{:S(2)}) copy-start(bf16[16,64,1024]{2,1,0:T(8,128)(2,1)} %dens.7) | copy-start | bytes 6291460
  10.0 2.7 %collective-permute-start.3 = (bf16[8,64,128]{2,1,0:T(8,128)(2,1)S(1)}, bf16[8,64,128]{2,1,0:T(8,128)(2,1)S(1)}, u32[]{:S(2)}, u32[]{:S(2)}) collective-permute-start(bf16[8,64,128]{2,1,0:T(8,128)(2,1)S(1)} %get-tuple-element.27), channel_id=1, source_target_pairs={{2,510},{6,2},{10,6},{14,10},{18,14},{22,18},{26,22},{30,26},{34,3... | collective-permute-start | bytes 393224 | tf_op jit(solution)/shard_map/ppermute | solution.py:395
  33.9 67.9 %copy-start.3 = (s32[16,4]{0,1:T(4,128)S(1)}, s32[16,4]{0,1:T(4,128)}, u32[]{:S(2)}) copy-start(s32[16,4]{0,1:T(4,128)} %param.5) | copy-start | bytes 772
  37.2 46.3 %collective-permute-start.6 = (bf16[8,64,256]{2,1,0:T(8,128)(2,1)S(1)}, bf16[8,64,256]{2,1,0:T(8,128)(2,1)S(1)}, u32[]{:S(2)}, u32[]{:S(2)}) collective-permute-start(bf16[8,64,256]{2,1,0:T(8,128)(2,1)S(1)} %get-tuple-element.33), channel_id=1, source_target_pairs={{0,1},{2,3},{3,0},{4,5},{6,7},{7,4},{8,9},{10,11},{11,8},{12,13},{... | collective-permute-start | bytes 786440 | tf_op jit(solution)/shard_map/ppermute | solution.py:414
  71.1 21.4 %collective-permute-start.7 = (bf16[8,64,256]{2,1,0:T(8,128)(2,1)S(1)}, bf16[8,64,256]{2,1,0:T(8,128)(2,1)S(1)}, u32[]{:S(2)}, u32[]{:S(2)}) collective-permute-start(bf16[8,64,256]{2,1,0:T(8,128)(2,1)S(1)} %get-tuple-element.34), channel_id=1, source_target_pairs={{0,3},{2,1},{3,2},{4,7},{6,5},{7,6},{8,11},{10,9},{11,10},{12,15},... | collective-permute-start | bytes 786440 | tf_op jit(solution)/shard_map/ppermute | solution.py:415
  73.0 28.8 %collective-permute-start.4 = (bf16[8,64,256]{2,1,0:T(8,128)(2,1)S(1)}, bf16[8,64,256]{2,1,0:T(8,128)(2,1)S(1)}, u32[]{:S(2)}, u32[]{:S(2)}) collective-permute-start(bf16[8,64,256]{2,1,0:T(8,128)(2,1)S(1)} %get-tuple-element.29), channel_id=1, source_target_pairs={{0,1},{2,3},{3,0},{4,5},{6,7},{7,4},{8,9},{10,11},{11,8},{12,13},{... | collective-permute-start | bytes 786440 | tf_op jit(solution)/shard_map/ppermute | solution.py:416
  81.6 20.3 %collective-permute-start.5 = (bf16[8,64,256]{2,1,0:T(8,128)(2,1)S(1)}, bf16[8,64,256]{2,1,0:T(8,128)(2,1)S(1)}, u32[]{:S(2)}, u32[]{:S(2)}) collective-permute-start(bf16[8,64,256]{2,1,0:T(8,128)(2,1)S(1)} %get-tuple-element.30), channel_id=1, source_target_pairs={{0,3},{2,1},{3,2},{4,7},{6,5},{7,6},{8,11},{10,9},{11,10},{12,15},... | collective-permute-start | bytes 786440 | tf_op jit(solution)/shard_map/ppermute | solution.py:417
  92.6 13.1 %collective-permute-start.8 = (bf16[8,64,256]{2,1,0:T(8,128)(2,1)S(1)}, bf16[8,64,256]{2,1,0:T(8,128)(2,1)S(1)}, u32[]{:S(2)}, u32[]{:S(2)}) collective-permute-start(bf16[8,64,256]{2,1,0:T(8,128)(2,1)S(1)} %get-tuple-element.35), channel_id=1, source_target_pairs={{0,1},{1,2},{2,3},{3,0},{4,5},{5,6},{6,7},{7,4},{8,9},{9,10},{10,1... | collective-permute-start | bytes 786440 | tf_op jit(solution)/shard_map/ppermute | solution.py:430
  99.8 11.9 %collective-permute-start.9 = (bf16[8,64,256]{2,1,0:T(8,128)(2,1)S(1)}, bf16[8,64,256]{2,1,0:T(8,128)(2,1)S(1)}, u32[]{:S(2)}, u32[]{:S(2)}) collective-permute-start(bf16[8,64,256]{2,1,0:T(8,128)(2,1)S(1)} %get-tuple-element.36), channel_id=1, source_target_pairs={{0,3},{1,0},{2,1},{3,2},{4,7},{5,4},{6,5},{7,6},{8,11},{9,8},{10,9... | collective-permute-start | bytes 786440 | tf_op jit(solution)/shard_map/ppermute | solution.py:431

commit v9 on v8

--- a/solution.py
+++ b/solution.py
@@ -11,6 +11,7 @@
 WIDE = ROWS * BS
 HALF = WIDE // 2
 TILE = 256
+MAIN = 14
 AXES = ("row", "col", "depth")
 NT = (((1,), (1,)), ((), ()))
 NN = (((1,), (0,)), ((), ()))
@@ -68,19 +69,31 @@
         put(7 + r, jnp.concatenate([left, right], axis=1))
 
 
-def pack_kernel(dens, pat, upper, diag, mask):
+def pack_kernel(dens, pat, upper, rest, mask):
     mask[...] = expand(pat[...], WIDE)
+    diagonal = lax.axis_index("depth") == 2
 
     def own(i, lo, hi):
         return masked_lanes(dens, mask, i, lo, hi)
 
     def put(n, part):
-        upper[n] = part
+        if n < MAIN:
+            upper[n] = part
+        else:
+
+            @pl.when(jnp.logical_not(diagonal))
+            def _():
+                rest[n - MAIN] = part
 
     put_upper(own, put)
-    for a in range(ROWS // 2):
-        pair = [own(2 * a + e, 0, 2 * BS)[:, :BS] for e in range(2)]
-        diag[a] = jnp.concatenate(pair, axis=1)
+
+    @pl.when(diagonal)
+    def _():
+        for a in range(ROWS // 2):
+            pair = [own(2 * a + e, 0, 2 * BS)[:, :BS] for e in range(2)]
+            lane = 2 * BS * (a % 4)
+            rest[a // 4, :, lane : lane + 2 * BS] = jnp.concatenate(pair, axis=1)
+        rest[2] = jnp.zeros((BS, HALF), jnp.bfloat16)
 
 
 def pack_first_kernel(dens, mask, lower, upper):
@@ -107,14 +120,18 @@
     return lower, upper
 
 
-def sent_upper(buf):
+def sent_upper(main, rest=None):
+    def part(n, lanes):
+        if rest is None or n < MAIN:
+            return main[n, :, :lanes]
+        return rest[n - MAIN, :, :lanes]
+
     def get(i):
         if i == 0:
-            return jnp.concatenate([buf[0], buf[1]], axis=1)
+            return jnp.concatenate([part(0, HALF), part(1, HALF)], axis=1)
         if i < 8:
-            rest = HALF - 128 * (i // 2)
-            return jnp.concatenate([buf[1 + i], buf[9 + i, :, :rest]], axis=1)
-        return buf[9 + ROWS - i if i > 8 else 9]
+            return jnp.concatenate([part(1 + i, HALF), part(9 + i, HALF - 128 * (i // 2))], axis=1)
+        return part(9 + ROWS - i if i > 8 else 9, HALF)
 
     return get
 
@@ -160,13 +177,15 @@
         dst[rows, HALF:] = right
 
 
-def put_diagonal(dst, base, diag):
+def put_diagonal(dst, base, rest):
     lane = lax.broadcasted_iota(jnp.int32, (BS, 2 * BS), 1)
     for i in range(ROWS):
         a = i // 2
         at = (slice(base + i * BS, base + (i + 1) * BS), slice(2 * BS * a, 2 * BS * (a + 1)))
+        first = 2 * BS * (a % 4)
+        diag = rest[a // 4, :, first : first + 2 * BS]
         mine = lane >= BS if i % 2 else lane < BS
-        dst[at] = jnp.where(mine, diag[a], dst[at])
+        dst[at] = jnp.where(mine, diag, dst[at])
 
 
 def mirror(dst, base, from_lower=False):
@@ -222,7 +241,7 @@
     got_lower,
     got_depth,
     got_y,
-    got_diag,
+    got_rest,
     own,
     first1,
     second1,
@@ -275,7 +294,7 @@
     @pl.when(q == 0)
     def _():
         build(z, 0, own_lower, sent_upper(got_depth), packed_upper=True)
-        build(z, WIDE, None, sent_upper(got_y), packed_upper=True)
+        build(z, WIDE, None, sent_upper(got_y, got_rest), packed_upper=True)
         products(0)
 
     @pl.when(q == 1)
@@ -287,13 +306,13 @@
     def _():
         build(z, 0, own_lower, sent_upper(got_depth), packed_upper=True)
         build(z, WIDE, sent_lower(got_lower), None, packed_lower=True)
-        put_diagonal(z, WIDE, got_diag)
+        put_diagonal(z, WIDE, got_rest)
         mirror(z, WIDE, True)
         products(2)
 
     @pl.when(q == 3)
     def _():
-        build(z, WIDE, sent_lower(got_lower), sent_upper(got_y), True, True)
+        build(z, WIDE, sent_lower(got_lower), sent_upper(got_y, got_rest), True, True)
         products(3)
 
 
@@ -344,9 +363,9 @@
     half_share = (ROWS // 2, BS, TILE)
     half = groups // 2
 
-    upper, diag, mask = call(
+    upper, rest, mask = call(
         pack_kernel,
-        (upper_part, (ROWS // 2, BS, 2 * BS), slot_mask),
+        ((MAIN, BS, HALF), (17 - MAIN, BS, HALF), slot_mask),
         [],
         16,
         4_000_000,
@@ -378,12 +397,12 @@
     def device(g, q):
         return (g % groups) * 4 + q
 
-    of_lower, by_depth, by_y, of_diag, first_route, second_route = [], [], [], [], [], []
+    of_lower, by_depth, by_y, of_rest, first_route, second_route = [], [], [], [], [], []
     for g in range(groups):
         of_lower += [(device(g, 1), device(g - 1, 2)), (device(g, 2), device(g - 1, 3))]
         by_depth += [(device(g, 1), device(g, 0)), (device(g, 3), device(g, 2))]
         by_y += [(device(g, 0), device(g - 1, 0)), (device(g, 3), device(g - 1, 3))]
-        of_diag.append((device(g, 2), device(g - 1, 2)))
+        of_rest += by_y[-2:] + [(device(g, 2), device(g - 1, 2))]
         for q in range(4):
             up = (device(g, q), device(g, (q + 1) % 4))
             down = (device(g, q), device(g, (q - 1) % 4))
@@ -392,7 +411,7 @@
     got_lower = lax.ppermute(lower, AXES, of_lower)
     got_depth = lax.ppermute(upper_first, AXES, by_depth)
     got_y = lax.ppermute(upper, AXES, by_y)
-    got_diag = lax.ppermute(diag, AXES, of_diag)
+    got_rest = lax.ppermute(rest, AXES, of_rest)
 
     own, first1, second1, first_free, second_free, first_due, second_due = call(
         functools.partial(main_kernel, half),
@@ -408,7 +427,7 @@
         got_lower,
         got_depth,
         got_y,
-        got_diag,
+        got_rest,
     )
 
     got_first = lax.ppermute(first1, AXES, [r for r in first_route if r[0] % 4 != 1])

time: 113 us -> 110 us (0.973)
  the two profiles are of different devices: /device:TPU:70 before, /device:TPU:63 now
where the time goes in v9:
time: 110 us
  waiting for transfers between devices  62.4 us (57%)
  starting transfers between devices  38.1 us (35%)
  Pallas kernels  6.94 us (6%)
  local copies, waits for them, and re-layouts  2.38 us (2%)
    ppermute x1, waiting for transfers between devices, per_device(): got_rest = lax.ppermute(rest, AXES, of_rest)  25 us
    ppermute x1, waiting for transfers between devices, per_device(): got_depth = lax.ppermute(upper_first, AXES, by_depth)  18.3 us
    ppermute x1, starting transfers between devices, per_device(): first_due = lax.ppermute(first_due, AXES, first_route)  8.7 us
    ppermute x1, starting transfers between devices, per_device(): lax.ppermute(second_free, AXES, [r for r in second_route if r[0] % 4 != 1])  8.43 us
    ppermute x1, waiting for transfers between devices, per_device(): second_due = lax.ppermute(second_due, AXES, second_route)  7.62 us
    ppermute x1, starting transfers between devices, per_device(): lax.ppermute(second1, AXES, [r for r in second_route if r[0] % 4 != 1])  7.11 us
    pallas_call x6, Pallas kernels, call(): pl.pallas_call(kernel, out_shape=tuple((jax.ShapeDtypeStruct(shape, jnp.f...  6.94 us
    ppermute x1, waiting for transfers between devices, per_device(): lax.ppermute(second1, AXES, [r for r in second_route if r[0] % 4 != 1])  6.59 us
  transfers between devices with their start and end apart: 10, of which 5 were waited for; matrix products, arithmetic and copies ran while one was open for 0% of the time, Pallas kernels for 2%

profile of v9, /device:TPU:63, one launch (start us, length us, event | category | flops | bytes accessed | tf_op | source)
XLA Modules:
  0.0 109.9 jit_solution(251092901560747572)
XLA Ops:
  0.0 1.6 %copy-done = bf16[16,64,1024]{2,1,0:T(8,128)(2,1)S(1)} copy-done((bf16[16,64,1024]{2,1,0:T(8,128)(2,1)S(1)}, bf16[16,64,1024]{2,1,0:T(8,128)(2,1)}, u32[]{:S(2)}) %copy-start) | copy-done | bytes 2097176
  1.6 0.7 copy-done.2
  2.3 0.4 shard_map.37
  2.7 0.2 shard_map.39
  2.9 1.3 %collective-permute-start.1 = (bf16[17,64,512]{2,1,0:T(8,128)(2,1)S(1)}, bf16[17,64,512]{2,1,0:T(8,128)(2,1)S(1)}, u32[]{:S(2)}, u32[]{:S(2)}) collective-permute-start(bf16[17,64,512]{2,1,0:T(8,128)(2,1)S(1)} %get-tuple-element.25), channel_id=1, source_target_pairs={{1,0},{3,2},{5,4},{7,6},{9,8},{11,10},{13,12},{15,14},{17,16},{19,... | collective-permute-start | bytes 3342344 | tf_op jit(solution)/shard_map/ppermute | solution.py:412
  4.2 0.7 collective-permute-start
  4.9 3.0 %collective-permute-start.2 = (bf16[14,64,512]{2,1,0:T(8,128)(2,1)S(1)}, bf16[14,64,512]{2,1,0:T(8,128)(2,1)S(1)}, u32[]{:S(2)}, u32[]{:S(2)}) collective-permute-start(bf16[14,64,512]{2,1,0:T(8,128)(2,1)S(1)} %get-tuple-element.26), channel_id=1, source_target_pairs={{0,508},{3,511},{4,0},{7,3},{8,4},{11,7},{12,8},{15,11},{16,12},{1... | collective-permute-start | bytes 2752520 | tf_op jit(solution)/shard_map/ppermute | solution.py:413
  7.9 0.0 copy-start.1
  7.9 3.1 %collective-permute-start.3 = (bf16[3,64,512]{2,1,0:T(8,128)(2,1)S(1)}, bf16[3,64,512]{2,1,0:T(8,128)(2,1)S(1)}, u32[]{:S(2)}, u32[]{:S(2)}) collective-permute-start(bf16[3,64,512]{2,1,0:T(8,128)(2,1)S(1)} %get-tuple-element.27), channel_id=1, source_target_pairs={{0,508},{3,511},{2,510},{4,0},{7,3},{6,2},{8,4},{11,7},{10,6},{12,... | collective-permute-start | bytes 589832 | tf_op jit(solution)/shard_map/ppermute | solution.py:414
  11.1 1.9 %shard_map.38 = (bf16[1024,1024]{1,0:T(8,128)(2,1)S(1)}, f32[4,256,1024]{2,1,0:T(8,128)S(1)}) custom-call(bf16[16,64,1024]{2,1,0:T(8,128)(2,1)S(1)} %copy-done, f32[16,1024]{1,0:T(8,128)S(1)} %get-tuple-element.21.mask), custom_call_target="tpu_custom_call" | custom-call | flops 3000000000 | bytes 9500000 | tf_op jit(solution)/shard_map/pallas_call | solution.py:347
  12.9 25.0 %collective-permute-done.3.got_rest = bf16[3,64,512]{2,1,0:T(8,128)(2,1)S(1)} collective-permute-done((bf16[3,64,512]{2,1,0:T(8,128)(2,1)S(1)}, bf16[3,64,512]{2,1,0:T(8,128)(2,1)S(1)}, u32[]{:S(2)}, u32[]{:S(2)}) %collective-permute-start.3) | collective-permute-done | bytes 196640 | tf_op jit(solution)/shard_map/ppermute | solution.py:414
  37.9 0.0 collective-permute-done.2.got_y
  37.9 0.0 collective-permute-done.got_lower
  37.9 18.3 %collective-permute-done.1.got_depth = bf16[17,64,512]{2,1,0:T(8,128)(2,1)S(1)} collective-permute-done((bf16[17,64,512]{2,1,0:T(8,128)(2,1)S(1)}, bf16[17,64,512]{2,1,0:T(8,128)(2,1)S(1)}, u32[]{:S(2)}, u32[]{:S(2)}) %collective-permute-start.1) | collective-permute-done | bytes 1114144 | tf_op jit(solution)/shard_map/ppermute | solution.py:412
  56.2 0.0 copy-done.1
  56.2 3.3 %shard_map.40 = (bf16[16,64,256]{2,1,0:T(8,128)(2,1)S(1)}, bf16[8,64,256]{2,1,0:T(8,128)(2,1)S(1)}, bf16[8,64,256]{2,1,0:T(8,128)(2,1)S(1)}, bf16[8,64,256]{2,1,...) custom-call(bf16[16,64,1024]{2,1,0:T(8,128)(2,1)S(1)} %copy-done.1, ...), custom_call_target="tpu_custom_call" | custom-call | flops 6000000000 | bytes 14000000 | tf_op jit(solution)/shard_map/pallas_call | solution.py:347
  59.5 1.9 %collective-permute-start.6 = (bf16[8,64,256]{2,1,0:T(8,128)(2,1)S(1)}, bf16[8,64,256]{2,1,0:T(8,128)(2,1)S(1)}, u32[]{:S(2)}, u32[]{:S(2)}) collective-permute-start(bf16[8,64,256]{2,1,0:T(8,128)(2,1)S(1)} %get-tuple-element.33), channel_id=1, source_target_pairs={{0,1},{2,3},{3,0},{4,5},{6,7},{7,4},{8,9},{10,11},{11,8},{12,13},{... | collective-permute-start | bytes 786440 | tf_op jit(solution)/shard_map/ppermute | solution.py:433
  61.5 7.1 %collective-permute-start.7 = (bf16[8,64,256]{2,1,0:T(8,128)(2,1)S(1)}, bf16[8,64,256]{2,1,0:T(8,128)(2,1)S(1)}, u32[]{:S(2)}, u32[]{:S(2)}) collective-permute-start(bf16[8,64,256]{2,1,0:T(8,128)(2,1)S(1)} %get-tuple-element.34), channel_id=1, source_target_pairs={{0,3},{2,1},{3,2},{4,7},{6,5},{7,6},{8,11},{10,9},{11,10},{12,15},... | collective-permute-start | bytes 786440 | tf_op jit(solution)/shard_map/ppermute | solution.py:434
  68.6 1.9 %collective-permute-start.4 = (bf16[8,64,256]{2,1,0:T(8,128)(2,1)S(1)}, bf16[8,64,256]{2,1,0:T(8,128)(2,1)S(1)}, u32[]{:S(2)}, u32[]{:S(2)}) collective-permute-start(bf16[8,64,256]{2,1,0:T(8,128)(2,1)S(1)} %get-tuple-element.29), channel_id=1, source_target_pairs={{0,1},{2,3},{3,0},{4,5},{6,7},{7,4},{8,9},{10,11},{11,8},{12,13},{... | collective-permute-start | bytes 786440 | tf_op jit(solution)/shard_map/ppermute | solution.py:435
  70.5 8.4 %collective-permute-start.5 = (bf16[8,64,256]{2,1,0:T(8,128)(2,1)S(1)}, bf16[8,64,256]{2,1,0:T(8,128)(2,1)S(1)}, u32[]{:S(2)}, u32[]{:S(2)}) collective-permute-start(bf16[8,64,256]{2,1,0:T(8,128)(2,1)S(1)} %get-tuple-element.30), channel_id=1, source_target_pairs={{0,3},{2,1},{3,2},{4,7},{6,5},{7,6},{8,11},{10,9},{11,10},{12,15},... | collective-permute-start | bytes 786440 | tf_op jit(solution)/shard_map/ppermute | solution.py:436
  79.0 0.0 collective-permute-done.6.got_first
  79.0 6.6 %collective-permute-done.7.got_second = bf16[8,64,256]{2,1,0:T(8,128)(2,1)S(1)} collective-permute-done((bf16[8,64,256]{2,1,0:T(8,128)(2,1)S(1)}, bf16[8,64,256]{2,1,0:T(8,128)(2,1)S(1)}, u32[]{:S(2)}, u32[]{:S(2)}) %collective-permute-start.7) | collective-permute-done | bytes 262176 | tf_op jit(solution)/shard_map/ppermute | solution.py:434
  85.6 0.1 shard_map.41
  85.7 8.7 %collective-permute-start.8 = (bf16[8,64,256]{2,1,0:T(8,128)(2,1)S(1)}, bf16[8,64,256]{2,1,0:T(8,128)(2,1)S(1)}, u32[]{:S(2)}, u32[]{:S(2)}) collective-permute-start(bf16[8,64,256]{2,1,0:T(8,128)(2,1)S(1)} %get-tuple-element.35), channel_id=1, source_target_pairs={{0,1},{1,2},{2,3},{3,0},{4,5},{5,6},{6,7},{7,4},{8,9},{9,10},{10,1... | collective-permute-start | bytes 786440 | tf_op jit(solution)/shard_map/ppermute | solution.py:449
  94.4 1.9 %collective-permute-start.9 = (bf16[8,64,256]{2,1,0:T(8,128)(2,1)S(1)}, bf16[8,64,256]{2,1,0:T(8,128)(2,1)S(1)}, u32[]{:S(2)}, u32[]{:S(2)}) collective-permute-start(bf16[8,64,256]{2,1,0:T(8,128)(2,1)S(1)} %get-tuple-element.36), channel_id=1, source_target_pairs={{0,3},{1,0},{2,1},{3,2},{4,7},{5,4},{6,5},{7,6},{8,11},{9,8},{10,9... | collective-permute-start | bytes 786440 | tf_op jit(solution)/shard_map/ppermute | solution.py:450
  96.3 0.0 copy-done.3
  96.3 0.1 copy.4.keep
  96.4 0.0 collective-permute-done.4.first_free
  96.4 0.0 collective-permute-done.5.second_free
  96.4 4.8 %collective-permute-done.8.first_due = bf16[8,64,256]{2,1,0:T(8,128)(2,1)S(1)} collective-permute-done((bf16[8,64,256]{2,1,0:T(8,128)(2,1)S(1)}, bf16[8,64,256]{2,1,0:T(8,128)(2,1)S(1)}, u32[]{:S(2)}, u32[]{:S(2)}) %collective-permute-start.8) | collective-permute-done | bytes 262176 | tf_op jit(solution)/shard_map/ppermute | solution.py:449
  101.3 7.6 %collective-permute-done.9.second_due = bf16[8,64,256]{2,1,0:T(8,128)(2,1)S(1)} collective-permute-done((bf16[8,64,256]{2,1,0:T(8,128)(2,1)S(1)}, bf16[8,64,256]{2,1,0:T(8,128)(2,1)S(1)}, u32[]{:S(2)}, u32[]{:S(2)}) %collective-permute-start.9) | collective-permute-done | bytes 262176 | tf_op jit(solution)/shard_map/ppermute | solution.py:450
  108.9 1.1 shard_map.42
  (3 shorter events, 0.0 us)
Async XLA Ops:
  0.0 1.6 %copy-start = (bf16[16,64,1024]{2,1,0:T(8,128)(2,1)S(1)}, bf16[16,64,1024]{2,1,0:T(8,128)(2,1)}, u32[]{:S(2)}) copy-start(bf16[16,64,1024]{2,1,0:T(8,128)(2,1)} %dens.7) | copy-start | bytes 6291460
  1.6 0.7 copy-start.2
  2.9 53.3 %collective-permute-start.1 = (bf16[17,64,512]{2,1,0:T(8,128)(2,1)S(1)}, bf16[17,64,512]{2,1,0:T(8,128)(2,1)S(1)}, u32[]{:S(2)}, u32[]{:S(2)}) collective-permute-start(bf16[17,64,512]{2,1,0:T(8,128)(2,1)S(1)} %get-tuple-element.25), channel_id=1, source_target_pairs={{1,0},{3,2},{5,4},{7,6},{9,8},{11,10},{13,12},{15,14},{17,16},{19,... | collective-permute-start | bytes 3342344 | tf_op jit(solution)/shard_map/ppermute | solution.py:412
  4.2 33.7 %collective-permute-start = (bf16[15,64,512]{2,1,0:T(8,128)(2,1)S(1)}, bf16[15,64,512]{2,1,0:T(8,128)(2,1)S(1)}, u32[]{:S(2)}, u32[]{:S(2)}) collective-permute-start(bf16[15,64,512]{2,1,0:T(8,128)(2,1)S(1)} %get-tuple-element.24), channel_id=1, source_target_pairs={{1,510},{2,511},{5,2},{6,3},{9,6},{10,7},{13,10},{14,11},{17,14},{... | collective-permute-start | bytes 2949128 | tf_op jit(solution)/shard_map/ppermute | solution.py:411
  4.9 33.0 %collective-permute-start.2 = (bf16[14,64,512]{2,1,0:T(8,128)(2,1)S(1)}, bf16[14,64,512]{2,1,0:T(8,128)(2,1)S(1)}, u32[]{:S(2)}, u32[]{:S(2)}) collective-permute-start(bf16[14,64,512]{2,1,0:T(8,128)(2,1)S(1)} %get-tuple-element.26), channel_id=1, source_target_pairs={{0,508},{3,511},{4,0},{7,3},{8,4},{11,7},{12,8},{15,11},{16,12},{1... | collective-permute-start | bytes 2752520 | tf_op jit(solution)/shard_map/ppermute | solution.py:413
  7.9 48.3 %copy-start.1 = (bf16[16,64,1024]{2,1,0:T(8,128)(2,1)S(1)}, bf16[16,64,1024]{2,1,0:T(8,128)(2,1)}, u32[]{:S(2)}) copy-start(bf16[16,64,1024]{2,1,0:T(8,128)(2,1)} %dens.7) | copy-start | bytes 6291460
  7.9 30.0 %collective-permute-start.3 = (bf16[3,64,512]{2,1,0:T(8,128)(2,1)S(1)}, bf16[3,64,512]{2,1,0:T(8,128)(2,1)S(1)}, u32[]{:S(2)}, u32[]{:S(2)}) collective-permute-start(bf16[3,64,512]{2,1,0:T(8,128)(2,1)S(1)} %get-tuple-element.27), channel_id=1, source_target_pairs={{0,508},{3,511},{2,510},{4,0},{7,3},{6,2},{8,4},{11,7},{10,6},{12,... | collective-permute-start | bytes 589832 | tf_op jit(solution)/shard_map/ppermute | solution.py:414
  56.2 40.1 %copy-start.3 = (s32[16,4]{0,1:T(4,128)S(1)}, s32[16,4]{0,1:T(4,128)}, u32[]{:S(2)}) copy-start(s32[16,4]{0,1:T(4,128)} %param.5) | copy-start | bytes 772
  59.5 19.4 %collective-permute-start.6 = (bf16[8,64,256]{2,1,0:T(8,128)(2,1)S(1)}, bf16[8,64,256]{2,1,0:T(8,128)(2,1)S(1)}, u32[]{:S(2)}, u32[]{:S(2)}) collective-permute-start(bf16[8,64,256]{2,1,0:T(8,128)(2,1)S(1)} %get-tuple-element.33), channel_id=1, source_target_pairs={{0,1},{2,3},{3,0},{4,5},{6,7},{7,4},{8,9},{10,11},{11,8},{12,13},{... | collective-permute-start | bytes 786440 | tf_op jit(solution)/shard_map/ppermute | solution.py:433
  61.5 24.1 %collective-permute-start.7 = (bf16[8,64,256]{2,1,0:T(8,128)(2,1)S(1)}, bf16[8,64,256]{2,1,0:T(8,128)(2,1)S(1)}, u32[]{:S(2)}, u32[]{:S(2)}) collective-permute-start(bf16[8,64,256]{2,1,0:T(8,128)(2,1)S(1)} %get-tuple-element.34), channel_id=1, source_target_pairs={{0,3},{2,1},{3,2},{4,7},{6,5},{7,6},{8,11},{10,9},{11,10},{12,15},... | collective-permute-start | bytes 786440 | tf_op jit(solution)/shard_map/ppermute | solution.py:434
  68.6 27.8 %collective-permute-start.4 = (bf16[8,64,256]{2,1,0:T(8,128)(2,1)S(1)}, bf16[8,64,256]{2,1,0:T(8,128)(2,1)S(1)}, u32[]{:S(2)}, u32[]{:S(2)}) collective-permute-start(bf16[8,64,256]{2,1,0:T(8,128)(2,1)S(1)} %get-tuple-element.29), channel_id=1, source_target_pairs={{0,1},{2,3},{3,0},{4,5},{6,7},{7,4},{8,9},{10,11},{11,8},{12,13},{... | collective-permute-start | bytes 786440 | tf_op jit(solution)/shard_map/ppermute | solution.py:435
  70.5 25.9 %collective-permute-start.5 = (bf16[8,64,256]{2,1,0:T(8,128)(2,1)S(1)}, bf16[8,64,256]{2,1,0:T(8,128)(2,1)S(1)}, u32[]{:S(2)}, u32[]{:S(2)}) collective-permute-start(bf16[8,64,256]{2,1,0:T(8,128)(2,1)S(1)} %get-tuple-element.30), channel_id=1, source_target_pairs={{0,3},{2,1},{3,2},{4,7},{6,5},{7,6},{8,11},{10,9},{11,10},{12,15},... | collective-permute-start | bytes 786440 | tf_op jit(solution)/shard_map/ppermute | solution.py:436
  85.7 15.6 %collective-permute-start.8 = (bf16[8,64,256]{2,1,0:T(8,128)(2,1)S(1)}, bf16[8,64,256]{2,1,0:T(8,128)(2,1)S(1)}, u32[]{:S(2)}, u32[]{:S(2)}) collective-permute-start(bf16[8,64,256]{2,1,0:T(8,128)(2,1)S(1)} %get-tuple-element.35), channel_id=1, source_target_pairs={{0,1},{1,2},{2,3},{3,0},{4,5},{5,6},{6,7},{7,4},{8,9},{9,10},{10,1... | collective-permute-start | bytes 786440 | tf_op jit(solution)/shard_map/ppermute | solution.py:449
  94.4 14.5 %collective-permute-start.9 = (bf16[8,64,256]{2,1,0:T(8,128)(2,1)S(1)}, bf16[8,64,256]{2,1,0:T(8,128)(2,1)S(1)}, u32[]{:S(2)}, u32[]{:S(2)}) collective-permute-start(bf16[8,64,256]{2,1,0:T(8,128)(2,1)S(1)} %get-tuple-element.36), channel_id=1, source_target_pairs={{0,3},{1,0},{2,1},{3,2},{4,7},{5,4},{6,5},{7,6},{8,11},{9,8},{10,9... | collective-permute-start | bytes 786440 | tf_op jit(solution)/shard_map/ppermute | solution.py:450

commit v10 on v9

--- a/solution.py
+++ b/solution.py
@@ -11,7 +11,7 @@
 WIDE = ROWS * BS
 HALF = WIDE // 2
 TILE = 256
-MAIN = 14
+MAIN = 15
 AXES = ("row", "col", "depth")
 NT = (((1,), (1,)), ((), ()))
 NN = (((1,), (0,)), ((), ()))
@@ -93,7 +93,6 @@
             pair = [own(2 * a + e, 0, 2 * BS)[:, :BS] for e in range(2)]
             lane = 2 * BS * (a % 4)
             rest[a // 4, :, lane : lane + 2 * BS] = jnp.concatenate(pair, axis=1)
-        rest[2] = jnp.zeros((BS, HALF), jnp.bfloat16)
 
 
 def pack_first_kernel(dens, mask, lower, upper):

time: 110 us -> 109 us (level)
  starting transfers between devices: 38.1 us -> 35 us
  waiting for transfers between devices: 62.4 us -> 64.1 us
    ppermute x1, waiting for transfers between devices: 4.83 us -> 6.91 us  [per_device(): first_due = lax.ppermute(first_due, AXES, first_route)]
    ppermute x1, waiting for transfers between devices: 7.62 us -> 5.56 us  [per_device(): second_due = lax.ppermute(second_due, AXES, second_route)]
    ppermute x1, waiting for transfers between devices: 6.59 us -> 8.32 us  [per_device(): lax.ppermute(second1, AXES, [r for r in second_route if r[0] % 4 != 1])]
    ppermute x1, starting transfers between devices: 8.43 us -> 6.85 us  [per_device(): lax.ppermute(second_free, AXES, [r for r in second_route if r[0] % 4 != 1])]
    ppermute x1, starting transfers between devices: 8.7 us -> 7.2 us  [per_device(): first_due = lax.ppermute(first_due, AXES, first_route)]
where the time goes in v10:
time: 109 us
  waiting for transfers between devices  64.1 us (59%)
  starting transfers between devices  35 us (32%)
  Pallas kernels  6.94 us (6%)
  local copies, waits for them, and re-layouts  2.38 us (2%)
    ppermute x1, waiting for transfers between devices, per_device(): got_rest = lax.ppermute(rest, AXES, of_rest)  25 us
    ppermute x1, waiting for transfers between devices, per_device(): got_depth = lax.ppermute(upper_first, AXES, by_depth)  18.3 us
    ppermute x1, waiting for transfers between devices, per_device(): lax.ppermute(second1, AXES, [r for r in second_route if r[0] % 4 != 1])  8.32 us
    ppermute x1, starting transfers between devices, per_device(): first_due = lax.ppermute(first_due, AXES, first_route)  7.2 us
    ppermute x1, starting transfers between devices, per_device(): lax.ppermute(second1, AXES, [r for r in second_route if r[0] % 4 != 1])  7.13 us
    pallas_call x6, Pallas kernels, call(): pl.pallas_call(kernel, out_shape=tuple((jax.ShapeDtypeStruct(shape, jnp.f...  6.94 us
    ppermute x1, waiting for transfers between devices, per_device(): first_due = lax.ppermute(first_due, AXES, first_route)  6.91 us
    ppermute x1, starting transfers between devices, per_device(): lax.ppermute(second_free, AXES, [r for r in second_route if r[0] % 4 != 1])  6.85 us
  transfers between devices with their start and end apart: 10, of which 5 were waited for; matrix products, arithmetic and copies ran while one was open for 0% of the time, Pallas kernels for 2%

profile of v10, /device:TPU:63, one launch (start us, length us, event | category | flops | bytes accessed | tf_op | source)
XLA Modules:
  0.0 108.6 jit_solution(9219755607899006402)
XLA Ops:
  0.0 1.6 %copy-done = bf16[16,64,1024]{2,1,0:T(8,128)(2,1)S(1)} copy-done((bf16[16,64,1024]{2,1,0:T(8,128)(2,1)S(1)}, bf16[16,64,1024]{2,1,0:T(8,128)(2,1)}, u32[]{:S(2)}) %copy-start) | copy-done | bytes 2097176
  1.6 0.7 copy-done.2
  2.3 0.4 shard_map.37
  2.7 0.2 shard_map.39
  2.9 1.3 %collective-permute-start.1 = (bf16[17,64,512]{2,1,0:T(8,128)(2,1)S(1)}, bf16[17,64,512]{2,1,0:T(8,128)(2,1)S(1)}, u32[]{:S(2)}, u32[]{:S(2)}) collective-permute-start(bf16[17,64,512]{2,1,0:T(8,128)(2,1)S(1)} %get-tuple-element.25), channel_id=1, source_target_pairs={{1,0},{3,2},{5,4},{7,6},{9,8},{11,10},{13,12},{15,14},{17,16},{19,... | collective-permute-start | bytes 3342344 | tf_op jit(solution)/shard_map/ppermute | solution.py:411
  4.2 0.7 collective-permute-start
  4.9 3.0 %collective-permute-start.2 = (bf16[15,64,512]{2,1,0:T(8,128)(2,1)S(1)}, bf16[15,64,512]{2,1,0:T(8,128)(2,1)S(1)}, u32[]{:S(2)}, u32[]{:S(2)}) collective-permute-start(bf16[15,64,512]{2,1,0:T(8,128)(2,1)S(1)} %get-tuple-element.26), channel_id=1, source_target_pairs={{0,508},{3,511},{4,0},{7,3},{8,4},{11,7},{12,8},{15,11},{16,12},{1... | collective-permute-start | bytes 2949128 | tf_op jit(solution)/shard_map/ppermute | solution.py:412
  7.9 0.0 copy-start.1
  7.9 3.1 %collective-permute-start.3 = (bf16[2,64,512]{2,1,0:T(8,128)(2,1)S(1)}, bf16[2,64,512]{2,1,0:T(8,128)(2,1)S(1)}, u32[]{:S(2)}, u32[]{:S(2)}) collective-permute-start(bf16[2,64,512]{2,1,0:T(8,128)(2,1)S(1)} %get-tuple-element.27), channel_id=1, source_target_pairs={{0,508},{3,511},{2,510},{4,0},{7,3},{6,2},{8,4},{11,7},{10,6},{12,... | collective-permute-start | bytes 393224 | tf_op jit(solution)/shard_map/ppermute | solution.py:413
  11.0 1.9 %shard_map.38 = (bf16[1024,1024]{1,0:T(8,128)(2,1)S(1)}, f32[4,256,1024]{2,1,0:T(8,128)S(1)}) custom-call(bf16[16,64,1024]{2,1,0:T(8,128)(2,1)S(1)} %copy-done, f32[16,1024]{1,0:T(8,128)S(1)} %get-tuple-element.21.mask), custom_call_target="tpu_custom_call" | custom-call | flops 3000000000 | bytes 9500000 | tf_op jit(solution)/shard_map/pallas_call | solution.py:346
  12.9 25.0 %collective-permute-done.3.got_rest = bf16[2,64,512]{2,1,0:T(8,128)(2,1)S(1)} collective-permute-done((bf16[2,64,512]{2,1,0:T(8,128)(2,1)S(1)}, bf16[2,64,512]{2,1,0:T(8,128)(2,1)S(1)}, u32[]{:S(2)}, u32[]{:S(2)}) %collective-permute-start.3) | collective-permute-done | bytes 131104 | tf_op jit(solution)/shard_map/ppermute | solution.py:413
  37.9 0.0 collective-permute-done.got_lower
  37.9 0.0 collective-permute-done.2.got_y
  37.9 18.3 %collective-permute-done.1.got_depth = bf16[17,64,512]{2,1,0:T(8,128)(2,1)S(1)} collective-permute-done((bf16[17,64,512]{2,1,0:T(8,128)(2,1)S(1)}, bf16[17,64,512]{2,1,0:T(8,128)(2,1)S(1)}, u32[]{:S(2)}, u32[]{:S(2)}) %collective-permute-start.1) | collective-permute-done | bytes 1114144 | tf_op jit(solution)/shard_map/ppermute | solution.py:411
  56.2 0.0 copy-done.1
  56.2 3.3 %shard_map.40 = (bf16[16,64,256]{2,1,0:T(8,128)(2,1)S(1)}, bf16[8,64,256]{2,1,0:T(8,128)(2,1)S(1)}, bf16[8,64,256]{2,1,0:T(8,128)(2,1)S(1)}, bf16[8,64,256]{2,1,...) custom-call(bf16[16,64,1024]{2,1,0:T(8,128)(2,1)S(1)} %copy-done.1, ...), custom_call_target="tpu_custom_call" | custom-call | flops 6000000000 | bytes 14000000 | tf_op jit(solution)/shard_map/pallas_call | solution.py:346
  59.5 1.9 %collective-permute-start.6 = (bf16[8,64,256]{2,1,0:T(8,128)(2,1)S(1)}, bf16[8,64,256]{2,1,0:T(8,128)(2,1)S(1)}, u32[]{:S(2)}, u32[]{:S(2)}) collective-permute-start(bf16[8,64,256]{2,1,0:T(8,128)(2,1)S(1)} %get-tuple-element.33), channel_id=1, source_target_pairs={{0,1},{2,3},{3,0},{4,5},{6,7},{7,4},{8,9},{10,11},{11,8},{12,13},{... | collective-permute-start | bytes 786440 | tf_op jit(solution)/shard_map/ppermute | solution.py:432
  61.5 7.1 %collective-permute-start.7 = (bf16[8,64,256]{2,1,0:T(8,128)(2,1)S(1)}, bf16[8,64,256]{2,1,0:T(8,128)(2,1)S(1)}, u32[]{:S(2)}, u32[]{:S(2)}) collective-permute-start(bf16[8,64,256]{2,1,0:T(8,128)(2,1)S(1)} %get-tuple-element.34), channel_id=1, source_target_pairs={{0,3},{2,1},{3,2},{4,7},{6,5},{7,6},{8,11},{10,9},{11,10},{12,15},... | collective-permute-start | bytes 786440 | tf_op jit(solution)/shard_map/ppermute | solution.py:433
  68.6 1.9 %collective-permute-start.4 = (bf16[8,64,256]{2,1,0:T(8,128)(2,1)S(1)}, bf16[8,64,256]{2,1,0:T(8,128)(2,1)S(1)}, u32[]{:S(2)}, u32[]{:S(2)}) collective-permute-start(bf16[8,64,256]{2,1,0:T(8,128)(2,1)S(1)} %get-tuple-element.29), channel_id=1, source_target_pairs={{0,1},{2,3},{3,0},{4,5},{6,7},{7,4},{8,9},{10,11},{11,8},{12,13},{... | collective-permute-start | bytes 786440 | tf_op jit(solution)/shard_map/ppermute | solution.py:434
  70.5 6.8 %collective-permute-start.5 = (bf16[8,64,256]{2,1,0:T(8,128)(2,1)S(1)}, bf16[8,64,256]{2,1,0:T(8,128)(2,1)S(1)}, u32[]{:S(2)}, u32[]{:S(2)}) collective-permute-start(bf16[8,64,256]{2,1,0:T(8,128)(2,1)S(1)} %get-tuple-element.30), channel_id=1, source_target_pairs={{0,3},{2,1},{3,2},{4,7},{6,5},{7,6},{8,11},{10,9},{11,10},{12,15},... | collective-permute-start | bytes 786440 | tf_op jit(solution)/shard_map/ppermute | solution.py:435
  77.4 0.0 collective-permute-done.6.got_first
  77.4 8.3 %collective-permute-done.7.got_second = bf16[8,64,256]{2,1,0:T(8,128)(2,1)S(1)} collective-permute-done((bf16[8,64,256]{2,1,0:T(8,128)(2,1)S(1)}, bf16[8,64,256]{2,1,0:T(8,128)(2,1)S(1)}, u32[]{:S(2)}, u32[]{:S(2)}) %collective-permute-start.7) | collective-permute-done | bytes 262176 | tf_op jit(solution)/shard_map/ppermute | solution.py:433
  85.7 0.1 shard_map.41
  85.8 7.2 %collective-permute-start.8 = (bf16[8,64,256]{2,1,0:T(8,128)(2,1)S(1)}, bf16[8,64,256]{2,1,0:T(8,128)(2,1)S(1)}, u32[]{:S(2)}, u32[]{:S(2)}) collective-permute-start(bf16[8,64,256]{2,1,0:T(8,128)(2,1)S(1)} %get-tuple-element.35), channel_id=1, source_target_pairs={{0,1},{1,2},{2,3},{3,0},{4,5},{5,6},{6,7},{7,4},{8,9},{9,10},{10,1... | collective-permute-start | bytes 786440 | tf_op jit(solution)/shard_map/ppermute | solution.py:448
  93.1 1.9 %collective-permute-start.9 = (bf16[8,64,256]{2,1,0:T(8,128)(2,1)S(1)}, bf16[8,64,256]{2,1,0:T(8,128)(2,1)S(1)}, u32[]{:S(2)}, u32[]{:S(2)}) collective-permute-start(bf16[8,64,256]{2,1,0:T(8,128)(2,1)S(1)} %get-tuple-element.36), channel_id=1, source_target_pairs={{0,3},{1,0},{2,1},{3,2},{4,7},{5,4},{6,5},{7,6},{8,11},{9,8},{10,9... | collective-permute-start | bytes 786440 | tf_op jit(solution)/shard_map/ppermute | solution.py:449
  95.0 0.0 copy-done.3
  95.0 0.1 copy.4.keep
  95.1 0.0 collective-permute-done.4.first_free
  95.1 0.0 collective-permute-done.5.second_free
  95.1 6.9 %collective-permute-done.8.first_due = bf16[8,64,256]{2,1,0:T(8,128)(2,1)S(1)} collective-permute-done((bf16[8,64,256]{2,1,0:T(8,128)(2,1)S(1)}, bf16[8,64,256]{2,1,0:T(8,128)(2,1)S(1)}, u32[]{:S(2)}, u32[]{:S(2)}) %collective-permute-start.8) | collective-permute-done | bytes 262176 | tf_op jit(solution)/shard_map/ppermute | solution.py:448
  102.0 5.6 %collective-permute-done.9.second_due = bf16[8,64,256]{2,1,0:T(8,128)(2,1)S(1)} collective-permute-done((bf16[8,64,256]{2,1,0:T(8,128)(2,1)S(1)}, bf16[8,64,256]{2,1,0:T(8,128)(2,1)S(1)}, u32[]{:S(2)}, u32[]{:S(2)}) %collective-permute-start.9) | collective-permute-done | bytes 262176 | tf_op jit(solution)/shard_map/ppermute | solution.py:449
  107.6 1.1 shard_map.42
  (3 shorter events, 0.0 us)
Async XLA Ops:
  0.0 1.6 %copy-start = (bf16[16,64,1024]{2,1,0:T(8,128)(2,1)S(1)}, bf16[16,64,1024]{2,1,0:T(8,128)(2,1)}, u32[]{:S(2)}) copy-start(bf16[16,64,1024]{2,1,0:T(8,128)(2,1)} %dens.7) | copy-start | bytes 6291460
  1.6 0.7 copy-start.2
  2.9 53.3 %collective-permute-start.1 = (bf16[17,64,512]{2,1,0:T(8,128)(2,1)S(1)}, bf16[17,64,512]{2,1,0:T(8,128)(2,1)S(1)}, u32[]{:S(2)}, u32[]{:S(2)}) collective-permute-start(bf16[17,64,512]{2,1,0:T(8,128)(2,1)S(1)} %get-tuple-element.25), channel_id=1, source_target_pairs={{1,0},{3,2},{5,4},{7,6},{9,8},{11,10},{13,12},{15,14},{17,16},{19,... | collective-permute-start | bytes 3342344 | tf_op jit(solution)/shard_map/ppermute | solution.py:411
  4.2 33.7 %collective-permute-start = (bf16[15,64,512]{2,1,0:T(8,128)(2,1)S(1)}, bf16[15,64,512]{2,1,0:T(8,128)(2,1)S(1)}, u32[]{:S(2)}, u32[]{:S(2)}) collective-permute-start(bf16[15,64,512]{2,1,0:T(8,128)(2,1)S(1)} %get-tuple-element.24), channel_id=1, source_target_pairs={{1,510},{2,511},{5,2},{6,3},{9,6},{10,7},{13,10},{14,11},{17,14},{... | collective-permute-start | bytes 2949128 | tf_op jit(solution)/shard_map/ppermute | solution.py:410
  4.9 33.0 %collective-permute-start.2 = (bf16[15,64,512]{2,1,0:T(8,128)(2,1)S(1)}, bf16[15,64,512]{2,1,0:T(8,128)(2,1)S(1)}, u32[]{:S(2)}, u32[]{:S(2)}) collective-permute-start(bf16[15,64,512]{2,1,0:T(8,128)(2,1)S(1)} %get-tuple-element.26), channel_id=1, source_target_pairs={{0,508},{3,511},{4,0},{7,3},{8,4},{11,7},{12,8},{15,11},{16,12},{1... | collective-permute-start | bytes 2949128 | tf_op jit(solution)/shard_map/ppermute | solution.py:412
  7.9 48.3 %copy-start.1 = (bf16[16,64,1024]{2,1,0:T(8,128)(2,1)S(1)}, bf16[16,64,1024]{2,1,0:T(8,128)(2,1)}, u32[]{:S(2)}) copy-start(bf16[16,64,1024]{2,1,0:T(8,128)(2,1)} %dens.7) | copy-start | bytes 6291460
  7.9 30.0 %collective-permute-start.3 = (bf16[2,64,512]{2,1,0:T(8,128)(2,1)S(1)}, bf16[2,64,512]{2,1,0:T(8,128)(2,1)S(1)}, u32[]{:S(2)}, u32[]{:S(2)}) collective-permute-start(bf16[2,64,512]{2,1,0:T(8,128)(2,1)S(1)} %get-tuple-element.27), channel_id=1, source_target_pairs={{0,508},{3,511},{2,510},{4,0},{7,3},{6,2},{8,4},{11,7},{10,6},{12,... | collective-permute-start | bytes 393224 | tf_op jit(solution)/shard_map/ppermute | solution.py:413
  56.2 38.7 %copy-start.3 = (s32[16,4]{0,1:T(4,128)S(1)}, s32[16,4]{0,1:T(4,128)}, u32[]{:S(2)}) copy-start(s32[16,4]{0,1:T(4,128)} %param.5) | copy-start | bytes 772
  59.5 17.9 %collective-permute-start.6 = (bf16[8,64,256]{2,1,0:T(8,128)(2,1)S(1)}, bf16[8,64,256]{2,1,0:T(8,128)(2,1)S(1)}, u32[]{:S(2)}, u32[]{:S(2)}) collective-permute-start(bf16[8,64,256]{2,1,0:T(8,128)(2,1)S(1)} %get-tuple-element.33), channel_id=1, source_target_pairs={{0,1},{2,3},{3,0},{4,5},{6,7},{7,4},{8,9},{10,11},{11,8},{12,13},{... | collective-permute-start | bytes 786440 | tf_op jit(solution)/shard_map/ppermute | solution.py:432
  61.5 24.3 %collective-permute-start.7 = (bf16[8,64,256]{2,1,0:T(8,128)(2,1)S(1)}, bf16[8,64,256]{2,1,0:T(8,128)(2,1)S(1)}, u32[]{:S(2)}, u32[]{:S(2)}) collective-permute-start(bf16[8,64,256]{2,1,0:T(8,128)(2,1)S(1)} %get-tuple-element.34), channel_id=1, source_target_pairs={{0,3},{2,1},{3,2},{4,7},{6,5},{7,6},{8,11},{10,9},{11,10},{12,15},... | collective-permute-start | bytes 786440 | tf_op jit(solution)/shard_map/ppermute | solution.py:433
  68.6 26.5 %collective-permute-start.4 = (bf16[8,64,256]{2,1,0:T(8,128)(2,1)S(1)}, bf16[8,64,256]{2,1,0:T(8,128)(2,1)S(1)}, u32[]{:S(2)}, u32[]{:S(2)}) collective-permute-start(bf16[8,64,256]{2,1,0:T(8,128)(2,1)S(1)} %get-tuple-element.29), channel_id=1, source_target_pairs={{0,1},{2,3},{3,0},{4,5},{6,7},{7,4},{8,9},{10,11},{11,8},{12,13},{... | collective-permute-start | bytes 786440 | tf_op jit(solution)/shard_map/ppermute | solution.py:434
  70.5 24.6 %collective-permute-start.5 = (bf16[8,64,256]{2,1,0:T(8,128)(2,1)S(1)}, bf16[8,64,256]{2,1,0:T(8,128)(2,1)S(1)}, u32[]{:S(2)}, u32[]{:S(2)}) collective-permute-start(bf16[8,64,256]{2,1,0:T(8,128)(2,1)S(1)} %get-tuple-element.30), channel_id=1, source_target_pairs={{0,3},{2,1},{3,2},{4,7},{6,5},{7,6},{8,11},{10,9},{11,10},{12,15},... | collective-permute-start | bytes 786440 | tf_op jit(solution)/shard_map/ppermute | solution.py:435
  85.8 16.1 %collective-permute-start.8 = (bf16[8,64,256]{2,1,0:T(8,128)(2,1)S(1)}, bf16[8,64,256]{2,1,0:T(8,128)(2,1)S(1)}, u32[]{:S(2)}, u32[]{:S(2)}) collective-permute-start(bf16[8,64,256]{2,1,0:T(8,128)(2,1)S(1)} %get-tuple-element.35), channel_id=1, source_target_pairs={{0,1},{1,2},{2,3},{3,0},{4,5},{5,6},{6,7},{7,4},{8,9},{9,10},{10,1... | collective-permute-start | bytes 786440 | tf_op jit(solution)/shard_map/ppermute | solution.py:448
  93.1 14.5 %collective-permute-start.9 = (bf16[8,64,256]{2,1,0:T(8,128)(2,1)S(1)}, bf16[8,64,256]{2,1,0:T(8,128)(2,1)S(1)}, u32[]{:S(2)}, u32[]{:S(2)}) collective-permute-start(bf16[8,64,256]{2,1,0:T(8,128)(2,1)S(1)} %get-tuple-element.36), channel_id=1, source_target_pairs={{0,3},{1,0},{2,1},{3,2},{4,7},{5,4},{6,5},{7,6},{8,11},{9,8},{10,9... | collective-permute-start | bytes 786440 | tf_op jit(solution)/shard_map/ppermute | solution.py:449
